TPU v7x, 32 devices: a whole 2x2x4 slice. The times are simulated.
32 devices in a mesh: group: 2 (over x), tensor: 8 (over z, y), adapter: 2 (over core).
Axes of the slice: x: 2, y: 2, z: 4, core: 2. Of those that a mesh axis runs over, the one named last changes fastest.
Arguments:
- hidden: bfloat16 [2, 256, 8192], P('adapter', 'group', 'tensor'), parts along dimension 1, may hold values from -6 to 6
- input_norm_scale: float32 [8192], replicated, may hold values from 0.5 to 1.5
- query_weight: bfloat16 [8192, 8192], P(None, 'tensor'), may hold values from -0.0625 to 0.0625
- key_value_weight: bfloat16 [8192, 2048], P('tensor'), may hold values from -0.0625 to 0.0625
- adapter_down_weight: bfloat16 [8, 8192, 192], P(('group', 'adapter'), 'tensor'), parts along dimension 0, may hold values from -0.0625 to 0.0625
- adapter_up_query: bfloat16 [8, 64, 8192], P(('group', 'adapter'), None, 'tensor'), parts along dimension 0, may hold values from -0.75 to 0.75
- adapter_up_key_value: bfloat16 [8, 2, 64, 1024], P(('group', 'adapter')), parts along dimension 0, may hold values from -0.75 to 0.75
- request_adapter: int32 [2, 256], P('adapter', 'group'), parts along dimension 1, may hold values from 0 to 3, never falling along the last dimension, each value on 1 to 64 neighbouring positions
- key_value_cache: bfloat16 [2, 256, 2, 96, 1024], P('adapter', ('group', 'tensor')), parts along dimension 1, may hold values from -240 to 240
- lengths: int32 [2, 256], P('adapter', ('group', 'tensor')), parts along dimension 1, may hold values from 1 to 96, 6144 in all within a row
Outputs:
- attended: bfloat16 [2, 256, 8192], P('adapter', ('group', 'tensor')), parts along dimension 1
- new_kv: bfloat16 [2, 256, 2, 1024], P('adapter', ('group', 'tensor')), parts along dimension 1
There are 2 independent parts, one for each index of `group`. A program takes and returns all parts, laid end to end along the dimension named above; an argument that names none is the same for every part. Nothing has to cross between parts.
Inputs may be any that keep to these rules, and one draw needn't show every extreme that they name: `request_adapter`: within each batch the ids never fall; every adapter has 1 to 64 rows of the batch and one has exactly 64. `lengths`: in each batch some row has exactly 96.
All inputs are finite; a program needn't handle non-finite values. No bound on the sum of `lengths` on one device may be relied on, other than what follows from the above.
Results may differ from a plain program's by a relative error of at most 0.0065.
The roundings to bfloat16 on the way count: a program that leaves them out, or rounds other values in their place, can miss the bound.
Values may be sent and summed in bfloat16 or wider, within the bound.
No kernel may reach another device: no remote copies, remote signals or barrier semaphores. Data moves between devices by JAX's collectives and lax.ppermute only.
A program may use at most 128 MiB of HBM per device.

v0:
```python
import math

import jax
import jax.numpy as jnp
from jax import lax
from jax.sharding import PartitionSpec as P

MODEL_WIDTH = 8192
QUERY_HEADS = 64
KEY_HEADS = 8
HEAD_WIDTH = 128
SEG = 128


EPS = 1e-05
THETA = 500000.0


def apply_rotary(value_rows, token_positions, heads):
    request_row_count = value_rows.shape[0]
    shaped = value_rows.reshape(request_row_count, heads, HEAD_WIDTH)
    half_dim = HEAD_WIDTH // 2
    frequency = THETA ** (-(jnp.arange(half_dim).astype(jnp.float32) * 2.0 / HEAD_WIDTH))
    angles = token_positions.astype(jnp.float32)[:, None] * frequency[None, :]
    cosine = jnp.cos(angles)[:, None, :]
    sine_values = jnp.sin(angles)[:, None, :]
    leading = shaped[..., :half_dim]
    second = shaped[..., half_dim:]
    turned = jnp.concatenate(
        [leading * cosine - second * sine_values, second * cosine + leading * sine_values], axis=-1
    )
    return turned.reshape(request_row_count, heads * HEAD_WIDTH)


def attend(query_vector, newest_token, layer_cache, request_lengths):
    request_row_count = query_vector.shape[0]
    query_group_width = QUERY_HEADS // KEY_HEADS
    token_positions = layer_cache.shape[2]
    score_scale = 1.0 / math.sqrt(HEAD_WIDTH)
    query_head_rows = query_vector.reshape(
        request_row_count, KEY_HEADS, query_group_width, HEAD_WIDTH
    )
    cached_key_rows = layer_cache[:, 0].reshape(
        request_row_count, token_positions, KEY_HEADS, HEAD_WIDTH
    )
    cached_value_rows = layer_cache[:, 1].reshape(
        request_row_count, token_positions, KEY_HEADS, HEAD_WIDTH
    )
    newest_key = newest_token[:, 0].reshape(request_row_count, KEY_HEADS, HEAD_WIDTH)
    newest_value = newest_token[:, 1].reshape(request_row_count, KEY_HEADS, HEAD_WIDTH)
    scores = (
        jnp.einsum(
            "rkgd,rpkd->rkgp", query_head_rows, cached_key_rows, preferred_element_type=jnp.float32
        )
        * score_scale
    )
    visible = jnp.arange(token_positions)[None, :] < request_lengths[:, None]
    scores = jnp.where(visible[:, None, None, :], scores, jnp.float32(-1e30))
    new_score = (
        jnp.einsum("rkgd,rkd->rkg", query_head_rows, newest_key, preferred_element_type=jnp.float32)
        * score_scale
    )
    top_score = jnp.maximum(jnp.max(scores, axis=-1), new_score)
    weights = jnp.exp(scores - top_score[..., None])
    new_weight = jnp.exp(new_score - top_score)
    denominator = jnp.sum(weights, axis=-1) + new_weight
    cache_weights = (weights / denominator[..., None]).astype(jnp.bfloat16)
    fresh_weights = (new_weight / denominator).astype(jnp.bfloat16)
    mixed = jnp.einsum(
        "rkgp,rpkd->rkgd", cache_weights, cached_value_rows, preferred_element_type=jnp.float32
    )
    mixed = (
        mixed
        + fresh_weights.astype(jnp.float32)[..., None]
        * newest_value.astype(jnp.float32)[:, :, None, :]
    )
    return mixed.reshape(request_row_count, QUERY_HEADS * HEAD_WIDTH).astype(jnp.bfloat16)


def block_table(request_row_index, adapters, seg_rows, total_rows):
    labels = jnp.arange(adapters)
    members = (request_row_index[:, None] == labels[None, :]).astype(jnp.int32)
    counts = jnp.sum(members, axis=0)
    first_rows = jnp.cumsum(counts) - counts
    block_spans = (counts + seg_rows - 1) // seg_rows
    block_ends = jnp.cumsum(block_spans)
    block_begins = block_ends - block_spans
    slot_count = total_rows // seg_rows + adapters
    slot_index = jnp.arange(slot_count)
    owners = jnp.sum((slot_index[:, None] >= block_ends[None, :]).astype(jnp.int32), axis=1)
    chosen = (owners[:, None] == labels[None, :]).astype(jnp.int32)
    owner_first = jnp.sum(chosen * first_rows[None, :], axis=1)
    owner_block = jnp.sum(chosen * block_begins[None, :], axis=1)
    owner_last = owner_first + jnp.sum(chosen * counts[None, :], axis=1)
    starts = owner_first + (slot_index - owner_block) * seg_rows
    live_rows = jnp.clip(owner_last - starts, 0, seg_rows)
    starts = jnp.clip(starts, 0, total_rows)
    return (jnp.minimum(owners, adapters - 1), starts, live_rows)


def to_blocks(value_rows, starts, live_rows, seg_rows):
    padded = jnp.concatenate(
        [value_rows, jnp.zeros((seg_rows, value_rows.shape[1]), value_rows.dtype)], axis=0
    )
    blocks = jax.vmap(lambda offset: lax.dynamic_slice_in_dim(padded, offset, seg_rows, 0))(starts)
    kept_rows = jnp.arange(seg_rows)[None, :] < live_rows[:, None]
    return jnp.where(kept_rows[:, :, None], blocks, jnp.zeros_like(blocks))


def to_rows(blocks, starts, live_rows, total_rows):
    seg_rows = blocks.shape[1]
    kept_rows = jnp.arange(seg_rows)[None, :] < live_rows[:, None]
    blocks = jnp.where(kept_rows[:, :, None], blocks, jnp.zeros_like(blocks))
    targets = (starts[:, None] + jnp.arange(seg_rows)[None, :]).reshape(-1)
    result = jnp.zeros((total_rows + seg_rows, blocks.shape[2]), blocks.dtype)
    result = result.at[targets].add(blocks.reshape(-1, blocks.shape[2]))
    return result[:total_rows]


def body(
    hidden,
    input_norm_scale,
    query_weight,
    key_value_weight,
    adapter_down_weight,
    adapter_up_query,
    adapter_up_key_value,
    request_adapter,
    key_value_cache,
    lengths,
):
    tensor_pos = lax.axis_index("tensor")
    local_rows = hidden[0]
    row_count = local_rows.shape[0]
    local_width = local_rows.shape[1]
    local_wide = local_rows.astype(jnp.float32)
    squares = lax.psum(jnp.sum(local_wide * local_wide, axis=1), "tensor")
    inverse = lax.rsqrt(squares / MODEL_WIDTH + EPS)
    gain_local = lax.dynamic_slice_in_dim(input_norm_scale, tensor_pos * local_width, local_width)
    normed = (local_wide * inverse[:, None] * gain_local[None, :]).astype(jnp.bfloat16)
    scaled = (
        lax.all_gather(hidden, "tensor", axis=2, tiled=True)[0].astype(jnp.float32)
        * inverse[:, None]
        * input_norm_scale[None, :]
    ).astype(jnp.bfloat16)
    query_base = jnp.dot(scaled, query_weight, preferred_element_type=jnp.float32)
    kv_term = jnp.dot(normed, key_value_weight, preferred_element_type=jnp.float32)
    all_down, all_up_q, all_up_kv = (
        lax.all_gather(adapter_down_weight, "adapter", axis=0, tiled=True),
        lax.all_gather(adapter_up_query, "adapter", axis=0, tiled=True),
        lax.all_gather(adapter_up_key_value, "adapter", axis=0, tiled=True),
    )
    adapters = all_down.shape[0]
    rank_size = all_up_q.shape[1]
    key_value_width = all_up_kv.shape[3]
    owners, starts, live_rows = block_table(request_adapter[0], adapters, SEG, row_count)
    normed_blocks = to_blocks(normed, starts, live_rows, SEG)
    down_blocks = jnp.take(all_down, owners, axis=0)
    shrink_blocks = jnp.einsum(
        "bsd,bdr->bsr", normed_blocks, down_blocks, preferred_element_type=jnp.float32
    )
    summed_blocks = lax.psum(shrink_blocks, "tensor")
    shrink_rows = to_rows(summed_blocks, starts, live_rows, row_count)
    shrink_low = shrink_rows.astype(jnp.bfloat16)
    query_shrink = to_blocks(shrink_low[:, :rank_size], starts, live_rows, SEG)
    up_query_blocks = jnp.take(all_up_q, owners, axis=0)
    query_delta_blocks = jnp.einsum(
        "bsr,brc->bsc", query_shrink, up_query_blocks, preferred_element_type=jnp.float32
    )
    query_delta = to_rows(query_delta_blocks, starts, live_rows, row_count)
    query_raw = (query_base + query_delta).astype(jnp.bfloat16)
    query_rows = lax.all_to_all(query_raw, "tensor", split_axis=0, concat_axis=1, tiled=True)
    key_value_rows = lax.psum_scatter(kv_term, "tensor", scatter_dimension=0, tiled=True)
    own_rows = query_rows.shape[0]
    own_start = tensor_pos * own_rows
    own_ids = lax.dynamic_slice_in_dim(request_adapter[0], own_start, own_rows)
    own_shrink = lax.dynamic_slice_in_dim(shrink_low, own_start, own_rows, 0)[:, rank_size:]
    own_shrink = own_shrink.reshape(own_rows, 2, rank_size)
    own_up = jnp.take(all_up_kv, own_ids, axis=0)
    own_delta = jnp.einsum("rjk,rjkc->rjc", own_shrink, own_up, preferred_element_type=jnp.float32)
    key_value_rows = key_value_rows + own_delta.reshape(own_rows, 2 * key_value_width)
    request_lengths = lengths[0]
    key_spun = apply_rotary(key_value_rows[:, :key_value_width], request_lengths, KEY_HEADS)
    newest_token = jnp.stack([key_spun, key_value_rows[:, key_value_width:]], axis=1).astype(
        jnp.bfloat16
    )
    query_turned = apply_rotary(
        query_rows.astype(jnp.float32), request_lengths, QUERY_HEADS
    ).astype(jnp.bfloat16)
    attention_rows = attend(query_turned, newest_token, key_value_cache[0], request_lengths)
    return (attention_rows[None], newest_token[None])


def solution(mesh):
    return jax.shard_map(
        body,
        mesh=mesh,
        in_specs=(
            P("adapter", "group", "tensor"),
            P(),
            P(None, "tensor"),
            P("tensor", None),
            P(("group", "adapter"), "tensor", None),
            P(("group", "adapter"), None, "tensor"),
            P(("group", "adapter"), None, None, None),
            P("adapter", "group"),
            P("adapter", ("group", "tensor"), None, None, None),
            P("adapter", ("group", "tensor")),
        ),
        out_specs=(
            P("adapter", ("group", "tensor"), None),
            P("adapter", ("group", "tensor"), None, None),
        ),
        check_vma=False,
    )
```

profile of v0, /device:TPU:0, one launch (start us, length us, event | category | flops | bytes accessed | tf_op | source)
XLA Modules:
  0.0 274.5 jit_solution(14411248402555921721)
XLA Ops:
  7.2 0.7 all-gather.6.cloned.1.call-update
  7.9 0.7 all-gather.8.cloned.1.call-update
  8.7 0.8 convert_reduce_fusion.1
  10.1 1.1 fusion.42
  11.2 23.1 %psum.14 = f32[128]{0:T(128)S(1)} all-reduce(f32[128]{0:T(128)S(1)} %fusion.42), channel_id=1, replica_groups=mesh['group'=2,'tensor'=8,'adapter'=2] {'tensor'}, use_global_device_ids=true, to_apply=%region_1.0 | all-reduce | flops 128 | bytes 1024 | tf_op jit(solution)/shard_map/psum | solution.py:137
  34.3 0.7 dynamic_slice.13
  35.0 1.1 fusion.44
  36.1 10.1 %while.4 = (s32[]{:T(128)}, bf16[256,1024]{1,0:T(8,128)(2,1)S(1)}, s32[5,2]{0,1:T(2,128)S(1)}, bf16[5,128,1024]{2,1,0:T(8,128)(2,1)}) while((s32[]{:T(128)}, bf16[256,1024]{1,0:T(8,128)(2,1)S(1)}, s32[5,2]{0,1:T(2,128)S(1)}, bf16[5,128,1024]{2,1,0:T(8,128)(2,1)}) %tuple.52), condition=%wide.while_cond.clone, body=%wide.while_body.sunk.clone | while | flops 2 | bytes 525393 | solution.py:105
  36.2 0.5 slice.112
  36.7 1.4 bitcast_dynamic-update-slice_fusion.6
  38.2 0.5 slice.112
  38.7 1.4 bitcast_dynamic-update-slice_fusion.6
  40.7 1.4 bitcast_dynamic-update-slice_fusion.6
  42.3 0.5 slice.112
  42.8 1.4 bitcast_dynamic-update-slice_fusion.6
  44.8 1.4 bitcast_dynamic-update-slice_fusion.6
  46.3 2.1 gather_fusion
  48.4 2.9 %fusion.15 = f32[5,128,192]{1,2,0:T(8,128)} fusion(bf16[5,1024,192]{1,2,0:T(8,128)(2,1)S(1)} %gather_fusion, pred[5]{0:T(512)(128)(4,1)S(1)} %compare_and_fusion.1, bf16[5,128,1024]{2,1,0:T(8,128)(2,1)} %get-tuple-element.9, pred[5,128]{1,0:T(8,128)(4,1)S(1)} %iota_compare_fusion.1), kind=kOutput, calls=%fused_computation.24 | convolution fusion | flops 253296640 | bytes 3768965 | tf_op jit(solution)/shard_map/bsd,bdr->bsr/dot_general | solution.py:159
  51.4 3.9 %fusion.76 = f32[128,2048]{1,0:T(8,128)} fusion(bf16[128,1024]{1,0:T(8,128)(2,1)S(1)} %fusion.44, bf16[1024,2048]{1,0:T(8,128)(2,1)} %param.13), kind=kOutput, calls=%fused_computation.133 | convolution fusion | flops 536870912 | bytes 5505024 | tf_op jit(solution)/shard_map/dot_general | solution.py:147
  55.4 0.5 all-gather.4.cloned.1.call-update
  56.0 0.6 compare_and_fusion
  56.6 2.2 all_gather.14
  58.8 6.7 %fusion.74 = (bf16[16,1,96,1024]{3,2,1,0:T(8,128)(2,1)}, bf16[16,1,96,1024]{3,2,1,0:T(8,128)(2,1)}) fusion(bf16[16,2,96,1024]{3,2,1,0:T(8,128)(2,1)} %bitcast.115), kind=kLoop, calls=%fused_computation.131 | loop fusion | bytes 12582912 | tf_op jit(solution)/shard_map/slice | solution.py:43
  65.5 1.5 gather_fusion.1
  66.9 2.9 %copy.38 = bf16[192,8,8,128]{3,2,1,0:T(8,128)(2,1)S(1)} copy(bf16[192,8,8,128]{3,1,2,0:T(8,128)(2,1)} %bitcast.114) | data formatting | bytes 6291456
  69.8 2.5 copy.41
  72.6 0.7 multiply_cosine_fusion
  73.3 4.0 %gather_fusion.2 = bf16[16,2,64,1024]{3,2,1,0:T(8,128)(2,1)} fusion(bf16[4,2,64,1024]{3,2,1,0:T(8,128)(2,1)} %all-gather.8.cloned.1.call-done, s32[1024]{0:T(1024)S(1)} %pad_clamp_fusion), kind=kCustom, calls=%fused_computation.2 | custom fusion | bytes 8388672 | tf_op jit(solution)/shard_map/jit(_take)/gather | solution.py:179
  77.2 43.8 %all-reduce.5.cloned.1.call-done = f32[5,128,192]{1,2,0:T(8,128)} async-done(((f32[5,128,192]{1,2,0:T(8,128)}), f32[5,128,192]{1,2,0:T(8,128)}) %all-reduce.5.cloned.1.call-update) | async-done | bytes 491536 | tf_op jit(solution)/shard_map/psum | solution.py:162
  121.1 1.9 broadcast_select_fusion
  122.9 2.1 copy.26
  125.1 6.3 %scatter_custom_fusion = f32[256,192]{1,0:T(8,128)S(1)} fusion(s32[640]{0:T(1024)S(1)} %fusion.61, f32[640,192]{1,0:T(8,128)} %bitcast.118, f32[]{:T(128)} %constant.44.clone.1), kind=kCustom, calls=%fused_computation.60 | custom fusion | flops 122880 | bytes 197120 | tf_op jit(solution)/shard_map/scatter-add | solution.py:116
  131.6 3.0 %fusion.2 = f32[16,2,1,1024]{3,2,1,0:T(1,128)S(1)} fusion(bf16[16,2,64,1]{2,3,1,0:T(2,128)(2,1)S(1)} %reshape.545, bf16[16,2,64,1024]{3,2,1,0:T(8,128)(2,1)} %gather_fusion.2, pred[16]{0:T(512)(128)(4,1)} %compare_and_fusion), kind=kOutput, calls=%fused_computation.12 | convolution fusion | flops 6291456 | bytes 4329488 | tf_op jit(solution)/shard_map/rjk,rjkc->rjc/dot_general | solution.py:180
  134.7 6.4 %while.5 = (s32[]{:T(128)}, bf16[256,64]{1,0:T(8,128)(2,1)S(1)}, s32[5,2]{0,1:T(2,128)S(1)}, bf16[5,128,64]{2,1,0:T(8,128)(2,1)S(1)}) while((s32[]{:T(128)}, bf16[256,64]{1,0:T(8,128)(2,1)S(1)}, s32[5,2]{0,1:T(2,128)S(1)}, bf16[5,128,64]{2,1,0:T(8,128)(2,1)S(1)}) %tuple.69), condition=%wide.while_cond.1.clone, body=%wide.while_body.1.sunk.clone | while | flops 2 | bytes 65625 | solution.py:105
  134.8 0.5 slice.113
  135.3 0.7 bitcast_dynamic-update-slice_fusion.7
  136.1 0.5 slice.113
  136.6 0.7 bitcast_dynamic-update-slice_fusion.7
  137.4 0.5 slice.113
  137.9 0.7 bitcast_dynamic-update-slice_fusion.7
  138.6 0.5 slice.113
  139.2 0.7 bitcast_dynamic-update-slice_fusion.7
  139.9 0.5 slice.113
  140.4 0.7 bitcast_dynamic-update-slice_fusion.7
  141.1 3.2 %convolution_select_fusion = f32[5,128,1024]{2,1,0:T(8,128)} fusion(pred[5,128]{1,0:T(8,128)(4,1)} %copy-done.4, bf16[5,64,1024]{2,1,0:T(8,128)(2,1)} %gather_fusion.1, pred[5]{0:T(512)(128)(4,1)} %copy-done.8, bf16[5,128,64]{2,1,0:T(8,128)(2,1)S(1)} %get-tuple-element.17), kind=kOutput, calls=%fused_computation.27 | convolution fusion | flops 84910080 | bytes 3359365 | tf_op jit(solution)/shard_map/bsr,brc->bsc/dot_general | solution.py:167
  144.3 11.3 %scatter_custom_fusion.1 = f32[256,1024]{1,0:T(8,128)} fusion(s32[640]{0:T(1024)} %copy-done.5, f32[640,1024]{1,0:T(8,128)} %bitcast.117, f32[]{:T(128)} %constant.44.clone.1), kind=kCustom, calls=%fused_computation.50 | custom fusion | flops 655360 | bytes 1049088 | tf_op jit(solution)/shard_map/scatter-add | solution.py:116
  155.6 31.5 %reduce-scatter.2.cloned.1.call-done = f32[16,2048]{1,0:T(8,128)} async-done(((f32[128,2048]{1,0:T(8,128)}), f32[16,2048]{1,0:T(8,128)}) %reduce-scatter.2.cloned.1.call-update) | async-done | bytes 131088 | tf_op jit(solution)/shard_map/reduce_scatter | solution.py:173
  187.1 0.9 add.210
  188.1 1.4 multiply_subtract_fusion
  189.5 48.0 %all-gather.4.cloned.1.call-done = bf16[1,128,8192]{2,1,0:T(8,128)(2,1)} async-done(((bf16[1,128,1024]{2,1,0:T(8,128)(2,1)}), bf16[1,128,8192]{2,1,0:T(8,128)(2,1)}) %all-gather.4.cloned.1.call-update) | async-done | bytes 2097168 | tf_op jit(solution)/shard_map/all_gather | solution.py:142
  237.5 9.5 %fusion.35 = bf16[128,1024]{1,0:T(8,128)(2,1)} fusion(bf16[8192,1024]{1,0:T(8,128)(2,1)} %param.12, bf16[1,128,8192]{2,1,0:T(8,128)(2,1)} %all-gather.4.cloned.1.call-done, f32[8192]{0:T(1024)} %param.11, f32[128]{0:T(128)} %copy-done.6, f32[256,1024]{1,0:T(8,128)} %scatter_custom_fusion.1), kind=kOutput, calls=%fused_computation.35 | convolution fusion | flops 2151940096 | bytes 19694080 | tf_op jit(solution)/shard_map/dot_general | solution.py:146
  247.0 3.6 %all-to-all-start = ((bf16[8,16,1024]{2,1,0:T(8,128)(2,1)}), bf16[8,16,1024]{2,1,0:T(8,128)(2,1)S(1)}, u32[]{:S(2)}, u32[]{:S(2)}) async-start(bf16[8,16,1024]{2,1,0:T(8,128)(2,1)} %bitcast.124), calls=%async_computation | async-start | bytes 524288 | tf_op jit(solution)/shard_map/all_to_all | solution.py:172
  250.7 1.5 maximum_convert_fusion
  252.1 1.4 stack.10
  253.5 0.8 pad_maximum_fusion
  254.3 0.7 copy.31
  255.0 0.9 fusion.81
  255.9 3.1 %all-to-all-done = bf16[8,16,1024]{2,1,0:T(8,128)(2,1)S(1)} async-done(((bf16[8,16,1024]{2,1,0:T(8,128)(2,1)}), bf16[8,16,1024]{2,1,0:T(8,128)(2,1)S(1)}, u32[]{:S(2)}, u32[]{:S(2)}) %all-to-all-start) | async-done | bytes 262176 | tf_op jit(solution)/shard_map/all_to_all | solution.py:172
  259.0 1.1 copy.28
  260.1 1.9 reshape.498
  262.0 1.4 subtract_convert_fusion
  263.9 1.9 fusion.75
  266.2 1.0 fusion.32
  267.2 0.8 convert_element_type.121
  (82 shorter events, 4.2 us)
Async XLA Ops:
  7.2 39.2 %all-gather.6.cloned.1.call-start = ((), (), s32[]{:S(2)}) async-start(), calls=%async_computation.3 | async-start | bytes 2359296 | tf_op jit(solution)/shard_map/all_gather | solution.py:149
  7.9 65.4 %all-gather.8.cloned.1.call-start = ((), (), s32[]{:S(2)}) async-start(), calls=%async_computation.6 | async-start | bytes 1572864 | tf_op jit(solution)/shard_map/all_gather | solution.py:151
  8.6 112.4 %all-reduce.5.cloned.1.call-start = ((), (), s32[]{:S(2)}) async-start(), calls=%async_computation.4 | async-start | bytes 983040 | tf_op jit(solution)/shard_map/psum | solution.py:162
  34.3 14.1 %copy-start.6 = (f32[128]{0:T(128)}, f32[128]{0:T(128)S(1)}, u32[]{:S(2)}) copy-start(f32[128]{0:T(128)S(1)} %add_rsqrt_fusion) | copy-start | bytes 1540
  46.2 5.1 %copy-start.8 = (pred[5]{0:T(512)(128)(4,1)}, pred[5]{0:T(512)(128)(4,1)S(1)}, u32[]{:S(2)}) copy-start(pred[5]{0:T(512)(128)(4,1)S(1)} %compare_and_fusion.1) | copy-start | bytes 19
  46.3 74.8 %copy-start.4 = (pred[5,128]{1,0:T(8,128)(4,1)}, pred[5,128]{1,0:T(8,128)(4,1)S(1)}, u32[]{:S(2)}) copy-start(pred[5,128]{1,0:T(8,128)(4,1)S(1)} %iota_compare_fusion.1) | copy-start | bytes 1924
  51.3 4.6 %copy-start.9 = (s32[1,128]{1,0:T(1,128)S(1)}, s32[1,128]{1,0:T(1,128)}, u32[]{:S(2)}) copy-start(s32[1,128]{1,0:T(1,128)} %param.17) | copy-start | bytes 1540
  51.3 5.3 %copy-start.2 = (bf16[2,64,1024]{2,1,0:T(8,128)(2,1)S(1)}, bf16[2,64,1024]{2,1,0:T(8,128)(2,1)}, u32[]{:S(2)}) copy-start(bf16[2,64,1024]{2,1,0:T(8,128)(2,1)} %param.15) | copy-start | bytes 786436
  51.4 135.8 %reduce-scatter.2.cloned.1.call-start = ((), (), s32[]{:S(2)}) async-start(), calls=%async_computation.5 | async-start | bytes 1179648 | tf_op jit(solution)/shard_map/reduce_scatter | solution.py:173
  55.3 182.1 %all-gather.4.cloned.1.call-start = ((), (), s32[]{:S(2)}) async-start(), calls=%async_computation.2 | async-start | bytes 2359296 | tf_op jit(solution)/shard_map/all_gather | solution.py:142
  66.9 2.9 %copy-start = (bf16[16,1,96,1024]{3,2,1,0:T(8,128)(2,1)S(1)}, bf16[16,1,96,1024]{3,2,1,0:T(8,128)(2,1)}, u32[]{:S(2)}) copy-start(bf16[16,1,96,1024]{3,2,1,0:T(8,128)(2,1)} %get-tuple-element.46) | copy-start | bytes 9437188
  69.8 2.6 copy-start.7
  72.5 52.6 %copy-start.5 = (s32[640]{0:T(1024)}, s32[640]{0:T(1024)S(1)}, u32[]{:S(2)}) copy-start(s32[640]{0:T(1024)S(1)} %fusion.61) | copy-start | bytes 7684
  131.6 3.2 %copy-start.3 = (bf16[5,128,64]{2,1,0:T(8,128)(2,1)S(1)}, bf16[5,128,64]{2,1,0:T(8,128)(2,1)}, u32[]{:S(2)}) copy-start(bf16[5,128,64]{2,1,0:T(8,128)(2,1)} %custom-call.7) | copy-start | bytes 245764
  247.0 11.9 %all-to-all-start = ((bf16[8,16,1024]{2,1,0:T(8,128)(2,1)}), bf16[8,16,1024]{2,1,0:T(8,128)(2,1)S(1)}, u32[]{:S(2)}, u32[]{:S(2)}) async-start(bf16[8,16,1024]{2,1,0:T(8,128)(2,1)} %bitcast.124), calls=%async_computation | async-start | bytes 524288 | tf_op jit(solution)/shard_map/all_to_all | solution.py:172
  263.5 2.7 copy-start.1
Sparse Core Ops, SparseCore 0:
  9.5 12.4 all-gather.5
  23.6 10.2 all-gather.7
  51.4 69.5 all-reduce.4
  124.7 62.3 reduce-scatter.1
  189.2 48.2 all-gather.3
where the time goes:
time: 276 us; the launch traced here: 275 us
  waiting for transfers between devices  128 us (46%)
  local copies, waits for them, and re-layouts  45.1 us (16%)
  other arithmetic  32 us (12%)
  matrix products  25.7 us (9%)
  blocking collectives  25.3 us (9%)
  between operations  14.1 us (5%)
  starting transfers between devices  3.83 us (1%)
    all_gather x1, waiting for transfers between devices, body(): lax.all_gather(hidden, 'tensor', axis=2, tiled=True)[0].astype(jnp.float32)  48 us
    psum x1, waiting for transfers between devices, body(): summed_blocks = lax.psum(shrink_blocks, 'tensor')  43.8 us
    reduce_scatter x1, waiting for transfers between devices, body(): lax.psum_scatter(kv_term, 'tensor', scatter_dimension=0, tiled=True)  31.5 us
    psum x1, blocking collectives, body(): squares = lax.psum(jnp.sum(local_wide * local_wide, axis=1), 'tensor')  23.1 us
    scatter-add x2, other arithmetic, to_rows(): result = result.at[targets].add(blocks.reshape(-1, blocks.shape[2]))  17.6 us
    gather x30, local copies, waits for them, and re-layouts  16.3 us
    dot_general x1, matrix products, body(): jnp.dot(scaled, query_weight, preferred_element_type=jnp.float32)  9.52 us
    slice x1, local copies, waits for them, and re-layouts, attend(): layer_cache[:, 0]  6.71 us
  transfers between devices with their start and end apart: 6, of which 4 were waited for; matrix products, arithmetic and copies ran while one was open for 31% of the time, Pallas kernels for 0%

commit v1 on v0

v1 whole, which is shorter than its diff:
```python
import functools
import math

import jax
import jax.numpy as jnp
import numpy as np
from jax import lax
from jax.experimental import pallas as pl
from jax.experimental.pallas import tpu as pltpu
from jax.sharding import PartitionSpec as P

HEAD_WIDTH = 128
LANES = 128
EPS = 1e-05
THETA = 500000.0
F32 = jnp.float32
BF16 = jnp.bfloat16
VMEM_LIMIT = 48 * 1024 * 1024


def ring_order(size):
    if size == 8:
        return [0, 2, 4, 6, 7, 5, 3, 1]
    return list(range(size))


def dot(a, b):
    return jnp.dot(a, b, preferred_element_type=F32)


def params(**more):
    return pltpu.CompilerParams(vmem_limit_bytes=VMEM_LIMIT, **more)


def after(value, *others):
    return lax.optimization_barrier((value, *others))[0]


def whole(shape):
    return pl.BlockSpec(shape, lambda *_: (0,) * len(shape))


def rotary_tables(positions):
    half = HEAD_WIDTH // 2
    frequency = THETA ** (-(jnp.arange(half).astype(F32) * 2.0 / HEAD_WIDTH))
    angles = positions.astype(F32)[:, None] * frequency[None, :]
    cosine = jnp.cos(angles)
    sine = jnp.sin(angles)
    return jnp.concatenate([cosine, cosine], axis=1), jnp.concatenate([-sine, sine], axis=1)


def rotate_heads(values, cosine, sine):
    turned = []
    for head in range(values.shape[1] // HEAD_WIDTH):
        part = values[:, head * HEAD_WIDTH : (head + 1) * HEAD_WIDTH]
        turned.append(part * cosine + pltpu.roll(part, HEAD_WIDTH // 2, 1) * sine)
    return jnp.concatenate(turned, axis=1)


def note_kernel(hidden_ref, lengths_ref, out_ref):
    wide = hidden_ref[...].astype(F32)
    squares = wide * wide
    rows, width = squares.shape
    lanes = squares[:, :LANES]
    for at in range(LANES, width, LANES):
        lanes = lanes + squares[:, at : at + LANES]
    sums = jnp.sum(lanes.T, axis=0, keepdims=True)
    row = lax.broadcasted_iota(jnp.int32, (8, rows), 0)
    out_ref[...] = jnp.where(row == 0, sums, jnp.where(row == 1, lengths_ref[...], 0.0))


def note(hidden, placed_lengths):
    return pl.pallas_call(
        note_kernel,
        out_shape=jax.ShapeDtypeStruct((8, hidden.shape[0]), F32),
        compiler_params=params(),
        cost_estimate=pl.CostEstimate(flops=100000, bytes_accessed=300000, transcendentals=0),
        name="square_sums",
    )(hidden, placed_lengths)


def prep_kernel(
    rank, scalar_ref, here_ref, there_ref, hidden_ref, gain_ref, ids_ref, own_ref, other_ref, weight_hbm,
    inverse_ref, keep_ref, give_ref, shrink_ref, kv_ref, weight_ref, sems,
):
    rows, width = hidden_ref.shape
    model_width = gain_ref.shape[0] * width
    chunks = sems.shape[0]
    depth = width // chunks
    copies = [
        pltpu.make_async_copy(
            weight_hbm.at[pl.ds(c * depth, depth)], weight_ref.at[pl.ds(c * depth, depth)], sems.at[c]
        )
        for c in range(chunks)
    ]
    for copy in copies:
        copy.start()
    total = here_ref[:1] + there_ref[:1]
    inverse_row = lax.rsqrt(total / model_width + EPS)
    inverse = jnp.broadcast_to(inverse_row, (LANES, rows)).T
    inverse_ref[...] = inverse
    gain = gain_ref[pl.ds(scalar_ref[0, 2], 1)].reshape(1, width)
    normed = (hidden_ref[...].astype(F32) * inverse[:, :1] * gain).astype(BF16)
    shrink = jnp.zeros((rows, 3 * rank), F32)
    for side, panel_ref in enumerate((own_ref, other_ref)):
        for j in range(panel_ref.shape[0]):
            part = lax.dot_general(normed, panel_ref[j], (((1,), (1,)), ((), ())), preferred_element_type=F32)
            shrink = shrink + jnp.where(ids_ref[:, :1] == scalar_ref[0, side] + j, part, 0.0)
    half = rows // 2
    packed = jnp.concatenate([shrink[:half, :rank], shrink[half:, :rank]], axis=1)
    tensor, page, _ = shrink_ref.shape
    own_rows = page - half
    for peer in range(tensor):
        shrink_ref[peer, :half] = packed
        shrink_ref[peer, half:] = shrink[peer * own_rows : (peer + 1) * own_rows, rank:]
    total = None
    for c, copy in enumerate(copies):
        copy.wait()
        part = dot(normed[:, c * depth : (c + 1) * depth], weight_ref[c * depth : (c + 1) * depth])
        total = part if total is None else total + part
    kv_ref[...] = total
    parity = scalar_ref[0, 2] % 2
    for pair in range(tensor // 2):
        keep_ref[pair] = kv_ref[pl.ds(pl.multiple_of((2 * pair + parity) * own_rows, own_rows), own_rows)]
        give_ref[pair] = kv_ref[pl.ds(pl.multiple_of((2 * pair + 1 - parity) * own_rows, own_rows), own_rows)]


def prep(scalars, here, there, hidden, gains, ids, weight, own, other, rank, tensor):
    rows, width = hidden.shape
    columns = weight.shape[1]
    chunks = 4 if width % 1024 == 0 else 1
    page = rows // 2 + rows // tensor
    vmem = pl.BlockSpec(memory_space=pltpu.VMEM)
    return pl.pallas_call(
        functools.partial(prep_kernel, rank),
        in_specs=[pl.BlockSpec(memory_space=pltpu.SMEM)] + [vmem] * 7 + [pl.BlockSpec(memory_space=pl.ANY)],
        out_specs=[vmem] * 4,
        out_shape=[
            jax.ShapeDtypeStruct((rows, LANES), F32),
            jax.ShapeDtypeStruct((tensor // 2, rows // tensor, columns), F32),
            jax.ShapeDtypeStruct((tensor // 2, rows // tensor, columns), F32),
            jax.ShapeDtypeStruct((tensor, page, LANES), F32),
        ],
        scratch_shapes=[
            pltpu.VMEM((rows, columns), F32),
            pltpu.VMEM(weight.shape, BF16),
            pltpu.SemaphoreType.DMA((chunks,)),
        ],
        compiler_params=params(),
        cost_estimate=pl.CostEstimate(flops=700000000, bytes_accessed=6000000, transcendentals=0),
        name="norm_key_value_shrink",
    )(scalars, here, there, hidden, gains, ids, own, other, weight)


def query_kernel(count, columns_at, first, scalar_ref, *refs):
    blocks = refs[:count]
    gain_ref, inverse_ref = refs[count : count + 2]
    weight_hbm = refs[-4]
    out_ref, weight_ref, sems = refs[-3:]
    width = blocks[0].shape[1]
    owners = [scalar_ref[0, columns_at + i] for i in range(count)]
    copies = [
        pltpu.make_async_copy(weight_hbm.at[pl.ds(owners[i] * width, width)], weight_ref.at[i], sems.at[i])
        for i in range(count)
    ]
    for copy in copies:
        copy.start()
    inverse = inverse_ref[:, :1]
    total = None if first else refs[count + 2][...]
    for i in range(count):
        gain = gain_ref[pl.ds(owners[i], 1)].reshape(1, width)
        normed = (blocks[i][...].astype(F32) * inverse * gain).astype(BF16)
        copies[i].wait()
        part = dot(normed, weight_ref[i])
        total = part if total is None else total + part
    out_ref[...] = total


def query_step(scalars, columns_at, blocks, gains, weight, inverse, acc):
    rows, width = blocks[0].shape
    columns = weight.shape[1]
    count = len(blocks)
    vmem = pl.BlockSpec(memory_space=pltpu.VMEM)
    operands = list(blocks) + [gains, inverse] + ([] if acc is None else [acc])
    return pl.pallas_call(
        functools.partial(query_kernel, count, columns_at, acc is None),
        in_specs=[pl.BlockSpec(memory_space=pltpu.SMEM)]
        + [vmem] * len(operands)
        + [pl.BlockSpec(memory_space=pl.ANY)],
        out_specs=vmem,
        out_shape=jax.ShapeDtypeStruct((rows, columns), F32),
        scratch_shapes=[pltpu.VMEM((count, width, columns), BF16), pltpu.SemaphoreType.DMA((count,))],
        compiler_params=params(),
        cost_estimate=pl.CostEstimate(flops=500000000, bytes_accessed=5000000, transcendentals=0),
        name="query_products",
    )(scalars, *operands, weight)


def delta_kernel(
    rank, first_ref, parts_ref, ids_ref, own_ids_ref, up_own_ref, up_other_ref, kv_own_ref, kv_other_ref,
    delta_ref, kv_delta_ref,
):
    rows = ids_ref.shape[0]
    half = rows // 2
    kv_width = kv_delta_ref.shape[1] // 2
    total = parts_ref[0]
    for peer in range(1, parts_ref.shape[0]):
        total = total + parts_ref[peer]
    shrink = jnp.concatenate([total[:half, :rank], total[:half, rank:]], axis=0)
    own = total[half:]
    delta = None
    key_delta = value_delta = None
    for side, (up_ref, kv_ref) in enumerate(((up_own_ref, kv_own_ref), (up_other_ref, kv_other_ref))):
        for j in range(up_ref.shape[0]):
            mine = ids_ref[:, :1] == first_ref[0, side] + j
            part = dot(jnp.where(mine, shrink, 0.0).astype(BF16), up_ref[j])
            delta = part if delta is None else delta + part
            kept = jnp.where(own_ids_ref[:, :1] == first_ref[0, side] + j, own, 0.0).astype(BF16)
            key_part = dot(kept[:, :rank], kv_ref[j, 0])
            value_part = dot(kept[:, rank:], kv_ref[j, 1])
            key_delta = key_part if key_delta is None else key_delta + key_part
            value_delta = value_part if value_delta is None else value_delta + value_part
    delta_ref[...] = delta
    kv_delta_ref[:, :kv_width] = key_delta
    kv_delta_ref[:, kv_width:] = value_delta


def deltas(scalars, parts, ids, own_ids, ups, kv_ups, rank):
    rows, own_rows = ids.shape[0], own_ids.shape[0]
    columns = ups[0].shape[2]
    kv_columns = 2 * kv_ups[0].shape[3]
    vmem = pl.BlockSpec(memory_space=pltpu.VMEM)
    return pl.pallas_call(
        functools.partial(delta_kernel, rank),
        in_specs=[pl.BlockSpec(memory_space=pltpu.SMEM)] + [vmem] * 7,
        out_specs=[vmem, vmem],
        out_shape=[
            jax.ShapeDtypeStruct((rows, columns), F32),
            jax.ShapeDtypeStruct((own_rows, kv_columns), F32),
        ],
        compiler_params=params(),
        cost_estimate=pl.CostEstimate(flops=100000000, bytes_accessed=2000000, transcendentals=0),
        name="adapter_terms",
    )(scalars, parts, ids, own_ids, *ups, *kv_ups)


def finish_kernel(
    column_at, scalar_ref, top_ref, bottom_ref, gain_ref, inverse_ref, acc_ref, delta_ref, cosine_ref, sine_ref,
    weight_hbm, out_ref, weight_ref, sems,
):
    width = top_ref.shape[1]
    chunks = sems.shape[0]
    depth = width // chunks
    owner = scalar_ref[0, column_at]
    copies = [
        pltpu.make_async_copy(
            weight_hbm.at[pl.ds(owner * width + c * depth, depth)], weight_ref.at[pl.ds(c * depth, depth)], sems.at[c]
        )
        for c in range(chunks)
    ]
    for copy in copies:
        copy.start()
    gain = gain_ref[pl.ds(owner, 1)].reshape(1, width)
    block = jnp.concatenate([top_ref[...], bottom_ref[...]], axis=0).astype(F32)
    normed = (block * inverse_ref[:, :1] * gain).astype(BF16)
    total = acc_ref[...] + delta_ref[...]
    for c, copy in enumerate(copies):
        copy.wait()
        total = total + dot(normed[:, c * depth : (c + 1) * depth], weight_ref[c * depth : (c + 1) * depth])
    raw = total.astype(BF16).astype(F32)
    out_ref[...] = rotate_heads(raw, cosine_ref[...], sine_ref[...]).astype(BF16)


def finish(scalars, column_at, top, bottom, gains, weight, inverse, acc, delta, cosine, sine):
    width = top.shape[1]
    rows, columns = acc.shape
    chunks = 2 if width % 1024 == 0 else 1
    vmem = pl.BlockSpec(memory_space=pltpu.VMEM)
    return pl.pallas_call(
        functools.partial(finish_kernel, column_at),
        in_specs=[pl.BlockSpec(memory_space=pltpu.SMEM)] + [vmem] * 8 + [pl.BlockSpec(memory_space=pl.ANY)],
        out_specs=vmem,
        out_shape=jax.ShapeDtypeStruct((rows, columns), BF16),
        scratch_shapes=[pltpu.VMEM((width, columns), BF16), pltpu.SemaphoreType.DMA((chunks,))],
        compiler_params=params(),
        cost_estimate=pl.CostEstimate(flops=270000000, bytes_accessed=3000000, transcendentals=0),
        name="query_finish",
    )(scalars, top, bottom, gains, inverse, acc, delta, cosine, sine, weight)


def pair_kernel(scalar_ref, keep_ref, got_ref, *out_refs):
    index = lax.div(scalar_ref[0, 2], 2)
    for distance, out_ref in enumerate(out_refs):
        other = index ^ distance
        out_ref[...] = keep_ref[other] + got_ref[other]


def pair_sums(scalars, keep, got):
    count, own_rows, columns = keep.shape
    vmem = pl.BlockSpec(memory_space=pltpu.VMEM)
    return pl.pallas_call(
        pair_kernel,
        in_specs=[pl.BlockSpec(memory_space=pltpu.SMEM), vmem, vmem],
        out_specs=[vmem] * count,
        out_shape=[jax.ShapeDtypeStruct((own_rows, columns), F32)] * count,
        compiler_params=params(),
        cost_estimate=pl.CostEstimate(flops=100000, bytes_accessed=1500000, transcendentals=0),
        name="pair_sums",
    )(scalars, keep, got)


def fresh_kernel(count, *refs):
    parts = refs[:count]
    delta_ref, cosine_ref, sine_ref, out_ref = refs[count:]
    total = parts[0][...]
    for part in parts[1:]:
        total = total + part[...]
    total = total + delta_ref[...]
    kv_width = total.shape[1] // 2
    out_ref[:, :kv_width] = rotate_heads(total[:, :kv_width], cosine_ref[...], sine_ref[...]).astype(BF16)
    out_ref[:, kv_width:] = total[:, kv_width:].astype(BF16)


def fresh(parts, delta, cosine, sine):
    return pl.pallas_call(
        functools.partial(fresh_kernel, len(parts)),
        out_shape=jax.ShapeDtypeStruct(delta.shape, BF16),
        compiler_params=params(),
        cost_estimate=pl.CostEstimate(flops=100000, bytes_accessed=1000000, transcendentals=0),
        name="new_key_value",
    )(*parts, delta, cosine, sine)


def attend(query_rows, new_key, new_value, cache, lengths):
    tensor, own_rows, columns = query_rows.shape
    positions = cache.shape[2]
    kv_width = cache.shape[3]
    key_heads = kv_width // HEAD_WIDTH
    groups = columns * tensor // kv_width
    scale = 1.0 / math.sqrt(HEAD_WIDTH)
    query_heads = (
        query_rows.reshape(tensor, own_rows, -1, HEAD_WIDTH)
        .transpose(1, 0, 2, 3)
        .reshape(own_rows, key_heads, groups, HEAD_WIDTH)
    )
    keys = cache[:, 0].reshape(own_rows, positions, key_heads, HEAD_WIDTH)
    values = cache[:, 1].reshape(own_rows, positions, key_heads, HEAD_WIDTH)
    fresh_key = new_key.reshape(own_rows, key_heads, HEAD_WIDTH)
    fresh_value = new_value.reshape(own_rows, key_heads, HEAD_WIDTH)
    scores = jnp.einsum("rkgd,rpkd->rkgp", query_heads, keys, preferred_element_type=F32) * scale
    visible = jnp.arange(positions)[None, :] < lengths[:, None]
    scores = jnp.where(visible[:, None, None, :], scores, F32(-1e30))
    new_score = jnp.einsum("rkgd,rkd->rkg", query_heads, fresh_key, preferred_element_type=F32) * scale
    top = jnp.maximum(jnp.max(scores, axis=-1), new_score)
    weights = jnp.exp(scores - top[..., None])
    new_weight = jnp.exp(new_score - top)
    denominator = jnp.sum(weights, axis=-1) + new_weight
    cache_weights = (weights / denominator[..., None]).astype(BF16)
    fresh_weights = (new_weight / denominator).astype(BF16)
    mixed = jnp.einsum("rkgp,rpkd->rkgd", cache_weights, values, preferred_element_type=F32)
    mixed = mixed + fresh_weights.astype(F32)[..., None] * fresh_value.astype(F32)[:, :, None, :]
    return mixed.reshape(own_rows, -1).astype(BF16)


def make_body(mesh):
    tensor = mesh.shape["tensor"]
    shards = mesh.shape["adapter"]
    order = ring_order(tensor)
    place_of = [order.index(t) for t in range(tensor)]
    right = [(order[i], order[(i + 1) % tensor]) for i in range(tensor)]
    left = [(b, a) for a, b in right]
    swap = [(i, shards - 1 - i) for i in range(shards)]

    distances = [1 << k for k in range(tensor.bit_length() - 1)]

    def table(own_adapters):
        lines = []
        for side in range(shards):
            for position in range(tensor):
                place = place_of[position]
                steps = [0] + [sign * step for step in range(1, tensor // 2) for sign in (-1, 1)] + [tensor // 2]
                owners = [order[(place + step) % tensor] for step in steps]
                lines.append([side * own_adapters, (shards - 1 - side) * own_adapters, position] + owners)
        return np.array(lines, np.int32)

    def everyone(x):
        return lax.all_to_all(x, "tensor", 0, 0, tiled=True)

    def body(
        hidden,
        input_norm_scale,
        query_weight,
        key_value_weight,
        adapter_down_weight,
        adapter_up_query,
        adapter_up_key_value,
        request_adapter,
        key_value_cache,
        lengths,
    ):
        position = lax.axis_index("tensor")
        side = lax.axis_index("adapter")
        local = hidden[0]
        rows, width = local.shape
        own_rows = rows // tensor
        start = position * own_rows
        own_adapters = adapter_down_weight.shape[0]
        rank = adapter_up_query.shape[1]
        kv_width = adapter_up_key_value.shape[3]
        gains = input_norm_scale.reshape(tensor, 1, width)
        ids = jnp.broadcast_to(request_adapter[0][:, None], (rows, LANES))
        own_ids = lax.dynamic_slice_in_dim(ids, start, own_rows, 0)
        scalars = lax.dynamic_slice_in_dim(jnp.asarray(table(own_adapters)), side * tensor + position, 1, 0)

        placed = lax.dynamic_update_slice_in_dim(jnp.zeros((rows,), F32), lengths[0].astype(F32), start, 0)
        here = note(local, placed[None])
        sent = after(local, here)
        from_left = lax.ppermute(sent, "tensor", right)
        from_right = lax.ppermute(sent, "tensor", left)
        for distance in distances:
            there = lax.ppermute(here, "tensor", [(t, t ^ distance) for t in range(tensor)])
            if distance != distances[-1]:
                here = here + there
        cosine, sine = rotary_tables(here[1] + there[1])
        own_cosine = lax.dynamic_slice_in_dim(cosine, start, own_rows, 0)
        own_sine = lax.dynamic_slice_in_dim(sine, start, own_rows, 0)

        own_down = adapter_down_weight.transpose(0, 2, 1)
        other_down, other_up, other_kv = (
            lax.ppermute(w, "adapter", swap) for w in (own_down, adapter_up_query, adapter_up_key_value)
        )
        inverse, keep, give, shrink = prep(
            scalars, here, there, local, gains, ids, key_value_weight, own_down, other_down, rank, tensor
        )
        shrink_parts = everyone(shrink)
        got = lax.ppermute(give, "tensor", [(t, t ^ 1) for t in range(tensor)])
        sums = pair_sums(scalars, keep, got)
        kv_parts = [sums[0]] + [
            lax.ppermute(sums[d], "tensor", [(t, t ^ (2 * d)) for t in range(tensor)]) for d in range(1, tensor // 2)
        ]
        delta, kv_delta = deltas(
            scalars, shrink_parts, ids, own_ids, (adapter_up_query, other_up), (adapter_up_key_value, other_kv), rank
        )

        early = tensor // 2 - 1
        arrived = [local, from_left, from_right]
        acc = None
        column_at = 3
        half = rows // 2
        for step in range(2, tensor // 2 + 1):
            if step == early:
                from_left, from_right = after((from_left, from_right), inverse)
            if step == tensor // 2:
                acc = query_step(scalars, column_at, arrived, gains, query_weight, inverse, acc)
                column_at += len(arrived)
                arrived = []
                last_left, last_right = after((from_left[:half], from_right[half:]), acc)
                top = lax.ppermute(last_left, "tensor", right)
                bottom = lax.ppermute(last_right, "tensor", left)
            else:
                from_left = lax.ppermute(from_left, "tensor", right)
                from_right = lax.ppermute(from_right, "tensor", left)
                if step == early:
                    acc = query_step(scalars, column_at, arrived, gains, query_weight, inverse, acc)
                    column_at += len(arrived)
                    arrived = []
                arrived += [from_left, from_right]
        query = finish(
            scalars, 2 + tensor, top, bottom, gains, query_weight, inverse, acc, delta, cosine, sine
        )
        query_rows = everyone(query.reshape(tensor, own_rows, -1))

        newest = fresh(kv_parts, kv_delta, own_cosine, own_sine)
        attended = attend(query_rows, newest[:, :kv_width], newest[:, kv_width:], key_value_cache[0], lengths[0])
        return attended[None], newest.reshape(1, own_rows, 2, kv_width)

    return body


def solution(mesh):
    return jax.shard_map(
        make_body(mesh),
        mesh=mesh,
        in_specs=(
            P("adapter", "group", "tensor"),
            P(),
            P(None, "tensor"),
            P("tensor", None),
            P(("group", "adapter"), "tensor", None),
            P(("group", "adapter"), None, "tensor"),
            P(("group", "adapter"), None, None, None),
            P("adapter", "group"),
            P("adapter", ("group", "tensor"), None, None, None),
            P("adapter", ("group", "tensor")),
        ),
        out_specs=(
            P("adapter", ("group", "tensor"), None),
            P("adapter", ("group", "tensor"), None, None),
        ),
        check_vma=False,
    )
```

time: 276 us -> 92.9 us (0.34)
  waiting for transfers between devices: 128 us -> 17.4 us
  other arithmetic: 32 us -> 1.7 us
  local copies, waits for them, and re-layouts: 45.1 us -> 19.2 us
  blocking collectives: 25.3 us -> 0 us
  starting transfers between devices: 3.83 us -> 27.9 us
  matrix products: 25.7 us -> 4.97 us
  Pallas kernels: 0 us -> 20.3 us
  between operations: 14.1 us -> 0.95 us
    all_gather x3 -> x0, waiting for transfers between devices: 48 us -> none  [the longest x1 48 us: body(): lax.all_gather(hidden, 'tensor', axis=2, tiled=True)[0].astype(jnp.float32)]
    psum x1 -> x0, waiting for transfers between devices: 43.8 us -> none  [body(): summed_blocks = lax.psum(shrink_blocks, 'tensor')]
    reduce_scatter x1 -> x0, waiting for transfers between devices: 31.5 us -> none  [body(): lax.psum_scatter(kv_term, 'tensor', scatter_dimension=0, tiled=True)]
    gather x33 -> x0, local copies, waits for them, and re-layouts: 23.8 us -> none
    psum x1 -> x0, blocking collectives: 23.1 us -> none  [body(): squares = lax.psum(jnp.sum(local_wide * local_wide, axis=1), 'tensor')]
    dot_general x8 -> x3, matrix products: 25.7 us -> 4.97 us  [the longest x1 3.69 us: attend(): jnp.einsum('rkgd,rpkd->rkgp', query_heads, keys, preferred_element_type=F32)]
    ppermute x0 -> x18, starting transfers between devices: none -> 20.6 us  [the longest x3 7.39 us: body(): lax.ppermute(here, 'tensor', [(t, t ^ distance) for t in range(tensor)])]
    pallas_call x0 -> x8, Pallas kernels: none -> 20.3 us  [the longest x2 8.9 us: query_step(): pl.pallas_call(functools.partial(query_kernel, count, columns_at, acc is...]
  transfers between devices with their start and end apart: 6 -> 20, of which waited for: 4 -> 2; matrix products, arithmetic and copies ran while one was open for 31% -> 19% of each run, Pallas kernels for 0% -> 22%
where the time goes in v1:
time: 92.9 us; the launch traced here: 92.4 us
  starting transfers between devices  27.9 us (30%)
  Pallas kernels  20.3 us (22%)
  local copies, waits for them, and re-layouts  19.2 us (21%)
  waiting for transfers between devices  17.4 us (19%)
  matrix products  4.97 us (5%)
  other arithmetic  1.7 us (2%)
  between operations  0.95 us (1%)
    ppermute x2, waiting for transfers between devices, body(): from_left = lax.ppermute(from_left, 'tensor', right)  12.1 us
    pallas_call x2, Pallas kernels, query_step(): pl.pallas_call(functools.partial(query_kernel, count, columns_at, acc is...  8.9 us
    unnamed x32, local copies, waits for them, and re-layouts  8.7 us
    ppermute x3, starting transfers between devices, body(): lax.ppermute(here, 'tensor', [(t, t ^ distance) for t in range(tensor)])  7.39 us
    all_to_all x2, starting transfers between devices, everyone(): return lax.all_to_all(x, 'tensor', 0, 0, tiled=True)  7.27 us
    slice x1, local copies, waits for them, and re-layouts, attend(): keys = cache[:, 0].reshape(own_rows, positions, key_heads, HEAD_WIDTH)  6.72 us
    ppermute x3, waiting for transfers between devices, body(): lax.ppermute(here, 'tensor', [(t, t ^ distance) for t in range(tensor)])  5.23 us
    pallas_call x1, Pallas kernels, prep(): pl.pallas_call(functools.partial(prep_kernel, rank), in_specs=[pl.BlockSp...  4.48 us
  transfers between devices with their start and end apart: 20, of which 2 were waited for; matrix products, arithmetic and copies ran while one was open for 19% of the time, Pallas kernels for 22%

profile of v1, /device:TPU:0, one launch (start us, length us, event | category | flops | bytes accessed | tf_op | source)
XLA Modules:
  0.0 92.4 jit_solution(2066499917327877302)
XLA Ops:
  0.6 0.7 convert_element_type.43
  1.3 0.1 dynamic_update_slice.4.lengths_ref
  1.4 0.0 copy-start
  1.4 0.9 %copy-done = bf16[1,128,1024]{2,1,0:T(8,128)(2,1)S(1)} copy-done((bf16[1,128,1024]{2,1,0:T(8,128)(2,1)S(1)}, bf16[1,128,1024]{2,1,0:T(8,128)(2,1)}, u32[]{:S(2)}) %copy-start) | copy-done | bytes 262168
  2.3 0.1 square_sums.1
  2.5 3.1 %collective-permute-start.4 = (f32[8,128]{1,0:T(8,128)S(1)}, f32[8,128]{1,0:T(8,128)S(1)}, u32[]{:S(2)}, u32[]{:S(2)}) collective-permute-start(f32[8,128]{1,0:T(8,128)S(1)} %square_sums.1), channel_id=1, source_target_pairs={{0,2},{2,0},{4,6},{6,4},{8,10},{10,8},{12,14},{14,12},{1,3},{3,1},... | collective-permute-start | bytes 12296 | tf_op jit(solution)/shard_map/ppermute | solution.py:421
  5.6 1.6 %collective-permute-start = (bf16[128,1024]{1,0:T(8,128)(2,1)S(1)}, bf16[128,1024]{1,0:T(8,128)(2,1)S(1)}, u32[]{:S(2)}, u32[]{:S(2)}) collective-permute-start(bf16[128,1024]{1,0:T(8,128)(2,1)S(1)} %bitcast.53), channel_id=1, source_target_pairs={{0,4},{4,8},{8,12},{12,14},{14,10},{10,6},{6,2},{2,0},{1,5},{5,9},... | collective-permute-start | bytes 786440 | tf_op jit(solution)/shard_map/ppermute | solution.py:418
  7.2 0.4 collective-permute-start.2
  7.6 0.0 collective-permute-start.7
  7.6 0.5 collective-permute-start.13
  8.2 6.7 %fusion.30 = (bf16[16,1,96,1024]{3,2,1,0:T(8,128)(2,1)}, bf16[16,1,96,1024]{3,2,1,0:T(8,128)(2,1)}) fusion(bf16[16,2,96,1024]{3,2,1,0:T(8,128)(2,1)} %bitcast.66), kind=kLoop, calls=%fused_computation.41 | loop fusion | bytes 12582912 | tf_op jit(solution)/shard_map/slice | solution.py:346
  14.9 0.0 collective-permute-done.4
  14.9 1.6 %collective-permute-start.5 = (f32[8,128]{1,0:T(8,128)S(1)}, f32[8,128]{1,0:T(8,128)S(1)}, u32[]{:S(2)}, u32[]{:S(2)}) collective-permute-start(f32[8,128]{1,0:T(8,128)S(1)} %add.37), channel_id=1, source_target_pairs={{0,4},{2,6},{4,0},{6,2},{8,12},{10,14},{12,8},{14,10},{1,5},{3,7},... | collective-permute-start | bytes 12296 | tf_op jit(solution)/shard_map/ppermute | solution.py:421
  16.5 0.0 collective-permute-done.refs_1_
  16.5 0.5 collective-permute-start.1
  17.0 1.6 %collective-permute-start.3 = (bf16[128,1024]{1,0:T(8,128)(2,1)}, bf16[128,1024]{1,0:T(8,128)(2,1)}, u32[]{:S(2)}, u32[]{:S(2)}) collective-permute-start(bf16[128,1024]{1,0:T(8,128)(2,1)} %collective-permute-done.2.refs_2_), channel_id=1, source_target_pairs={{4,0},{8,4},{12,8},{14,12},{10,14},{6,10},{2,6},{0,2},{5,1},{9,5},... | collective-permute-start | bytes 786440 | tf_op jit(solution)/shard_map/ppermute | solution.py:462
  18.6 0.1 fusion.29
  18.7 2.6 %collective-permute-start.6 = (f32[8,128]{1,0:T(8,128)S(1)}, f32[8,128]{1,0:T(8,128)S(1)}, u32[]{:S(2)}, u32[]{:S(2)}) collective-permute-start(f32[8,128]{1,0:T(8,128)S(1)} %add.38.here_ref), channel_id=1, source_target_pairs={{0,8},{2,10},{4,12},{6,14},{8,0},{10,2},{12,4},{14,6},{1,9},{3,11}... | collective-permute-start | bytes 12296 | tf_op jit(solution)/shard_map/ppermute | solution.py:421
  21.3 0.7 constant_dynamic-slice_fusion.1.scalar_ref.first_ref
  22.0 5.2 %collective-permute-done.6.there_ref = f32[8,128]{1,0:T(8,128)S(1)} collective-permute-done((f32[8,128]{1,0:T(8,128)S(1)}, f32[8,128]{1,0:T(8,128)S(1)}, u32[]{:S(2)}, u32[]{:S(2)}) %collective-permute-start.6) | collective-permute-done | bytes 4128 | tf_op jit(solution)/shard_map/ppermute | solution.py:421
  27.2 0.1 broadcast_in_dim.37.ids_ref
  27.3 0.0 copy-done.1
  27.3 4.5 %norm_key_value_shrink.1 = (f32[128,128]{1,0:T(8,128)S(1)}, f32[4,16,2048]{2,1,0:T(8,128)S(1)}, f32[4,16,2048]{2,1,0:T(8,128)}, f32[8,80,128]{2,1,0:T(8,128)}) custom-call(s32[1,11]{1,0:T(1,128)S(1)} %constant_dynamic-slice_fusion.1.scalar_ref.first_ref, f32[8,128]{1,0:T(8,128)S(1)} %add.38.here_ref, f32[8,128]{1,0:T(8,128)S(1)} %collective-permute-done.6.there_ref, ...), custom_call_target="tpu_custom_call" | custom-call | flops 700000000 | bytes 6000000 | tf_op jit(solution)/shard_map/norm_key_value_shrink/pallas_call | solution.py:134
  31.8 0.1 collective-permute-start.14
  31.9 3.7 %all-to-all-start = ((f32[8,80,128]{2,1,0:T(8,128)}), f32[8,80,128]{2,1,0:T(8,128)S(1)}, u32[]{:S(2)}, u32[]{:S(2)}) async-start(f32[8,80,128]{2,1,0:T(8,128)} %get-tuple-element.23), calls=%async_computation | async-start | bytes 655360 | tf_op jit(solution)/shard_map/all_to_all | solution.py:387
  35.5 0.0 collective-permute-done.1.refs_3_
  35.6 2.1 %collective-permute-start.8 = (bf16[128,1024]{1,0:T(8,128)(2,1)}, bf16[128,1024]{1,0:T(8,128)(2,1)S(1)}, u32[]{:S(2)}, u32[]{:S(2)}) collective-permute-start(bf16[128,1024]{1,0:T(8,128)(2,1)} %collective-permute-done.1.refs_3_), channel_id=1, source_target_pairs={{0,4},{4,8},{8,12},{12,14},{14,10},{10,6},{6,2},{2,0},{1,5},{5,9},... | collective-permute-start | bytes 786440 | tf_op jit(solution)/shard_map/ppermute | solution.py:461
  37.6 0.1 collective-permute-start.9
  37.7 5.7 %query_products.2.refs_4_ = f32[128,1024]{1,0:T(8,128)S(1)} custom-call(s32[1,11]{1,0:T(1,128)S(1)} %constant_dynamic-slice_fusion.1.scalar_ref.first_ref, bf16[128,1024]{1,0:T(8,128)(2,1)S(1)} %bitcast.56, bf16[128,1024]{1,0:T(8,128)(2,1)S(1)} %collective-permute-done.refs_1_, bf16[128,1024]{1,0:T(8,128)(2,1)} %collective-permute-done.2.refs_2_, ...), custom_call_target="tpu_custom_call" | custom-call | flops 500000000 | bytes 5000000 | tf_op jit(solution)/shard_map/query_products/pallas_call | solution.py:185
  43.4 12.1 %collective-permute-done.8.refs_0_ = bf16[128,1024]{1,0:T(8,128)(2,1)S(1)} collective-permute-done((bf16[128,1024]{1,0:T(8,128)(2,1)}, bf16[128,1024]{1,0:T(8,128)(2,1)S(1)}, u32[]{:S(2)}, u32[]{:S(2)}) %collective-permute-start.8) | collective-permute-done | bytes 262176 | tf_op jit(solution)/shard_map/ppermute | solution.py:461
  55.5 0.7 slice.32
  56.2 0.7 slice.33
  56.9 3.2 %query_products.3.acc_ref = f32[128,1024]{1,0:T(8,128)S(1)} custom-call(s32[1,11]{1,0:T(1,128)S(1)} %constant_dynamic-slice_fusion.1.scalar_ref.first_ref, bf16[128,1024]{1,0:T(8,128)(2,1)S(1)} %collective-permute-done.8.refs_0_, bf16[128,1024]{1,0:T(8,128)(2,1)S(1)} %collective-permute-done.9.refs_1_, f32[8,1,1024]{2,1,0:T(1,128)S(1)} %bitcast.61, ...), custom_call_target="tpu_custom_call" | custom-call | flops 500000000 | bytes 5000000 | tf_op jit(solution)/shard_map/query_products/pallas_call | solution.py:185
  60.1 0.1 collective-permute-start.10
  60.2 2.0 %collective-permute-start.11 = (bf16[64,1024]{1,0:T(8,128)(2,1)}, bf16[64,1024]{1,0:T(8,128)(2,1)S(1)}, u32[]{:S(2)}, u32[]{:S(2)}) collective-permute-start(bf16[64,1024]{1,0:T(8,128)(2,1)} %slice.33), channel_id=1, source_target_pairs={{4,0},{8,4},{12,8},{14,12},{10,14},{6,10},{2,6},{0,2},{5,1},{9,5},... | collective-permute-start | bytes 393224 | tf_op jit(solution)/shard_map/ppermute | solution.py:459
  62.2 0.3 fusion.26
  62.5 0.0 copy-start.9
  62.5 0.1 pad_maximum_fusion
  62.6 1.8 %pair_sums.1 = (f32[16,2048]{1,0:T(8,128)S(1)}, f32[16,2048]{1,0:T(8,128)}, f32[16,2048]{1,0:T(8,128)S(1)}, f32[16,2048]{1,0:T(8,128)S(1)}) custom-call(s32[1,11]{1,0:T(1,128)S(1)} %constant_dynamic-slice_fusion.1.scalar_ref.first_ref, f32[4,16,2048]{2,1,0:T(8,128)S(1)} %copy-done.6, f32[4,16,2048]{2,1,0:T(8,128)} %collective-permute-done.14.got_ref), custom_call_target="tpu_custom_call" | custom-call | flops 100000 | bytes 1500000 | tf_op jit(solution)/shard_map/pair_sums/pallas_call | solution.py:301
  64.4 0.1 collective-permute-start.15
  64.5 0.8 collective-permute-start.16
  65.3 0.0 collective-permute-done.13.kv_other_ref
  65.3 3.5 %collective-permute-start.17 = (f32[16,2048]{1,0:T(8,128)S(1)}, f32[16,2048]{1,0:T(8,128)S(1)}, u32[]{:S(2)}, u32[]{:S(2)}) collective-permute-start(f32[16,2048]{1,0:T(8,128)S(1)} %get-tuple-element.30), channel_id=1, source_target_pairs={{0,12},{2,14},{4,8},{6,10},{8,4},{10,6},{12,0},{14,2},{1,13},{3,15... | collective-permute-start | bytes 393224 | tf_op jit(solution)/shard_map/ppermute | solution.py:439
  68.8 0.0 all-to-all-done.parts_ref
  68.8 0.1 broadcast_in_dim.38.own_ids_ref
  68.9 1.7 %adapter_terms.1 = (f32[128,1024]{1,0:T(8,128)S(1)}, f32[16,2048]{1,0:T(8,128)S(1)}) custom-call(s32[1,11]{1,0:T(1,128)S(1)} %constant_dynamic-slice_fusion.1.scalar_ref.first_ref, f32[8,80,128]{2,1,0:T(8,128)S(1)} %all-to-all-done.parts_ref, s32[128,128]{1,0:T(8,128)S(1)} %broadcast_in_dim.37.ids_ref, s32[16,128]{1,0:T(8,128)S(1)} %broadcast_in_dim.38.own_ids_ref, ...), custom_call_target="tpu_custom_call" | custom-call | flops 100000000 | bytes 2000000 | tf_op jit(solution)/shard_map/adapter_terms/pallas_call | solution.py:233
  70.5 0.0 collective-permute-done.10.top_ref
  70.5 0.0 collective-permute-done.11.bottom_ref
  70.5 0.0 copy-start.13
  70.5 3.2 %query_finish.1 = bf16[128,1024]{1,0:T(8,128)(2,1)} custom-call(s32[1,11]{1,0:T(1,128)S(1)} %constant_dynamic-slice_fusion.1.scalar_ref.first_ref, bf16[64,1024]{1,0:T(8,128)(2,1)S(1)} %collective-permute-done.10.top_ref, bf16[64,1024]{1,0:T(8,128)(2,1)S(1)} %collective-permute-done.11.bottom_ref, f32[8,1,1024]{2,1,0:T(1,128)S(1)} %bitcast.62, ...), custom_call_target="tpu_custom_call" | custom-call | flops 270000000 | bytes 3000000 | tf_op jit(solution)/shard_map/query_finish/pallas_call | solution.py:279
  73.8 3.6 %all-to-all-start.1 = ((bf16[8,16,1024]{2,1,0:T(8,128)(2,1)}), bf16[8,16,1024]{2,1,0:T(8,128)(2,1)S(1)}, u32[]{:S(2)}, u32[]{:S(2)}) async-start(bf16[8,16,1024]{2,1,0:T(8,128)(2,1)} %bitcast.7), calls=%async_computation.1 | async-start | bytes 524288 | tf_op jit(solution)/shard_map/all_to_all | solution.py:387
  77.4 0.1 iota_compare_fusion
  77.5 4.6 %copy.21 = bf16[192,8,8,128]{3,2,1,0:T(8,128)(2,1)} copy(bf16[192,8,8,128]{3,1,2,0:T(8,128)(2,1)} %bitcast.65) | data formatting | bytes 6291456
  82.1 2.5 %copy.22 = bf16[192,8,8,128]{3,2,1,0:T(8,128)(2,1)} copy(bf16[192,8,8,128]{3,1,2,0:T(8,128)(2,1)S(1)} %bitcast.64) | data formatting | bytes 6291456
  84.5 0.1 fusion.27
  84.6 0.1 new_key_value.1
  84.7 0.7 reshape.87
  85.4 0.6 copy.23
  86.1 0.0 all-to-all-done.1
  86.1 0.3 fusion.17
  86.4 3.7 %fusion.32 = (f32[16,8,8]{2,1,0:T(8,128)S(1)}, f32[16,8,8,96]{3,2,1,0:T(8,128)S(1)}) fusion(bf16[16,96,8,128]{3,2,1,0:T(8,128)(2,1)} %bitcast.63, pred[16,96]{1,0:T(8,128)(4,1)S(1)} %iota_compare_fusion, bf16[8,16,8,128]{3,2,1,0:T(8,128)(2,1)S(1)} %bitcast.69), kind=kOutput, calls=%fused_computation.43 | convolution fusion | flops 25459712 | bytes 3806720 | tf_op jit(solution)/shard_map/rkgd,rpkd->rkgp/dot_general | solution.py:350
  90.1 0.4 fusion.16
  90.6 1.0 %fusion.13 = bf16[16,8,8,128]{3,2,1,0:T(8,128)(2,1)S(1)} fusion(bf16[16,96,8,128]{3,2,1,0:T(8,128)(2,1)S(1)} %bitcast.67, f32[16,8,8,96]{3,2,1,0:T(8,128)S(1)} %get-tuple-element.42, f32[16,8,128]{2,1,0:T(8,128)S(1)} %bitcast.73, f32[16,8,8]{2,1,0:T(8,128)S(1)} %get-tuple-element.35, f32[16,8,8]{2,1,0:T(8,128)S(1)} %get-tuple-element.34, ...), kind=kOutput, calls=%fused_computation.7 | convolution fusion | flops 25853952 | bytes 3878912 | tf_op jit(solution)/shard_map/rkgp,rpkd->rkgd/dot_general | solution.py:360
  91.6 0.8 convert_element_type.51
  (44 shorter events, 0.2 us)
Async XLA Ops:
  1.4 1.0 %copy-start = (bf16[1,128,1024]{2,1,0:T(8,128)(2,1)S(1)}, bf16[1,128,1024]{2,1,0:T(8,128)(2,1)}, u32[]{:S(2)}) copy-start(bf16[1,128,1024]{2,1,0:T(8,128)(2,1)} %param.11) | copy-start | bytes 786436
  2.5 12.4 %collective-permute-start.4 = (f32[8,128]{1,0:T(8,128)S(1)}, f32[8,128]{1,0:T(8,128)S(1)}, u32[]{:S(2)}, u32[]{:S(2)}) collective-permute-start(f32[8,128]{1,0:T(8,128)S(1)} %square_sums.1), channel_id=1, source_target_pairs={{0,2},{2,0},{4,6},{6,4},{8,10},{10,8},{12,14},{14,12},{1,3},{3,1},... | collective-permute-start | bytes 12296 | tf_op jit(solution)/shard_map/ppermute | solution.py:421
  5.6 10.9 %collective-permute-start = (bf16[128,1024]{1,0:T(8,128)(2,1)S(1)}, bf16[128,1024]{1,0:T(8,128)(2,1)S(1)}, u32[]{:S(2)}, u32[]{:S(2)}) collective-permute-start(bf16[128,1024]{1,0:T(8,128)(2,1)S(1)} %bitcast.53), channel_id=1, source_target_pairs={{0,4},{4,8},{8,12},{12,14},{14,10},{10,6},{6,2},{2,0},{1,5},{5,9},... | collective-permute-start | bytes 786440 | tf_op jit(solution)/shard_map/ppermute | solution.py:418
  7.2 9.8 %collective-permute-start.2 = (bf16[128,1024]{1,0:T(8,128)(2,1)S(1)}, bf16[128,1024]{1,0:T(8,128)(2,1)}, u32[]{:S(2)}, u32[]{:S(2)}) collective-permute-start(bf16[128,1024]{1,0:T(8,128)(2,1)S(1)} %bitcast.54), channel_id=1, source_target_pairs={{4,0},{8,4},{12,8},{14,12},{10,14},{6,10},{2,6},{0,2},{5,1},{9,5},... | collective-permute-start | bytes 786440 | tf_op jit(solution)/shard_map/ppermute | solution.py:419
  7.6 19.6 %collective-permute-start.7 = (bf16[2,192,1024]{2,1,0:T(8,128)(2,1)}, bf16[2,192,1024]{2,1,0:T(8,128)(2,1)S(1)}, u32[]{:S(2)}, u32[]{:S(2)}) collective-permute-start(bf16[2,192,1024]{2,1,0:T(8,128)(2,1)} %bitcast.57), channel_id=1, source_target_pairs={{0,1},{1,0},{2,3},{3,2},{4,5},{5,4},{6,7},{7,6},{8,9},{9,8},{10,11... | collective-permute-start | bytes 2359304 | tf_op jit(solution)/shard_map/ppermute | solution.py:430
  7.6 57.6 %collective-permute-start.13 = (bf16[2,2,64,1024]{3,2,1,0:T(8,128)(2,1)}, bf16[2,2,64,1024]{3,2,1,0:T(8,128)(2,1)S(1)}, u32[]{:S(2)}, u32[]{:S(2)}) collective-permute-start(bf16[2,2,64,1024]{3,2,1,0:T(8,128)(2,1)} %kv_own_ref.1), channel_id=1, source_target_pairs={{0,1},{1,0},{2,3},{3,2},{4,5},{5,4},{6,7},{7,6},{8,9},{9,8},{10,11... | collective-permute-start | bytes 1572872 | tf_op jit(solution)/shard_map/ppermute | solution.py:430
  8.1 10.4 %copy-start.12 = (s32[1,128]{1,0:T(1,128)S(1)}, s32[1,128]{1,0:T(1,128)}, u32[]{:S(2)}) copy-start(s32[1,128]{1,0:T(1,128)} %param.18) | copy-start | bytes 1540
  8.1 19.1 %copy-start.1 = (bf16[1,128,1024]{2,1,0:T(8,128)(2,1)S(1)}, bf16[1,128,1024]{2,1,0:T(8,128)(2,1)}, u32[]{:S(2)}) copy-start(bf16[1,128,1024]{2,1,0:T(8,128)(2,1)} %param.11) | copy-start | bytes 786436
  8.1 19.1 %copy-start.2 = (bf16[2,1024,192]{1,2,0:T(8,128)(2,1)S(1)}, bf16[2,1024,192]{1,2,0:T(8,128)(2,1)}, u32[]{:S(2)}) copy-start(bf16[2,1024,192]{1,2,0:T(8,128)(2,1)} %param.15) | copy-start | bytes 2359300
  8.1 19.1 %copy-start.3 = (f32[8192]{0:T(1024)S(1)}, f32[8192]{0:T(1024)}, u32[]{:S(2)}) copy-start(f32[8192]{0:T(1024)} %param.12) | copy-start | bytes 98308
  14.9 3.8 %collective-permute-start.5 = (f32[8,128]{1,0:T(8,128)S(1)}, f32[8,128]{1,0:T(8,128)S(1)}, u32[]{:S(2)}, u32[]{:S(2)}) collective-permute-start(f32[8,128]{1,0:T(8,128)S(1)} %add.37), channel_id=1, source_target_pairs={{0,4},{2,6},{4,0},{6,2},{8,12},{10,14},{12,8},{14,10},{1,5},{3,7},... | collective-permute-start | bytes 12296 | tf_op jit(solution)/shard_map/ppermute | solution.py:421
  16.5 19.0 %collective-permute-start.1 = (bf16[128,1024]{1,0:T(8,128)(2,1)S(1)}, bf16[128,1024]{1,0:T(8,128)(2,1)}, u32[]{:S(2)}, u32[]{:S(2)}) collective-permute-start(bf16[128,1024]{1,0:T(8,128)(2,1)S(1)} %collective-permute-done.refs_1_), channel_id=1, source_target_pairs={{0,4},{4,8},{8,12},{12,14},{14,10},{10,6},{6,2},{2,0},{1,5},{5,9},... | collective-permute-start | bytes 786440 | tf_op jit(solution)/shard_map/ppermute | solution.py:461
  17.0 18.6 %collective-permute-start.3 = (bf16[128,1024]{1,0:T(8,128)(2,1)}, bf16[128,1024]{1,0:T(8,128)(2,1)}, u32[]{:S(2)}, u32[]{:S(2)}) collective-permute-start(bf16[128,1024]{1,0:T(8,128)(2,1)} %collective-permute-done.2.refs_2_), channel_id=1, source_target_pairs={{4,0},{8,4},{12,8},{14,12},{10,14},{6,10},{2,6},{0,2},{5,1},{9,5},... | collective-permute-start | bytes 786440 | tf_op jit(solution)/shard_map/ppermute | solution.py:462
  18.7 8.5 %collective-permute-start.6 = (f32[8,128]{1,0:T(8,128)S(1)}, f32[8,128]{1,0:T(8,128)S(1)}, u32[]{:S(2)}, u32[]{:S(2)}) collective-permute-start(f32[8,128]{1,0:T(8,128)S(1)} %add.38.here_ref), channel_id=1, source_target_pairs={{0,8},{2,10},{4,12},{6,14},{8,0},{10,2},{12,4},{14,6},{1,9},{3,11}... | collective-permute-start | bytes 12296 | tf_op jit(solution)/shard_map/ppermute | solution.py:421
  27.2 37.3 %collective-permute-start.12 = (bf16[2,64,1024]{2,1,0:T(8,128)(2,1)}, bf16[2,64,1024]{2,1,0:T(8,128)(2,1)}, u32[]{:S(2)}, u32[]{:S(2)}) collective-permute-start(bf16[2,64,1024]{2,1,0:T(8,128)(2,1)} %up_own_ref.1), channel_id=1, source_target_pairs={{0,1},{1,0},{2,3},{3,2},{4,5},{5,4},{6,7},{7,6},{8,9},{9,8},{10,11... | collective-permute-start | bytes 786440 | tf_op jit(solution)/shard_map/ppermute | solution.py:430
  31.8 11.6 %copy-start.5 = (f32[4,16,2048]{2,1,0:T(8,128)}, f32[4,16,2048]{2,1,0:T(8,128)S(1)}, u32[]{:S(2)}) copy-start(f32[4,16,2048]{2,1,0:T(8,128)S(1)} %get-tuple-element.25.keep_ref) | copy-start | bytes 1572868
  31.8 30.8 %collective-permute-start.14 = (f32[4,16,2048]{2,1,0:T(8,128)}, f32[4,16,2048]{2,1,0:T(8,128)}, u32[]{:S(2)}, u32[]{:S(2)}) collective-permute-start(f32[4,16,2048]{2,1,0:T(8,128)} %get-tuple-element.26), channel_id=1, source_target_pairs={{0,2},{2,0},{4,6},{6,4},{8,10},{10,8},{12,14},{14,12},{1,3},{3,1},... | collective-permute-start | bytes 1572872 | tf_op jit(solution)/shard_map/ppermute | solution.py:436
  31.9 36.9 %all-to-all-start = ((f32[8,80,128]{2,1,0:T(8,128)}), f32[8,80,128]{2,1,0:T(8,128)S(1)}, u32[]{:S(2)}, u32[]{:S(2)}) async-start(f32[8,80,128]{2,1,0:T(8,128)} %get-tuple-element.23), calls=%async_computation | async-start | bytes 655360 | tf_op jit(solution)/shard_map/all_to_all | solution.py:387
  35.6 20.0 %collective-permute-start.8 = (bf16[128,1024]{1,0:T(8,128)(2,1)}, bf16[128,1024]{1,0:T(8,128)(2,1)S(1)}, u32[]{:S(2)}, u32[]{:S(2)}) collective-permute-start(bf16[128,1024]{1,0:T(8,128)(2,1)} %collective-permute-done.1.refs_3_), channel_id=1, source_target_pairs={{0,4},{4,8},{8,12},{12,14},{14,10},{10,6},{6,2},{2,0},{1,5},{5,9},... | collective-permute-start | bytes 786440 | tf_op jit(solution)/shard_map/ppermute | solution.py:461
  37.6 18.6 %collective-permute-start.9 = (bf16[128,1024]{1,0:T(8,128)(2,1)}, bf16[128,1024]{1,0:T(8,128)(2,1)S(1)}, u32[]{:S(2)}, u32[]{:S(2)}) collective-permute-start(bf16[128,1024]{1,0:T(8,128)(2,1)} %collective-permute-done.3.refs_4_), channel_id=1, source_target_pairs={{4,0},{8,4},{12,8},{14,12},{10,14},{6,10},{2,6},{0,2},{5,1},{9,5},... | collective-permute-start | bytes 786440 | tf_op jit(solution)/shard_map/ppermute | solution.py:462
  56.8 5.8 %copy-start.6 = (f32[4,16,2048]{2,1,0:T(8,128)S(1)}, f32[4,16,2048]{2,1,0:T(8,128)}, u32[]{:S(2)}) copy-start(f32[4,16,2048]{2,1,0:T(8,128)} %copy-done.5) | copy-start | bytes 1572868
  56.9 12.0 %copy-start.4 = (bf16[2,2,64,1024]{3,2,1,0:T(8,128)(2,1)S(1)}, bf16[2,2,64,1024]{3,2,1,0:T(8,128)(2,1)}, u32[]{:S(2)}) copy-start(bf16[2,2,64,1024]{3,2,1,0:T(8,128)(2,1)} %kv_own_ref.1) | copy-start | bytes 1572868
  60.1 10.4 %collective-permute-start.10 = (bf16[64,1024]{1,0:T(8,128)(2,1)}, bf16[64,1024]{1,0:T(8,128)(2,1)S(1)}, u32[]{:S(2)}, u32[]{:S(2)}) collective-permute-start(bf16[64,1024]{1,0:T(8,128)(2,1)} %slice.32), channel_id=1, source_target_pairs={{0,4},{4,8},{8,12},{12,14},{14,10},{10,6},{6,2},{2,0},{1,5},{5,9},... | collective-permute-start | bytes 393224 | tf_op jit(solution)/shard_map/ppermute | solution.py:458
  60.2 10.4 %collective-permute-start.11 = (bf16[64,1024]{1,0:T(8,128)(2,1)}, bf16[64,1024]{1,0:T(8,128)(2,1)S(1)}, u32[]{:S(2)}, u32[]{:S(2)}) collective-permute-start(bf16[64,1024]{1,0:T(8,128)(2,1)} %slice.33), channel_id=1, source_target_pairs={{4,0},{8,4},{12,8},{14,12},{10,14},{6,10},{2,6},{0,2},{5,1},{9,5},... | collective-permute-start | bytes 393224 | tf_op jit(solution)/shard_map/ppermute | solution.py:459
  62.5 6.3 %copy-start.9 = (f32[128,64]{1,0:T(8,128)}, f32[128,64]{1,0:T(8,128)S(1)}, u32[]{:S(2)}) copy-start(f32[128,64]{1,0:T(8,128)S(1)} %get-tuple-element.40) | copy-start | bytes 98308
  64.4 20.2 %collective-permute-start.15 = (f32[16,2048]{1,0:T(8,128)}, f32[16,2048]{1,0:T(8,128)S(1)}, u32[]{:S(2)}, u32[]{:S(2)}) collective-permute-start(f32[16,2048]{1,0:T(8,128)} %get-tuple-element.28), channel_id=1, source_target_pairs={{0,4},{2,6},{4,0},{6,2},{8,12},{10,14},{12,8},{14,10},{1,5},{3,7},... | collective-permute-start | bytes 393224 | tf_op jit(solution)/shard_map/ppermute | solution.py:439
  64.5 20.1 %collective-permute-start.16 = (f32[16,2048]{1,0:T(8,128)S(1)}, f32[16,2048]{1,0:T(8,128)S(1)}, u32[]{:S(2)}, u32[]{:S(2)}) collective-permute-start(f32[16,2048]{1,0:T(8,128)S(1)} %get-tuple-element.29), channel_id=1, source_target_pairs={{0,8},{2,10},{4,12},{6,14},{8,0},{10,2},{12,4},{14,6},{1,9},{3,11}... | collective-permute-start | bytes 393224 | tf_op jit(solution)/shard_map/ppermute | solution.py:439
  65.3 19.3 %collective-permute-start.17 = (f32[16,2048]{1,0:T(8,128)S(1)}, f32[16,2048]{1,0:T(8,128)S(1)}, u32[]{:S(2)}, u32[]{:S(2)}) collective-permute-start(f32[16,2048]{1,0:T(8,128)S(1)} %get-tuple-element.30), channel_id=1, source_target_pairs={{0,12},{2,14},{4,8},{6,10},{8,4},{10,6},{12,0},{14,2},{1,13},{3,15... | collective-permute-start | bytes 393224 | tf_op jit(solution)/shard_map/ppermute | solution.py:439
  70.5 6.9 %copy-start.13 = (s32[1,16]{1,0:T(1,128)S(1)}, s32[1,16]{1,0:T(1,128)}, u32[]{:S(2)}) copy-start(s32[1,16]{1,0:T(1,128)} %param.20) | copy-start | bytes 196
  73.8 12.3 %all-to-all-start.1 = ((bf16[8,16,1024]{2,1,0:T(8,128)(2,1)}), bf16[8,16,1024]{2,1,0:T(8,128)(2,1)S(1)}, u32[]{:S(2)}, u32[]{:S(2)}) async-start(bf16[8,16,1024]{2,1,0:T(8,128)(2,1)} %bitcast.7), calls=%async_computation.1 | async-start | bytes 524288 | tf_op jit(solution)/shard_map/all_to_all | solution.py:387
  77.5 4.6 %copy-start.7 = (bf16[16,1,96,1024]{3,2,1,0:T(8,128)(2,1)S(1)}, bf16[16,1,96,1024]{3,2,1,0:T(8,128)(2,1)}, u32[]{:S(2)}) copy-start(bf16[16,1,96,1024]{3,2,1,0:T(8,128)(2,1)} %get-tuple-element.33) | copy-start | bytes 9437188
  82.1 2.5 %copy-start.10 = (f32[128,64]{1,0:T(8,128)S(1)}, f32[128,64]{1,0:T(8,128)}, u32[]{:S(2)}) copy-start(f32[128,64]{1,0:T(8,128)} %copy-done.9) | copy-start | bytes 98308
  85.4 5.2 %copy-start.8 = (bf16[192,8,8,128]{3,2,1,0:T(8,128)(2,1)S(1)}, bf16[192,8,8,128]{3,2,1,0:T(8,128)(2,1)}, u32[]{:S(2)}) copy-start(bf16[192,8,8,128]{3,2,1,0:T(8,128)(2,1)} %copy.22) | copy-start | bytes 9437188
  86.1 4.5 %copy-start.11 = (f32[2,8,8,128]{3,2,1,0:T(8,128)S(1)}, f32[2,8,8,128]{3,2,1,0:T(8,128)}, u32[]{:S(2)}) copy-start(f32[2,8,8,128]{3,2,1,0:T(8,128)} %copy.23) | copy-start | bytes 196612

commit v2 on v1

v2 whole, which is shorter than its diff:
```python
import functools
import math

import jax
import jax.numpy as jnp
import numpy as np
from jax import lax
from jax.experimental import pallas as pl
from jax.experimental.pallas import tpu as pltpu
from jax.sharding import PartitionSpec as P

HEAD_WIDTH = 128
LANES = 128
EPS = 1e-05
THETA = 500000.0
UNROLL = 4
NARROW = jnp.float16
SLOTS = 4
F32 = jnp.float32
BF16 = jnp.bfloat16


def ring_order(size):
    if size == 8:
        return [0, 2, 4, 6, 7, 5, 3, 1]
    return list(range(size))


def dot(a, b):
    return jnp.dot(a, b, preferred_element_type=F32)


def params(mib=16):
    return pltpu.CompilerParams(vmem_limit_bytes=mib * 1024 * 1024)


def after(value, *others):
    return lax.optimization_barrier((value, *others))[0]


VMEM = pl.BlockSpec(memory_space=pltpu.VMEM)
SMEM = pl.BlockSpec(memory_space=pltpu.SMEM)
HBM = pl.BlockSpec(memory_space=pltpu.HBM)


def in_hbm(value):
    return pltpu.with_memory_space_constraint(value, pltpu.HBM)


def rotary_tables(positions):
    half = HEAD_WIDTH // 2
    frequency = THETA ** (-(jnp.arange(half).astype(F32) * 2.0 / HEAD_WIDTH))
    angles = positions.astype(F32)[:, None] * frequency[None, :]
    cosine = jnp.cos(angles)
    sine = jnp.sin(angles)
    return jnp.concatenate([cosine, cosine], axis=1), jnp.concatenate([-sine, sine], axis=1)


def rotate_heads(values, cosine, sine):
    turned = []
    for head in range(values.shape[1] // HEAD_WIDTH):
        part = values[:, head * HEAD_WIDTH : (head + 1) * HEAD_WIDTH]
        turned.append(part * cosine + pltpu.roll(part, HEAD_WIDTH // 2, 1) * sine)
    return jnp.concatenate(turned, axis=1)


def pack_rows(values):
    most = jnp.max(jnp.abs(values), axis=1, keepdims=True)
    exponent = jnp.ceil(jnp.log2(jnp.maximum(most, 1e-30)))
    scaled = values * jnp.exp2(14.0 - exponent)
    return jnp.concatenate([scaled, jnp.broadcast_to(exponent, (values.shape[0], LANES))], axis=1)


def unpack_rows(values):
    width = values.shape[1] - LANES
    return values[:, :width] * jnp.exp2(values[:, width : width + 1] - 14.0)


def lane_sums(block):
    wide = block.astype(F32)
    squares = wide * wide
    lanes = squares[:, :LANES]
    for at in range(LANES, squares.shape[1], LANES):
        lanes = lanes + squares[:, at : at + LANES]
    return lanes


def sums_kernel(first, *refs):
    out_ref = refs[-1]
    half = out_ref.shape[0] // 2
    tops = refs[0:-1:2] if first else refs[0:-2:2]
    bottoms = refs[1:-1:2] if first else refs[1:-2:2]
    top = None if first else refs[-2][:half]
    bottom = None if first else refs[-2][half:]
    for top_ref, bottom_ref in zip(tops, bottoms):
        more, below = lane_sums(top_ref[...]), lane_sums(bottom_ref[...])
        top = more if top is None else top + more
        bottom = below if bottom is None else bottom + below
    out_ref[:half] = top
    out_ref[half:] = bottom


def square_sums(blocks, before):
    flat = [half for block in blocks for half in block]
    rows = 2 * flat[0].shape[0]
    operands = flat + ([] if before is None else [before])
    return pl.pallas_call(
        functools.partial(sums_kernel, before is None),
        in_specs=[VMEM] * len(operands),
        out_specs=VMEM,
        out_shape=jax.ShapeDtypeStruct((rows, LANES), F32),
        compiler_params=params(),
        cost_estimate=pl.CostEstimate(flops=1000000, bytes_accessed=600000, transcendentals=0),
        name="square_sums",
    )(*operands)


def id_column(request_ref):
    rows = request_ref.shape[1]
    return jnp.broadcast_to(request_ref[...].astype(F32), (LANES, rows)).T.astype(jnp.int32)


def prep_kernel(
    rank, scalar_ref, sums_ref, last_top_ref, last_bottom_ref, top_ref, bottom_ref, request_ref, other_ref,
    gain_hbm, own_hbm, weight_hbm, inverse_ref, keep_ref, give_ref, shrink_ref,
    kv_ref, gain_ref, own_ref, weight_ref, sems,
):
    rows, width = inverse_ref.shape[0], top_ref.shape[1]
    model_width = gain_hbm.shape[0] * width
    chunks = sems.shape[0] - 2
    depth = width // chunks
    first = [
        pltpu.make_async_copy(gain_hbm.at[scalar_ref[0, 2]], gain_ref, sems.at[chunks]),
        pltpu.make_async_copy(own_hbm, own_ref, sems.at[chunks + 1]),
    ]
    copies = [
        pltpu.make_async_copy(
            weight_hbm.at[pl.ds(c * depth, depth)], weight_ref.at[pl.ds(c * depth, depth)], sems.at[c]
        )
        for c in range(chunks)
    ]
    for copy in first + copies:
        copy.start()
    last = jnp.concatenate([lane_sums(last_top_ref[...]), lane_sums(last_bottom_ref[...])], axis=0)
    total = jnp.sum((sums_ref[...] + last).T, axis=0, keepdims=True)
    inverse_row = lax.rsqrt(total / model_width + EPS)
    inverse = jnp.broadcast_to(inverse_row, (LANES, rows)).T
    inverse_ref[...] = inverse
    ids = id_column(request_ref)
    first[0].wait()
    block = jnp.concatenate([top_ref[...], bottom_ref[...]], axis=0).astype(F32)
    normed = (block * inverse[:, :1] * gain_ref[...]).astype(BF16)
    first[1].wait()
    shrink = jnp.zeros((rows, 3 * rank), F32)
    for side, panel_ref in enumerate((own_ref, other_ref)):
        for j in range(panel_ref.shape[0]):
            part = lax.dot_general(normed, panel_ref[j], (((1,), (1,)), ((), ())), preferred_element_type=F32)
            shrink = shrink + jnp.where(ids[:, :1] == scalar_ref[0, side] + j, part, 0.0)
    half = rows // 2
    packed = jnp.concatenate([shrink[:half, :rank], shrink[half:, :rank]], axis=1)
    tensor, page, _ = shrink_ref.shape
    own_rows = page - half
    for peer in range(tensor):
        shrink_ref[peer, :half] = packed
        shrink_ref[peer, half:] = shrink[peer * own_rows : (peer + 1) * own_rows, rank:]
    total = None
    for c, copy in enumerate(copies):
        copy.wait()
        part = dot(normed[:, c * depth : (c + 1) * depth], weight_ref[c * depth : (c + 1) * depth])
        total = part if total is None else total + part
    kv_ref[...] = total
    parity = scalar_ref[0, 2] % 2
    for pair in range(tensor // 2):
        keep_ref[pair] = kv_ref[pl.ds(pl.multiple_of((2 * pair + parity) * own_rows, own_rows), own_rows)]
        give_ref[pair] = pack_rows(
            kv_ref[pl.ds(pl.multiple_of((2 * pair + 1 - parity) * own_rows, own_rows), own_rows)]
        )


def prep(scalars, sums, last, local, request, gains, weight, own, other, rank, tensor):
    half, width = local[0].shape
    rows = 2 * half
    columns = weight.shape[1]
    chunks = 4 if width % 1024 == 0 else 1
    page = rows // 2 + rows // tensor
    return pl.pallas_call(
        functools.partial(prep_kernel, rank),
        in_specs=[SMEM] + [VMEM] * 7 + [HBM] * 3,
        out_specs=[VMEM] * 4,
        out_shape=[
            jax.ShapeDtypeStruct((rows, LANES), F32),
            pltpu.HBM((tensor // 2, rows // tensor, columns), F32),
            jax.ShapeDtypeStruct((tensor // 2, rows // tensor, columns + LANES), F32),
            pltpu.HBM((tensor, page, LANES), F32),
        ],
        scratch_shapes=[
            pltpu.VMEM((rows, columns), F32),
            pltpu.VMEM((1, width), F32),
            pltpu.VMEM(own.shape, BF16),
            pltpu.VMEM(weight.shape, BF16),
            pltpu.SemaphoreType.DMA((chunks + 2,)),
        ],
        compiler_params=params(),
        cost_estimate=pl.CostEstimate(flops=700000000, bytes_accessed=6000000, transcendentals=0),
        name="norm_key_value_shrink",
    )(scalars, sums, *last, *local, in_hbm(request), other, in_hbm(gains), in_hbm(own), in_hbm(weight))


def query_kernel(count, columns_at, scalar_ref, *refs):
    blocks = refs[: 2 * count]
    inverse_ref, gain_hbm, weight_hbm, out_ref, gain_ref, weight_ref, sems = refs[2 * count :]
    width = blocks[0].shape[1]
    slots = weight_ref.shape[0]
    owners = [scalar_ref[0, columns_at + i] for i in range(count)]
    gain_copy = pltpu.make_async_copy(gain_hbm, gain_ref, sems.at[slots])

    def fetch(i):
        return pltpu.make_async_copy(
            weight_hbm.at[pl.ds(pl.multiple_of(owners[i] * width, width), width)],
            weight_ref.at[i % slots],
            sems.at[i % slots],
        )

    gain_copy.start()
    for i in range(min(slots, count)):
        fetch(i).start()
    gain_copy.wait()
    inverse = inverse_ref[:, :1]
    for i in range(count):
        gain = gain_ref[pl.ds(owners[i], 1)].reshape(1, width)
        block = jnp.concatenate([blocks[2 * i][...], blocks[2 * i + 1][...]], axis=0).astype(F32)
        normed = (block * inverse * gain).astype(BF16)
        fetch(i).wait()
        part = dot(normed, weight_ref[i % slots])
        out_ref[...] = part if i == 0 else out_ref[...] + part
        if i + slots < count:
            fetch(i + slots).start()


def query_products(scalars, columns_at, blocks, gains, weight, inverse):
    width = blocks[0][0].shape[1]
    columns = weight.shape[1]
    count = len(blocks)
    flat = [half for block in blocks for half in block]
    slots = min(SLOTS, count)
    return pl.pallas_call(
        functools.partial(query_kernel, count, columns_at),
        in_specs=[SMEM] + [VMEM] * (2 * count + 1) + [HBM] * 2,
        out_specs=VMEM,
        out_shape=jax.ShapeDtypeStruct((inverse.shape[0], columns), F32),
        scratch_shapes=[
            pltpu.VMEM(gains.shape, F32),
            pltpu.VMEM((slots, width, columns), BF16),
            pltpu.SemaphoreType.DMA((slots + 1,)),
        ],
        compiler_params=params(16),
        cost_estimate=pl.CostEstimate(flops=2000000000, bytes_accessed=17000000, transcendentals=0),
        name="query_products",
    )(scalars, *flat, inverse, in_hbm(gains), in_hbm(weight))


def finish_kernel(
    rank, first_ref, parts_ref, request_ref, acc_ref, up_own_hbm, up_other_hbm, kv_own_hbm, kv_other_hbm,
    out_ref, kv_delta_ref, up_own_ref, up_other_ref, kv_own_ref, kv_other_ref, column_ref, sems,
):
    rows = request_ref.shape[1]
    half = rows // 2
    kv_width = kv_delta_ref.shape[1] // 2
    sources = (up_own_hbm, up_other_hbm, kv_own_hbm, kv_other_hbm)
    targets = (up_own_ref, up_other_ref, kv_own_ref, kv_other_ref)
    copies = [pltpu.make_async_copy(sources[i], targets[i], sems.at[i]) for i in range(4)]
    for copy in copies:
        copy.start()
    ids_ref = id_column(request_ref)
    total = parts_ref[0]
    for peer in range(1, parts_ref.shape[0]):
        total = total + parts_ref[peer]
    for copy in copies:
        copy.wait()
    shrink = jnp.concatenate([total[:half, :rank], total[:half, rank:]], axis=0)
    own_rows = kv_delta_ref.shape[0]
    own = total[half:]
    column_ref[...] = ids_ref
    own_ids = column_ref[pl.ds(pl.multiple_of(first_ref[0, 2] * own_rows, own_rows), own_rows)]
    delta = None
    key_delta = value_delta = None
    for side, (up_ref, kv_ref) in enumerate(((up_own_ref, kv_own_ref), (up_other_ref, kv_other_ref))):
        for j in range(up_ref.shape[0]):
            mine = ids_ref[:, :1] == first_ref[0, side] + j
            part = dot(jnp.where(mine, shrink, 0.0).astype(BF16), up_ref[j])
            delta = part if delta is None else delta + part
            kept = jnp.where(own_ids[:, :1] == first_ref[0, side] + j, own, 0.0).astype(BF16)
            key_part = dot(kept[:, :rank], kv_ref[j, 0])
            value_part = dot(kept[:, rank:], kv_ref[j, 1])
            key_delta = key_part if key_delta is None else key_delta + key_part
            value_delta = value_part if value_delta is None else value_delta + value_part
    out_ref[...] = (acc_ref[...] + delta).astype(BF16)
    kv_delta_ref[:, :kv_width] = key_delta
    kv_delta_ref[:, kv_width:] = value_delta


def finish(scalars, parts, request, ups, kv_ups, acc, rank):
    rows = request.shape[1]
    own_rows = rows // parts.shape[0]
    columns = ups[0].shape[2]
    kv_columns = 2 * kv_ups[0].shape[3]
    return pl.pallas_call(
        functools.partial(finish_kernel, rank),
        in_specs=[SMEM] + [VMEM] * 3 + [HBM] * 4,
        out_specs=[VMEM, VMEM],
        out_shape=[
            jax.ShapeDtypeStruct((rows, columns), BF16),
            jax.ShapeDtypeStruct((own_rows, kv_columns), F32),
        ],
        scratch_shapes=[
            pltpu.VMEM(ups[0].shape, BF16),
            pltpu.VMEM(ups[1].shape, BF16),
            pltpu.VMEM(kv_ups[0].shape, BF16),
            pltpu.VMEM(kv_ups[1].shape, BF16),
            pltpu.VMEM((rows, LANES), jnp.int32),
            pltpu.SemaphoreType.DMA((4,)),
        ],
        compiler_params=params(),
        cost_estimate=pl.CostEstimate(flops=100000000, bytes_accessed=2000000, transcendentals=0),
        name="adapter_terms",
    )(scalars, parts, in_hbm(request), acc, *[in_hbm(value) for value in (*ups, *kv_ups)])


def pair_kernel(scalar_ref, keep_ref, got_ref, *out_refs):
    index = lax.div(scalar_ref[0, 2], 2)
    for distance, out_ref in enumerate(out_refs):
        other = index ^ distance
        total = keep_ref[other] + unpack_rows(got_ref[other])
        out_ref[...] = total if distance == 0 else pack_rows(total)


def pair_sums(scalars, keep, got):
    count, own_rows, columns = keep.shape
    return pl.pallas_call(
        pair_kernel,
        in_specs=[SMEM, VMEM, VMEM],
        out_specs=[VMEM] * count,
        out_shape=[jax.ShapeDtypeStruct((own_rows, columns), F32)]
        + [jax.ShapeDtypeStruct((own_rows, columns + LANES), F32)] * (count - 1),
        compiler_params=params(),
        cost_estimate=pl.CostEstimate(flops=100000, bytes_accessed=1500000, transcendentals=0),
        name="pair_sums",
    )(scalars, in_hbm(keep), got)


def fresh_kernel(count, *refs):
    parts = refs[:count]
    delta_ref, cosine_ref, sine_ref, out_ref, heads_ref = refs[count:]
    total = parts[0][...]
    for part in parts[1:]:
        total = total + unpack_rows(part[...])
    total = total + delta_ref[...]
    kv_width = total.shape[1] // 2
    newest = jnp.concatenate(
        [rotate_heads(total[:, :kv_width], cosine_ref[...], sine_ref[...]), total[:, kv_width:]], axis=1
    ).astype(BF16)
    out_ref[:, 0, :] = newest[:, :kv_width]
    out_ref[:, 1, :] = newest[:, kv_width:]
    spread = newest.astype(F32)
    for head in range(heads_ref.shape[1]):
        heads_ref[:, head, :] = spread[:, head * HEAD_WIDTH : (head + 1) * HEAD_WIDTH]


def fresh(parts, delta, cosine, sine):
    own_rows, columns = delta.shape
    return pl.pallas_call(
        functools.partial(fresh_kernel, len(parts)),
        out_shape=[
            jax.ShapeDtypeStruct((own_rows, 2, columns // 2), BF16),
            jax.ShapeDtypeStruct((own_rows, columns // HEAD_WIDTH, HEAD_WIDTH), F32),
        ],
        compiler_params=params(),
        cost_estimate=pl.CostEstimate(flops=100000, bytes_accessed=1000000, transcendentals=0),
        name="new_key_value",
    )(*parts, delta, cosine, sine)


def attend_kernel(
    lengths_ref, query_ref, newest_ref, cosine_ref, sine_ref, cache_hbm, out_ref, query_heads_ref, scores_ref, weights_ref, fresh_ref,
    cache_ref, sems,
):
    tensor, own_rows, columns = query_ref.shape
    per_peer = columns // HEAD_WIDTH
    positions = cache_ref.shape[2]
    key_heads = cache_ref.shape[3] // HEAD_WIDTH
    heads = tensor * per_peer
    groups = heads // key_heads
    scale = 1.0 / math.sqrt(HEAD_WIDTH)
    pair = 2 * groups
    parts = sems.shape[1]
    step = own_rows // parts
    copies = [
        [
            pltpu.make_async_copy(
                cache_hbm.at[pl.ds(i * step, step), which], cache_ref.at[which, pl.ds(i * step, step)], sems.at[which, i]
            )
            for i in range(parts)
        ]
        for which in range(2)
    ]
    for copy in copies[0] + copies[1]:
        copy.start()
    for peer in range(tensor):
        part = rotate_heads(query_ref[peer].astype(F32), cosine_ref[...], sine_ref[...]).astype(BF16).astype(F32)
        for j in range(per_peer):
            query_heads_ref[:, peer * per_peer + j, :] = part[:, j * HEAD_WIDTH : (j + 1) * HEAD_WIDTH]
    side = lax.broadcasted_iota(jnp.int32, (pair, 2 * HEAD_WIDTH), 0) < groups
    on_side = side == (lax.broadcasted_iota(jnp.int32, (pair, 2 * HEAD_WIDTH), 1) < HEAD_WIDTH)
    lane = lax.broadcasted_iota(jnp.int32, (heads, positions), 1)

    def to_heads(part):
        return jnp.broadcast_to(part[:, None, :], (key_heads, groups, HEAD_WIDTH)).reshape(heads, HEAD_WIDTH)

    def score_step(row, carry):
        query = query_heads_ref[row]
        for k in range(0, key_heads, 2):
            two = query[k * groups : (k + 2) * groups]
            spread = jnp.where(on_side, jnp.concatenate([two, two], axis=1), 0.0).astype(BF16)
            keys = cache_ref[0, row, :, k * HEAD_WIDTH : (k + 2) * HEAD_WIDTH]
            scores_ref[row, k * groups : (k + 2) * groups] = lax.dot_general(
                spread, keys, (((1,), (1,)), ((), ())), preferred_element_type=F32
            )
        return carry

    def weight_step(row, carry):
        score = jnp.where(lane < lengths_ref[0, row], scores_ref[row] * scale, -1e30)
        new_key = to_heads(newest_ref[row, :key_heads])
        new_value = to_heads(newest_ref[row, key_heads:])
        new_score = jnp.sum(query_heads_ref[row] * new_key, axis=1, keepdims=True) * scale
        top = jnp.maximum(jnp.max(score, axis=1, keepdims=True), new_score)
        weights = jnp.exp(score - top)
        new_weight = jnp.exp(new_score - top)
        denominator = jnp.sum(weights, axis=1, keepdims=True) + new_weight
        weights_ref[row] = (weights / denominator).astype(BF16)
        fresh_ref[row] = (new_weight / denominator).astype(BF16).astype(F32) * new_value
        return carry

    def value_step(row, carry):
        for k in range(0, key_heads, 2):
            values = cache_ref[1, row, :, k * HEAD_WIDTH : (k + 2) * HEAD_WIDTH]
            both = dot(weights_ref[row, k * groups : (k + 2) * groups], values)
            query_heads_ref[row, k * groups : (k + 1) * groups] = (
                both[:groups, :HEAD_WIDTH] + fresh_ref[row, k * groups : (k + 1) * groups]
            )
            query_heads_ref[row, (k + 1) * groups : (k + 2) * groups] = (
                both[groups:, HEAD_WIDTH:] + fresh_ref[row, (k + 1) * groups : (k + 2) * groups]
            )
        return carry

    for i, copy in enumerate(copies[0]):
        copy.wait()
        lax.fori_loop(i * step, (i + 1) * step, score_step, 0, unroll=True)
    lax.fori_loop(0, own_rows, weight_step, 0, unroll=UNROLL)
    for i, copy in enumerate(copies[1]):
        copy.wait()
        lax.fori_loop(i * step, (i + 1) * step, value_step, 0, unroll=True)
    for head in range(heads):
        out_ref[:, head * HEAD_WIDTH : (head + 1) * HEAD_WIDTH] = query_heads_ref[:, head, :].astype(BF16)


def attend(query_rows, newest_heads, cosine, sine, cache, lengths):
    tensor, own_rows, columns = query_rows.shape
    heads = tensor * columns // HEAD_WIDTH
    return pl.pallas_call(
        attend_kernel,
        in_specs=[SMEM] + [VMEM] * 4 + [HBM],
        out_specs=VMEM,
        out_shape=jax.ShapeDtypeStruct((own_rows, tensor * columns), BF16),
        scratch_shapes=[
            pltpu.VMEM((own_rows, heads, HEAD_WIDTH), F32),
            pltpu.VMEM((own_rows, heads, cache.shape[2]), F32),
            pltpu.VMEM((own_rows, heads, cache.shape[2]), BF16),
            pltpu.VMEM((own_rows, heads, HEAD_WIDTH), F32),
            pltpu.VMEM((2, own_rows) + cache.shape[2:], BF16),
            pltpu.SemaphoreType.DMA((2, 4)),
        ],
        compiler_params=params(),
        cost_estimate=pl.CostEstimate(flops=400000000, bytes_accessed=7000000, transcendentals=100000),
        name="attention",
    )(lengths, query_rows, newest_heads, cosine, sine, in_hbm(cache))


def make_body(mesh):
    tensor = mesh.shape["tensor"]
    shards = mesh.shape["adapter"]
    order = ring_order(tensor)
    place_of = [order.index(t) for t in range(tensor)]
    right = [(order[i], order[(i + 1) % tensor]) for i in range(tensor)]
    left = [(b, a) for a, b in right]
    swap = [(i, shards - 1 - i) for i in range(shards)]

    def table(own_adapters):
        lines = []
        for side in range(shards):
            for position in range(tensor):
                place = place_of[position]
                steps = [0] + [sign * step for step in range(1, tensor // 2) for sign in (-1, 1)] + [tensor // 2]
                owners = [order[(place + step) % tensor] for step in steps]
                lines.append([side * own_adapters, (shards - 1 - side) * own_adapters, position] + owners)
        return np.array(lines, np.int32)

    def everyone(x):
        return lax.all_to_all(x, "tensor", 0, 0, tiled=True)

    def go(x, pairs):
        return lax.ppermute(x, "tensor", pairs)

    def body(
        hidden,
        input_norm_scale,
        query_weight,
        key_value_weight,
        adapter_down_weight,
        adapter_up_query,
        adapter_up_key_value,
        request_adapter,
        key_value_cache,
        lengths,
    ):
        position = lax.axis_index("tensor")
        side = lax.axis_index("adapter")
        rows, width = hidden.shape[1:]
        own_rows = rows // tensor
        half = rows // 2
        own_adapters = adapter_down_weight.shape[0]
        rank = adapter_up_query.shape[1]
        kv_width = adapter_up_key_value.shape[3]
        gains = input_norm_scale.reshape(tensor, 1, width)
        scalars = lax.dynamic_slice_in_dim(jnp.asarray(table(own_adapters)), side * tensor + position, 1, 0)
        own_down = adapter_down_weight.transpose(0, 2, 1)
        other_down, other_up, other_kv = (
            lax.ppermute(w, "adapter", swap) for w in (own_down, adapter_up_query, adapter_up_key_value)
        )
        cosine, sine = rotary_tables(lengths[0])

        local = (hidden[0, :half], hidden[0, half:])
        from_left = from_right = local
        blocks = []
        sums = None
        fresh_blocks = [local]
        for step in range(1, tensor // 2):
            top_left = go(from_left[0], right)
            bottom_right = go(from_right[1], left)
            top_right = go(from_right[0], left)
            bottom_left = go(from_left[1], right)
            from_left, from_right = (top_left, bottom_left), (top_right, bottom_right)
            if step == tensor // 2 - 1:
                sums = square_sums(fresh_blocks, sums)
                fresh_blocks = []
            blocks += [from_left, from_right]
            fresh_blocks += [from_left, from_right]
        last = (go(from_left[0], right), go(from_right[1], left))
        sums = square_sums(fresh_blocks, sums)
        blocks.append(last)

        inverse, keep, give, shrink = prep(
            scalars, sums, last, local, request_adapter, gains, key_value_weight, own_down, other_down, rank, tensor
        )
        shrink_parts = everyone(shrink)
        got = go(give.astype(NARROW), [(t, t ^ 1) for t in range(tensor)])
        pair = pair_sums(scalars, keep, got.astype(F32))
        kv_parts = [pair[0]] + [
            go(pair[d].astype(NARROW), [(t, t ^ (2 * d)) for t in range(tensor)]).astype(F32)
            for d in range(1, tensor // 2)
        ]
        acc = query_products(scalars, 3, [local] + blocks, gains, query_weight, inverse)
        query, kv_delta = finish(
            scalars, shrink_parts, request_adapter, (adapter_up_query, other_up), (adapter_up_key_value, other_kv), after(acc, *pair), rank
        )
        query_rows = everyone(query.reshape(tensor, own_rows, -1))
        newest, newest_heads = fresh(kv_parts, kv_delta, cosine, sine)
        attended = attend(query_rows, newest_heads, cosine, sine, key_value_cache[0], lengths)
        return attended[None], newest[None]

    return body


def solution(mesh):
    return jax.shard_map(
        make_body(mesh),
        mesh=mesh,
        in_specs=(
            P("adapter", "group", "tensor"),
            P(),
            P(None, "tensor"),
            P("tensor", None),
            P(("group", "adapter"), "tensor", None),
            P(("group", "adapter"), None, "tensor"),
            P(("group", "adapter"), None, None, None),
            P("adapter", "group"),
            P("adapter", ("group", "tensor"), None, None, None),
            P("adapter", ("group", "tensor")),
        ),
        out_specs=(
            P("adapter", ("group", "tensor"), None),
            P("adapter", ("group", "tensor"), None, None),
        ),
        check_vma=False,
    )
```

time: 92.9 us -> 81 us (0.87)
  local copies, waits for them, and re-layouts: 19.2 us -> 3.84 us
  matrix products: 4.97 us -> 0 us
  starting transfers between devices: 27.9 us -> 31.4 us
  Pallas kernels: 20.3 us -> 23.6 us
  waiting for transfers between devices: 17.4 us -> 20.5 us
  other arithmetic: 1.7 us -> 0.34 us
    slice x3 -> x0, local copies, waits for them, and re-layouts: 8.05 us -> none  [the longest x1 6.72 us: attend(): keys = cache[:, 0].reshape(own_rows, positions, key_heads, HEAD_WIDTH)]
    unnamed x32 -> x8, local copies, waits for them, and re-layouts: 8.7 us -> 2.16 us
    dot_general x3 -> x0, matrix products: 4.97 us -> none  [the longest x1 3.69 us: attend(): jnp.einsum('rkgd,rpkd->rkgp', query_heads, keys, preferred_element_type=F32)]
    pallas_call x8, Pallas kernels: 20.3 us -> 23.6 us  [the longest x1 7.14 us: query_products(): pl.pallas_call(functools.partial(query_kernel, count, columns_at), in_spe...]
    ppermute x15 -> x18, waiting for transfers between devices: 17.4 us -> 20.5 us  [go(): return lax.ppermute(x, 'tensor', pairs)]
    all_to_all x2, starting transfers between devices: 7.27 us -> 9.21 us  [everyone(): return lax.all_to_all(x, 'tensor', 0, 0, tiled=True)]
    ppermute x15 -> x18, starting transfers between devices: 20.1 us -> 21.5 us  [go(): return lax.ppermute(x, 'tensor', pairs)]
    squeeze x0 -> x1, local copies, waits for them, and re-layouts: none -> 0.98 us  [body(): local = (hidden[0, :half], hidden[0, half:])]
  transfers between devices with their start and end apart: 20 -> 23, of which waited for: 2 -> 12; matrix products, arithmetic and copies ran while one was open for 19% -> 3% of each run, Pallas kernels for 22% -> 12%
where the time goes in v2:
time: 81 us; the launch traced here: 80.5 us
  starting transfers between devices  31.4 us (39%)
  Pallas kernels  23.6 us (29%)
  waiting for transfers between devices  20.5 us (25%)
  local copies, waits for them, and re-layouts  3.84 us (5%)
  between operations  0.81 us (1%)
    ppermute x18, starting transfers between devices, go(): return lax.ppermute(x, 'tensor', pairs)  21.5 us
    ppermute x18, waiting for transfers between devices, go(): return lax.ppermute(x, 'tensor', pairs)  20.5 us
    all_to_all x2, starting transfers between devices, everyone(): return lax.all_to_all(x, 'tensor', 0, 0, tiled=True)  9.21 us
    pallas_call x1, Pallas kernels, query_products(): pl.pallas_call(functools.partial(query_kernel, count, columns_at), in_spe...  7.14 us
    pallas_call x1, Pallas kernels, attend(): pl.pallas_call(attend_kernel, in_specs=[SMEM] + [VMEM] * 4 + [HBM], out_s...  6.08 us
    pallas_call x1, Pallas kernels, prep(): pl.pallas_call(functools.partial(prep_kernel, rank), in_specs=[SMEM] + [V...  4.47 us
    pallas_call x1, Pallas kernels, finish(): pl.pallas_call(functools.partial(finish_kernel, rank), in_specs=[SMEM] +...  3.36 us
    unnamed x8, local copies, waits for them, and re-layouts  2.16 us
  transfers between devices with their start and end apart: 23, of which 12 were waited for; matrix products, arithmetic and copies ran while one was open for 3% of the time, Pallas kernels for 12%

profile of v2, /device:TPU:0, one launch (start us, length us, event | category | flops | bytes accessed | tf_op | source)
XLA Modules:
  0.0 80.5 jit_solution(13975592306368831779)
XLA Ops:
  0.6 0.5 collective-permute-start.14
  1.1 1.0 %slice_bitcast_fusion = (bf16[64,1024]{1,0:T(8,128)(2,1)S(1)}, bf16[64,1024]{1,0:T(8,128)(2,1)S(1)}) fusion(bf16[1,128,1024]{2,1,0:T(8,128)(2,1)} %param.11), kind=kLoop, calls=%fused_computation | loop fusion | bytes 524288 | tf_op jit(solution)/shard_map/squeeze | solution.py:541
  2.1 2.6 %collective-permute-start = (bf16[64,1024]{1,0:T(8,128)(2,1)S(1)}, bf16[64,1024]{1,0:T(8,128)(2,1)S(1)}, u32[]{:S(2)}, u32[]{:S(2)}) collective-permute-start(bf16[64,1024]{1,0:T(8,128)(2,1)S(1)} %get-tuple-element.29.refs_0_.top_ref), channel_id=1, source_target_pairs={{0,4},{4,8},{8,12},{12,14},{14,10},{10,6},{6,2},{2,0},{1,5},{5,9},... | collective-permute-start | bytes 393224 | tf_op jit(solution)/shard_map/ppermute | solution.py:511
  4.8 0.0 collective-permute-start.9
  4.8 2.0 %collective-permute-start.3 = (bf16[64,1024]{1,0:T(8,128)(2,1)S(1)}, bf16[64,1024]{1,0:T(8,128)(2,1)S(1)}, u32[]{:S(2)}, u32[]{:S(2)}) collective-permute-start(bf16[64,1024]{1,0:T(8,128)(2,1)S(1)} %get-tuple-element.28.refs_1_.bottom_ref), channel_id=1, source_target_pairs={{0,4},{4,8},{8,12},{12,14},{14,10},{10,6},{6,2},{2,0},{1,5},{5,9},... | collective-permute-start | bytes 393224 | tf_op jit(solution)/shard_map/ppermute | solution.py:511
  6.8 0.0 collective-permute-start.6
  6.8 2.3 %collective-permute-done.refs_2_ = bf16[64,1024]{1,0:T(8,128)(2,1)S(1)} collective-permute-done((bf16[64,1024]{1,0:T(8,128)(2,1)S(1)}, bf16[64,1024]{1,0:T(8,128)(2,1)S(1)}, u32[]{:S(2)}, u32[]{:S(2)}) %collective-permute-start) | collective-permute-done | bytes 131104 | tf_op jit(solution)/shard_map/ppermute | solution.py:511
  9.1 2.0 %collective-permute-start.1 = (bf16[64,1024]{1,0:T(8,128)(2,1)S(1)}, bf16[64,1024]{1,0:T(8,128)(2,1)S(1)}, u32[]{:S(2)}, u32[]{:S(2)}) collective-permute-start(bf16[64,1024]{1,0:T(8,128)(2,1)S(1)} %collective-permute-done.refs_2_), channel_id=1, source_target_pairs={{0,4},{4,8},{8,12},{12,14},{14,10},{10,6},{6,2},{2,0},{1,5},{5,9},... | collective-permute-start | bytes 393224 | tf_op jit(solution)/shard_map/ppermute | solution.py:511
  11.1 0.0 collective-permute-done.9.refs_5_
  11.1 0.0 collective-permute-start.10
  11.1 0.8 collective-permute-done.3.refs_3_
  11.9 2.0 %collective-permute-start.4 = (bf16[64,1024]{1,0:T(8,128)(2,1)S(1)}, bf16[64,1024]{1,0:T(8,128)(2,1)S(1)}, u32[]{:S(2)}, u32[]{:S(2)}) collective-permute-start(bf16[64,1024]{1,0:T(8,128)(2,1)S(1)} %collective-permute-done.3.refs_3_), channel_id=1, source_target_pairs={{0,4},{4,8},{8,12},{12,14},{14,10},{10,6},{6,2},{2,0},{1,5},{5,9},... | collective-permute-start | bytes 393224 | tf_op jit(solution)/shard_map/ppermute | solution.py:511
  13.9 0.0 collective-permute-done.6.refs_4_
  13.9 0.0 collective-permute-start.7
  13.9 0.8 %collective-permute-done.1.refs_6_ = bf16[64,1024]{1,0:T(8,128)(2,1)S(1)} collective-permute-done((bf16[64,1024]{1,0:T(8,128)(2,1)S(1)}, bf16[64,1024]{1,0:T(8,128)(2,1)S(1)}, u32[]{:S(2)}, u32[]{:S(2)}) %collective-permute-start.1) | collective-permute-done | bytes 131104 | tf_op jit(solution)/shard_map/ppermute | solution.py:511
  14.7 2.1 %collective-permute-start.2 = (bf16[64,1024]{1,0:T(8,128)(2,1)S(1)}, bf16[64,1024]{1,0:T(8,128)(2,1)S(1)}, u32[]{:S(2)}, u32[]{:S(2)}) collective-permute-start(bf16[64,1024]{1,0:T(8,128)(2,1)S(1)} %collective-permute-done.1.refs_6_), channel_id=1, source_target_pairs={{0,4},{4,8},{8,12},{12,14},{14,10},{10,6},{6,2},{2,0},{1,5},{5,9},... | collective-permute-start | bytes 393224 | tf_op jit(solution)/shard_map/ppermute | solution.py:511
  16.8 0.0 collective-permute-done.10.refs_9_
  16.8 0.0 collective-permute-start.11
  16.8 1.5 %collective-permute-done.4.refs_7_ = bf16[64,1024]{1,0:T(8,128)(2,1)S(1)} collective-permute-done((bf16[64,1024]{1,0:T(8,128)(2,1)S(1)}, bf16[64,1024]{1,0:T(8,128)(2,1)S(1)}, u32[]{:S(2)}, u32[]{:S(2)}) %collective-permute-start.4) | collective-permute-done | bytes 131104 | tf_op jit(solution)/shard_map/ppermute | solution.py:511
  18.3 2.1 %collective-permute-start.5 = (bf16[64,1024]{1,0:T(8,128)(2,1)S(1)}, bf16[64,1024]{1,0:T(8,128)(2,1)S(1)}, u32[]{:S(2)}, u32[]{:S(2)}) collective-permute-start(bf16[64,1024]{1,0:T(8,128)(2,1)S(1)} %collective-permute-done.4.refs_7_), channel_id=1, source_target_pairs={{0,4},{4,8},{8,12},{12,14},{14,10},{10,6},{6,2},{2,0},{1,5},{5,9},... | collective-permute-start | bytes 393224 | tf_op jit(solution)/shard_map/ppermute | solution.py:511
  20.3 0.0 collective-permute-done.7.refs_8_
  20.4 0.0 collective-permute-start.8
  20.4 0.8 collective-permute-done.2.refs_0_.refs_10_
  21.2 2.1 %collective-permute-start.12 = (bf16[64,1024]{1,0:T(8,128)(2,1)S(1)}, bf16[64,1024]{1,0:T(8,128)(2,1)S(1)}, u32[]{:S(2)}, u32[]{:S(2)}) collective-permute-start(bf16[64,1024]{1,0:T(8,128)(2,1)S(1)} %collective-permute-done.2.refs_0_.refs_10_), channel_id=1, source_target_pairs={{0,4},{4,8},{8,12},{12,14},{14,10},{10,6},{6,2},{2,0},{1,5},{5,9},... | collective-permute-start | bytes 393224 | tf_op jit(solution)/shard_map/ppermute | solution.py:511
  23.2 0.0 collective-permute-done.11.refs_3_.refs_13_
  23.2 0.0 collective-permute-start.13
  23.2 0.7 constant_dynamic-slice_fusion.scalar_ref.first_ref
  23.9 0.3 square_sums.2.refs_4_
  24.2 0.4 collective-permute-done.5.refs_1_.refs_11_
  24.6 1.4 %collective-permute-done.8.refs_2_.refs_12_ = bf16[64,1024]{1,0:T(8,128)(2,1)S(1)} collective-permute-done((bf16[64,1024]{1,0:T(8,128)(2,1)S(1)}, bf16[64,1024]{1,0:T(8,128)(2,1)S(1)}, u32[]{:S(2)}, u32[]{:S(2)}) %collective-permute-start.8) | collective-permute-done | bytes 131104 | tf_op jit(solution)/shard_map/ppermute | solution.py:511
  25.9 0.1 square_sums.3.sums_ref
  26.0 0.1 collective-permute-done.12.last_top_ref.refs_14_
  26.1 2.1 %collective-permute-done.13.last_bottom_ref.refs_15_ = bf16[64,1024]{1,0:T(8,128)(2,1)S(1)} collective-permute-done((bf16[64,1024]{1,0:T(8,128)(2,1)S(1)}, bf16[64,1024]{1,0:T(8,128)(2,1)S(1)}, u32[]{:S(2)}, u32[]{:S(2)}) %collective-permute-start.13) | collective-permute-done | bytes 131104 | tf_op jit(solution)/shard_map/ppermute | solution.py:511
  28.2 0.0 collective-permute-done.14.other_ref
  28.2 4.5 %norm_key_value_shrink.1 = (f32[128,128]{1,0:T(8,128)S(1)}, f32[4,16,2048]{2,1,0:T(8,128)}, f32[4,16,2176]{2,1,0:T(8,128)S(1)}, f32[8,80,128]{2,1,0:T(8,128)}) custom-call(s32[1,11]{1,0:T(1,128)S(1)} %constant_dynamic-slice_fusion.scalar_ref.first_ref, f32[128,128]{1,0:T(8,128)S(1)} %square_sums.3.sums_ref, ...), custom_call_target="tpu_custom_call" | custom-call | flops 700000000 | bytes 6000000 | tf_op jit(solution)/shard_map/norm_key_value_shrink/pallas_call | solution.py:186
  32.7 0.0 copy-start
  32.7 0.6 copy-done
  33.3 4.8 %all-to-all-start = ((f32[8,80,128]{2,1,0:T(8,128)}), f32[8,80,128]{2,1,0:T(8,128)S(1)}, u32[]{:S(2)}, u32[]{:S(2)}) async-start(f32[8,80,128]{2,1,0:T(8,128)} %get-tuple-element.15), calls=%async_computation | async-start | bytes 655360 | tf_op jit(solution)/shard_map/all_to_all | solution.py:508
  38.1 0.0 collective-permute-start.17
  38.2 2.1 %collective-permute-start.15 = (f16[4,16,2176]{2,1,0:T(8,128)(2,1)S(1)}, f16[4,16,2176]{2,1,0:T(8,128)(2,1)S(1)}, u32[]{:S(2)}, u32[]{:S(2)}) collective-permute-start(f16[4,16,2176]{2,1,0:T(8,128)(2,1)S(1)} %convert_element_type.41), channel_id=1, source_target_pairs={{0,2},{2,0},{4,6},{6,4},{8,10},{10,8},{12,14},{14,12},{1,3},{3,1},... | collective-permute-start | bytes 835592 | tf_op jit(solution)/shard_map/ppermute | solution.py:511
  40.2 0.2 collective-permute-start.16
  40.5 0.8 %copy-done.1 = f32[128,128]{1,0:T(8,128)S(1)} copy-done((f32[128,128]{1,0:T(8,128)S(1)}, f32[128,128]{1,0:T(8,128)}, u32[]{:S(2)}) %copy-start.1) | copy-done | bytes 65560
  41.3 7.1 %query_products.1.acc_ref = f32[128,1024]{1,0:T(8,128)S(1)} custom-call(s32[1,11]{1,0:T(1,128)S(1)} %constant_dynamic-slice_fusion.scalar_ref.first_ref, bf16[64,1024]{1,0:T(8,128)(2,1)S(1)} %get-tuple-element.29.refs_0_.top_ref, bf16[64,1024]{1,0:T(8,128)(2,1)S(1)} %get-tuple-element.28.refs_1_.bottom_ref, ...), custom_call_target="tpu_custom_call" | custom-call | flops 2000000000 | bytes 17000000 | tf_op jit(solution)/shard_map/query_products/pallas_call | solution.py:246
  48.5 1.3 %collective-permute-done.15 = f16[4,16,2176]{2,1,0:T(8,128)(2,1)S(1)} collective-permute-done((f16[4,16,2176]{2,1,0:T(8,128)(2,1)S(1)}, f16[4,16,2176]{2,1,0:T(8,128)(2,1)S(1)}, u32[]{:S(2)}, u32[]{:S(2)}) %collective-permute-start.15) | collective-permute-done | bytes 278560 | tf_op jit(solution)/shard_map/ppermute | solution.py:511
  49.8 1.3 %pair_sums.1 = (f32[16,2048]{1,0:T(8,128)S(1)}, f32[16,2176]{1,0:T(8,128)S(1)}, f32[16,2176]{1,0:T(8,128)S(1)}, f32[16,2176]{1,0:T(8,128)S(1)}) custom-call(s32[1,11]{1,0:T(1,128)S(1)} %constant_dynamic-slice_fusion.scalar_ref.first_ref, f32[4,16,2048]{2,1,0:T(8,128)} %get-tuple-element.17.keep_ref, f32[4,16,2176]{2,1,0:T(8,128)S(1)} %convert_element_type.42.got_ref), custom_call_target="tpu_custom_call" | custom-call | flops 100000 | bytes 1500000 | tf_op jit(solution)/shard_map/pair_sums/pallas_call | solution.py:339
  51.1 0.0 collective-permute-done.16.up_other_hbm
  51.1 0.0 copy-start.3
  51.1 0.7 copy-done.3
  51.8 0.0 collective-permute-done.17.kv_other_hbm
  51.8 0.0 all-to-all-done.parts_ref
  51.8 3.4 %adapter_terms.1 = (bf16[128,1024]{1,0:T(8,128)(2,1)}, f32[16,2048]{1,0:T(8,128)S(1)}) custom-call(s32[1,11]{1,0:T(1,128)S(1)} %constant_dynamic-slice_fusion.scalar_ref.first_ref, f32[8,80,128]{2,1,0:T(8,128)S(1)} %all-to-all-done.parts_ref, s32[1,128]{1,0:T(1,128)} %request_ref.3, f32[128,1024]{1,0:T(8,128)S(1)} %query_products.1.acc_ref, ...), custom_call_target="tpu_custom_call" | custom-call | flops 100000000 | bytes 2000000 | tf_op jit(solution)/shard_map/adapter_terms/pallas_call | solution.py:307
  55.2 4.4 %all-to-all-start.1 = ((bf16[8,16,1024]{2,1,0:T(8,128)(2,1)}), bf16[8,16,1024]{2,1,0:T(8,128)(2,1)S(1)}, u32[]{:S(2)}, u32[]{:S(2)}) async-start(bf16[8,16,1024]{2,1,0:T(8,128)(2,1)} %bitcast.4), calls=%async_computation.1 | async-start | bytes 524288 | tf_op jit(solution)/shard_map/all_to_all | solution.py:508
  59.6 0.0 copy-done.2
  59.6 0.1 fusion
  59.8 2.1 %collective-permute-start.18 = (f16[16,2176]{1,0:T(8,128)(2,1)S(1)}, f16[16,2176]{1,0:T(8,128)(2,1)S(1)}, u32[]{:S(2)}, u32[]{:S(2)}) collective-permute-start(f16[16,2176]{1,0:T(8,128)(2,1)S(1)} %convert_element_type.43), channel_id=1, source_target_pairs={{0,4},{2,6},{4,0},{6,2},{8,12},{10,14},{12,8},{14,10},{1,5},{3,7},... | collective-permute-start | bytes 208904 | tf_op jit(solution)/shard_map/ppermute | solution.py:511
  61.9 2.4 %collective-permute-start.19 = (f16[16,2176]{1,0:T(8,128)(2,1)S(1)}, f16[16,2176]{1,0:T(8,128)(2,1)S(1)}, u32[]{:S(2)}, u32[]{:S(2)}) collective-permute-start(f16[16,2176]{1,0:T(8,128)(2,1)S(1)} %convert_element_type.45), channel_id=1, source_target_pairs={{0,8},{2,10},{4,12},{6,14},{8,0},{10,2},{12,4},{14,6},{1,9},{3,11}... | collective-permute-start | bytes 208904 | tf_op jit(solution)/shard_map/ppermute | solution.py:511
  64.2 0.1 collective-permute-start.20
  64.3 0.1 pad_maximum_fusion
  64.4 2.9 %collective-permute-done.18 = f16[16,2176]{1,0:T(8,128)(2,1)S(1)} collective-permute-done((f16[16,2176]{1,0:T(8,128)(2,1)S(1)}, f16[16,2176]{1,0:T(8,128)(2,1)S(1)}, u32[]{:S(2)}, u32[]{:S(2)}) %collective-permute-start.18) | collective-permute-done | bytes 69664 | tf_op jit(solution)/shard_map/ppermute | solution.py:511
  67.3 6.3 %collective-permute-done.19 = f16[16,2176]{1,0:T(8,128)(2,1)S(1)} collective-permute-done((f16[16,2176]{1,0:T(8,128)(2,1)S(1)}, f16[16,2176]{1,0:T(8,128)(2,1)S(1)}, u32[]{:S(2)}, u32[]{:S(2)}) %collective-permute-start.19) | collective-permute-done | bytes 69664 | tf_op jit(solution)/shard_map/ppermute | solution.py:511
  73.6 0.0 collective-permute-done.20
  73.6 0.8 %new_key_value.1 = (bf16[16,2,1024]{2,1,0:T(2,128)(2,1)}, f32[16,16,128]{2,1,0:T(8,128)S(1)}) custom-call(f32[16,2048]{1,0:T(8,128)S(1)} %get-tuple-element.19.refs_0_, f32[16,2176]{1,0:T(8,128)S(1)} %convert_element_type.44.refs_1_, f32[16,2176]{1,0:T(8,128)S(1)} %convert_element_type.46.refs_2_, f32[16,2176]{1,0:T(8,128)S(1)} %convert_element_type.48.refs_3_, ...), custom_call_target="tpu_custom_call" | custom-call | flops 100000 | bytes 1000000 | tf_op jit(solution)/shard_map/new_key_value/pallas_call | solution.py:371
  74.4 0.0 all-to-all-done.1.query_ref
  74.4 6.1 %attention.1 = bf16[16,8192]{1,0:T(8,128)(2,1)} custom-call(s32[1,16]{1,0:T(1,128)S(1)} %copy-done.2, bf16[8,16,1024]{2,1,0:T(8,128)(2,1)S(1)} %all-to-all-done.1.query_ref, f32[16,16,128]{2,1,0:T(8,128)S(1)} %get-tuple-element.26.newest_ref, f32[16,128]{1,0:T(8,128)S(1)} %get-tuple-element.33.refs_5_.cosine_ref, ...), custom_call_target="tpu_custom_call" | custom-call | flops 400000000 | bytes 7000000 | tf_op jit(solution)/shard_map/attention/pallas_call | solution.py:469
  (12 shorter events, 0.2 us)
Async XLA Ops:
  0.6 27.6 %collective-permute-start.14 = (bf16[2,192,1024]{2,1,0:T(8,128)(2,1)}, bf16[2,192,1024]{2,1,0:T(8,128)(2,1)S(1)}, u32[]{:S(2)}, u32[]{:S(2)}) collective-permute-start(bf16[2,192,1024]{2,1,0:T(8,128)(2,1)} %bitcast.13), channel_id=1, source_target_pairs={{0,1},{1,0},{2,3},{3,2},{4,5},{5,4},{6,7},{7,6},{8,9},{9,8},{10,11... | collective-permute-start | bytes 2359304 | tf_op jit(solution)/shard_map/ppermute | solution.py:537
  2.1 6.9 %collective-permute-start = (bf16[64,1024]{1,0:T(8,128)(2,1)S(1)}, bf16[64,1024]{1,0:T(8,128)(2,1)S(1)}, u32[]{:S(2)}, u32[]{:S(2)}) collective-permute-start(bf16[64,1024]{1,0:T(8,128)(2,1)S(1)} %get-tuple-element.29.refs_0_.top_ref), channel_id=1, source_target_pairs={{0,4},{4,8},{8,12},{12,14},{14,10},{10,6},{6,2},{2,0},{1,5},{5,9},... | collective-permute-start | bytes 393224 | tf_op jit(solution)/shard_map/ppermute | solution.py:511
  4.8 6.3 %collective-permute-start.9 = (bf16[64,1024]{1,0:T(8,128)(2,1)S(1)}, bf16[64,1024]{1,0:T(8,128)(2,1)S(1)}, u32[]{:S(2)}, u32[]{:S(2)}) collective-permute-start(bf16[64,1024]{1,0:T(8,128)(2,1)S(1)} %get-tuple-element.28.refs_1_.bottom_ref), channel_id=1, source_target_pairs={{4,0},{8,4},{12,8},{14,12},{10,14},{6,10},{2,6},{0,2},{5,1},{9,5},... | collective-permute-start | bytes 393224 | tf_op jit(solution)/shard_map/ppermute | solution.py:511
  4.8 7.1 %collective-permute-start.3 = (bf16[64,1024]{1,0:T(8,128)(2,1)S(1)}, bf16[64,1024]{1,0:T(8,128)(2,1)S(1)}, u32[]{:S(2)}, u32[]{:S(2)}) collective-permute-start(bf16[64,1024]{1,0:T(8,128)(2,1)S(1)} %get-tuple-element.28.refs_1_.bottom_ref), channel_id=1, source_target_pairs={{0,4},{4,8},{8,12},{12,14},{14,10},{10,6},{6,2},{2,0},{1,5},{5,9},... | collective-permute-start | bytes 393224 | tf_op jit(solution)/shard_map/ppermute | solution.py:511
  6.8 7.1 %collective-permute-start.6 = (bf16[64,1024]{1,0:T(8,128)(2,1)S(1)}, bf16[64,1024]{1,0:T(8,128)(2,1)S(1)}, u32[]{:S(2)}, u32[]{:S(2)}) collective-permute-start(bf16[64,1024]{1,0:T(8,128)(2,1)S(1)} %get-tuple-element.29.refs_0_.top_ref), channel_id=1, source_target_pairs={{4,0},{8,4},{12,8},{14,12},{10,14},{6,10},{2,6},{0,2},{5,1},{9,5},... | collective-permute-start | bytes 393224 | tf_op jit(solution)/shard_map/ppermute | solution.py:511
  9.1 5.7 %collective-permute-start.1 = (bf16[64,1024]{1,0:T(8,128)(2,1)S(1)}, bf16[64,1024]{1,0:T(8,128)(2,1)S(1)}, u32[]{:S(2)}, u32[]{:S(2)}) collective-permute-start(bf16[64,1024]{1,0:T(8,128)(2,1)S(1)} %collective-permute-done.refs_2_), channel_id=1, source_target_pairs={{0,4},{4,8},{8,12},{12,14},{14,10},{10,6},{6,2},{2,0},{1,5},{5,9},... | collective-permute-start | bytes 393224 | tf_op jit(solution)/shard_map/ppermute | solution.py:511
  11.1 5.7 %collective-permute-start.10 = (bf16[64,1024]{1,0:T(8,128)(2,1)S(1)}, bf16[64,1024]{1,0:T(8,128)(2,1)S(1)}, u32[]{:S(2)}, u32[]{:S(2)}) collective-permute-start(bf16[64,1024]{1,0:T(8,128)(2,1)S(1)} %collective-permute-done.9.refs_5_), channel_id=1, source_target_pairs={{4,0},{8,4},{12,8},{14,12},{10,14},{6,10},{2,6},{0,2},{5,1},{9,5},... | collective-permute-start | bytes 393224 | tf_op jit(solution)/shard_map/ppermute | solution.py:511
  11.9 6.4 %collective-permute-start.4 = (bf16[64,1024]{1,0:T(8,128)(2,1)S(1)}, bf16[64,1024]{1,0:T(8,128)(2,1)S(1)}, u32[]{:S(2)}, u32[]{:S(2)}) collective-permute-start(bf16[64,1024]{1,0:T(8,128)(2,1)S(1)} %collective-permute-done.3.refs_3_), channel_id=1, source_target_pairs={{0,4},{4,8},{8,12},{12,14},{14,10},{10,6},{6,2},{2,0},{1,5},{5,9},... | collective-permute-start | bytes 393224 | tf_op jit(solution)/shard_map/ppermute | solution.py:511
  13.9 6.5 %collective-permute-start.7 = (bf16[64,1024]{1,0:T(8,128)(2,1)S(1)}, bf16[64,1024]{1,0:T(8,128)(2,1)S(1)}, u32[]{:S(2)}, u32[]{:S(2)}) collective-permute-start(bf16[64,1024]{1,0:T(8,128)(2,1)S(1)} %collective-permute-done.6.refs_4_), channel_id=1, source_target_pairs={{4,0},{8,4},{12,8},{14,12},{10,14},{6,10},{2,6},{0,2},{5,1},{9,5},... | collective-permute-start | bytes 393224 | tf_op jit(solution)/shard_map/ppermute | solution.py:511
  14.7 6.4 %collective-permute-start.2 = (bf16[64,1024]{1,0:T(8,128)(2,1)S(1)}, bf16[64,1024]{1,0:T(8,128)(2,1)S(1)}, u32[]{:S(2)}, u32[]{:S(2)}) collective-permute-start(bf16[64,1024]{1,0:T(8,128)(2,1)S(1)} %collective-permute-done.1.refs_6_), channel_id=1, source_target_pairs={{0,4},{4,8},{8,12},{12,14},{14,10},{10,6},{6,2},{2,0},{1,5},{5,9},... | collective-permute-start | bytes 393224 | tf_op jit(solution)/shard_map/ppermute | solution.py:511
  16.8 6.4 %collective-permute-start.11 = (bf16[64,1024]{1,0:T(8,128)(2,1)S(1)}, bf16[64,1024]{1,0:T(8,128)(2,1)S(1)}, u32[]{:S(2)}, u32[]{:S(2)}) collective-permute-start(bf16[64,1024]{1,0:T(8,128)(2,1)S(1)} %collective-permute-done.10.refs_9_), channel_id=1, source_target_pairs={{4,0},{8,4},{12,8},{14,12},{10,14},{6,10},{2,6},{0,2},{5,1},{9,5},... | collective-permute-start | bytes 393224 | tf_op jit(solution)/shard_map/ppermute | solution.py:511
  18.3 6.3 %collective-permute-start.5 = (bf16[64,1024]{1,0:T(8,128)(2,1)S(1)}, bf16[64,1024]{1,0:T(8,128)(2,1)S(1)}, u32[]{:S(2)}, u32[]{:S(2)}) collective-permute-start(bf16[64,1024]{1,0:T(8,128)(2,1)S(1)} %collective-permute-done.4.refs_7_), channel_id=1, source_target_pairs={{0,4},{4,8},{8,12},{12,14},{14,10},{10,6},{6,2},{2,0},{1,5},{5,9},... | collective-permute-start | bytes 393224 | tf_op jit(solution)/shard_map/ppermute | solution.py:511
  20.4 5.6 %collective-permute-start.8 = (bf16[64,1024]{1,0:T(8,128)(2,1)S(1)}, bf16[64,1024]{1,0:T(8,128)(2,1)S(1)}, u32[]{:S(2)}, u32[]{:S(2)}) collective-permute-start(bf16[64,1024]{1,0:T(8,128)(2,1)S(1)} %collective-permute-done.7.refs_8_), channel_id=1, source_target_pairs={{4,0},{8,4},{12,8},{14,12},{10,14},{6,10},{2,6},{0,2},{5,1},{9,5},... | collective-permute-start | bytes 393224 | tf_op jit(solution)/shard_map/ppermute | solution.py:511
  21.2 5.0 %collective-permute-start.12 = (bf16[64,1024]{1,0:T(8,128)(2,1)S(1)}, bf16[64,1024]{1,0:T(8,128)(2,1)S(1)}, u32[]{:S(2)}, u32[]{:S(2)}) collective-permute-start(bf16[64,1024]{1,0:T(8,128)(2,1)S(1)} %collective-permute-done.2.refs_0_.refs_10_), channel_id=1, source_target_pairs={{0,4},{4,8},{8,12},{12,14},{14,10},{10,6},{6,2},{2,0},{1,5},{5,9},... | collective-permute-start | bytes 393224 | tf_op jit(solution)/shard_map/ppermute | solution.py:511
  23.2 5.0 %collective-permute-start.13 = (bf16[64,1024]{1,0:T(8,128)(2,1)S(1)}, bf16[64,1024]{1,0:T(8,128)(2,1)S(1)}, u32[]{:S(2)}, u32[]{:S(2)}) collective-permute-start(bf16[64,1024]{1,0:T(8,128)(2,1)S(1)} %collective-permute-done.11.refs_3_.refs_13_), channel_id=1, source_target_pairs={{4,0},{8,4},{12,8},{14,12},{10,14},{6,10},{2,6},{0,2},{5,1},{9,5},... | collective-permute-start | bytes 393224 | tf_op jit(solution)/shard_map/ppermute | solution.py:511
  32.7 0.6 copy-start
  33.3 18.5 %all-to-all-start = ((f32[8,80,128]{2,1,0:T(8,128)}), f32[8,80,128]{2,1,0:T(8,128)S(1)}, u32[]{:S(2)}, u32[]{:S(2)}) async-start(f32[8,80,128]{2,1,0:T(8,128)} %get-tuple-element.15), calls=%async_computation | async-start | bytes 655360 | tf_op jit(solution)/shard_map/all_to_all | solution.py:508
  38.1 13.7 %collective-permute-start.17 = (bf16[2,2,64,1024]{3,2,1,0:T(8,128)(2,1)}, bf16[2,2,64,1024]{3,2,1,0:T(8,128)(2,1)}, u32[]{:S(2)}, u32[]{:S(2)}) collective-permute-start(bf16[2,2,64,1024]{3,2,1,0:T(8,128)(2,1)} %kv_own_hbm.1), channel_id=1, source_target_pairs={{0,1},{1,0},{2,3},{3,2},{4,5},{5,4},{6,7},{7,6},{8,9},{9,8},{10,11... | collective-permute-start | bytes 1572872 | tf_op jit(solution)/shard_map/ppermute | solution.py:537
  38.2 11.6 %collective-permute-start.15 = (f16[4,16,2176]{2,1,0:T(8,128)(2,1)S(1)}, f16[4,16,2176]{2,1,0:T(8,128)(2,1)S(1)}, u32[]{:S(2)}, u32[]{:S(2)}) collective-permute-start(f16[4,16,2176]{2,1,0:T(8,128)(2,1)S(1)} %convert_element_type.41), channel_id=1, source_target_pairs={{0,2},{2,0},{4,6},{6,4},{8,10},{10,8},{12,14},{14,12},{1,3},{3,1},... | collective-permute-start | bytes 835592 | tf_op jit(solution)/shard_map/ppermute | solution.py:511
  40.2 10.9 %collective-permute-start.16 = (bf16[2,64,1024]{2,1,0:T(8,128)(2,1)}, bf16[2,64,1024]{2,1,0:T(8,128)(2,1)S(1)}, u32[]{:S(2)}, u32[]{:S(2)}) collective-permute-start(bf16[2,64,1024]{2,1,0:T(8,128)(2,1)} %up_own_hbm.1), channel_id=1, source_target_pairs={{0,1},{1,0},{2,3},{3,2},{4,5},{5,4},{6,7},{7,6},{8,9},{9,8},{10,11... | collective-permute-start | bytes 786440 | tf_op jit(solution)/shard_map/ppermute | solution.py:537
  40.5 0.8 %copy-start.1 = (f32[128,128]{1,0:T(8,128)S(1)}, f32[128,128]{1,0:T(8,128)}, u32[]{:S(2)}) copy-start(f32[128,128]{1,0:T(8,128)} %copy-done) | copy-start | bytes 196612
  41.3 18.3 %copy-start.2 = (s32[1,16]{1,0:T(1,128)S(1)}, s32[1,16]{1,0:T(1,128)}, u32[]{:S(2)}) copy-start(s32[1,16]{1,0:T(1,128)} %lengths_ref.1) | copy-start | bytes 196
  51.1 0.7 copy-start.3
  55.2 19.2 %all-to-all-start.1 = ((bf16[8,16,1024]{2,1,0:T(8,128)(2,1)}), bf16[8,16,1024]{2,1,0:T(8,128)(2,1)S(1)}, u32[]{:S(2)}, u32[]{:S(2)}) async-start(bf16[8,16,1024]{2,1,0:T(8,128)(2,1)} %bitcast.4), calls=%async_computation.1 | async-start | bytes 524288 | tf_op jit(solution)/shard_map/all_to_all | solution.py:508
  59.8 7.5 %collective-permute-start.18 = (f16[16,2176]{1,0:T(8,128)(2,1)S(1)}, f16[16,2176]{1,0:T(8,128)(2,1)S(1)}, u32[]{:S(2)}, u32[]{:S(2)}) collective-permute-start(f16[16,2176]{1,0:T(8,128)(2,1)S(1)} %convert_element_type.43), channel_id=1, source_target_pairs={{0,4},{2,6},{4,0},{6,2},{8,12},{10,14},{12,8},{14,10},{1,5},{3,7},... | collective-permute-start | bytes 208904 | tf_op jit(solution)/shard_map/ppermute | solution.py:511
  61.9 11.7 %collective-permute-start.19 = (f16[16,2176]{1,0:T(8,128)(2,1)S(1)}, f16[16,2176]{1,0:T(8,128)(2,1)S(1)}, u32[]{:S(2)}, u32[]{:S(2)}) collective-permute-start(f16[16,2176]{1,0:T(8,128)(2,1)S(1)} %convert_element_type.45), channel_id=1, source_target_pairs={{0,8},{2,10},{4,12},{6,14},{8,0},{10,2},{12,4},{14,6},{1,9},{3,11}... | collective-permute-start | bytes 208904 | tf_op jit(solution)/shard_map/ppermute | solution.py:511
  64.2 9.3 %collective-permute-start.20 = (f16[16,2176]{1,0:T(8,128)(2,1)S(1)}, f16[16,2176]{1,0:T(8,128)(2,1)S(1)}, u32[]{:S(2)}, u32[]{:S(2)}) collective-permute-start(f16[16,2176]{1,0:T(8,128)(2,1)S(1)} %convert_element_type.47), channel_id=1, source_target_pairs={{0,12},{2,14},{4,8},{6,10},{8,4},{10,6},{12,0},{14,2},{1,13},{3,15... | collective-permute-start | bytes 208904 | tf_op jit(solution)/shard_map/ppermute | solution.py:511

commit v3 on v2

--- a/solution.py
+++ b/solution.py
@@ -115,13 +115,16 @@
     )(*operands)
 
 
-def id_column(request_ref):
-    rows = request_ref.shape[1]
-    return jnp.broadcast_to(request_ref[...].astype(F32), (LANES, rows)).T.astype(jnp.int32)
+def id_column(scalar_ref, at, count, start, rows):
+    row = start + lax.broadcasted_iota(jnp.int32, (rows, LANES), 0)
+    ids = jnp.zeros((rows, LANES), jnp.int32)
+    for label in range(1, count):
+        ids = ids + jnp.where(row >= scalar_ref[0, at + label], 1, 0)
+    return ids[:, :1]
 
 
 def prep_kernel(
-    rank, scalar_ref, sums_ref, last_top_ref, last_bottom_ref, top_ref, bottom_ref, request_ref, other_ref,
+    rank, scalar_ref, sums_ref, last_top_ref, last_bottom_ref, top_ref, bottom_ref, other_ref,
     gain_hbm, own_hbm, weight_hbm, inverse_ref, keep_ref, give_ref, shrink_ref,
     kv_ref, gain_ref, own_ref, weight_ref, sems,
 ):
@@ -146,7 +149,8 @@
     inverse_row = lax.rsqrt(total / model_width + EPS)
     inverse = jnp.broadcast_to(inverse_row, (LANES, rows)).T
     inverse_ref[...] = inverse
-    ids = id_column(request_ref)
+    adapters = 2 * own_ref.shape[0]
+    ids = id_column(scalar_ref, 3 + gain_hbm.shape[0], adapters, 0, rows)
     first[0].wait()
     block = jnp.concatenate([top_ref[...], bottom_ref[...]], axis=0).astype(F32)
     normed = (block * inverse[:, :1] * gain_ref[...]).astype(BF16)
@@ -155,7 +159,7 @@
     for side, panel_ref in enumerate((own_ref, other_ref)):
         for j in range(panel_ref.shape[0]):
             part = lax.dot_general(normed, panel_ref[j], (((1,), (1,)), ((), ())), preferred_element_type=F32)
-            shrink = shrink + jnp.where(ids[:, :1] == scalar_ref[0, side] + j, part, 0.0)
+            shrink = shrink + jnp.where(ids == scalar_ref[0, side] + j, part, 0.0)
     half = rows // 2
     packed = jnp.concatenate([shrink[:half, :rank], shrink[half:, :rank]], axis=1)
     tensor, page, _ = shrink_ref.shape
@@ -177,7 +181,7 @@
         )
 
 
-def prep(scalars, sums, last, local, request, gains, weight, own, other, rank, tensor):
+def prep(scalars, sums, last, local, gains, weight, own, other, rank, tensor):
     half, width = local[0].shape
     rows = 2 * half
     columns = weight.shape[1]
@@ -185,10 +189,10 @@
     page = rows // 2 + rows // tensor
     return pl.pallas_call(
         functools.partial(prep_kernel, rank),
-        in_specs=[SMEM] + [VMEM] * 7 + [HBM] * 3,
+        in_specs=[SMEM] + [VMEM] * 6 + [HBM] * 3,
         out_specs=[VMEM] * 4,
         out_shape=[
-            jax.ShapeDtypeStruct((rows, LANES), F32),
+            pltpu.HBM((rows, LANES), F32),
             pltpu.HBM((tensor // 2, rows // tensor, columns), F32),
             jax.ShapeDtypeStruct((tensor // 2, rows // tensor, columns + LANES), F32),
             pltpu.HBM((tensor, page, LANES), F32),
@@ -203,32 +207,48 @@
         compiler_params=params(),
         cost_estimate=pl.CostEstimate(flops=700000000, bytes_accessed=6000000, transcendentals=0),
         name="norm_key_value_shrink",
-    )(scalars, sums, *last, *local, in_hbm(request), other, in_hbm(gains), in_hbm(own), in_hbm(weight))
-
-
-def query_kernel(count, columns_at, scalar_ref, *refs):
-    blocks = refs[: 2 * count]
-    inverse_ref, gain_hbm, weight_hbm, out_ref, gain_ref, weight_ref, sems = refs[2 * count :]
-    width = blocks[0].shape[1]
+    )(scalars, sums, *last, *local, other, in_hbm(gains), in_hbm(own), in_hbm(weight))
+
+
+def query_kernel(columns_at, scalar_ref, *refs):
+    blocks = refs[:-10]
+    hidden_hbm, inverse_hbm, gain_hbm, weight_hbm, out_ref, own_ref, inverse_ref, gain_ref, weight_ref, sems = refs[-10:]
+    count = 1 + len(blocks) // 2
+    width = own_ref.shape[1]
     slots = weight_ref.shape[0]
-    owners = [scalar_ref[0, columns_at + i] for i in range(count)]
-    gain_copy = pltpu.make_async_copy(gain_hbm, gain_ref, sems.at[slots])
+    order = list(range(1, count)) + [0]
+
+    def owner(i):
+        return scalar_ref[0, columns_at + order[i]]
 
     def fetch(i):
         return pltpu.make_async_copy(
-            weight_hbm.at[pl.ds(pl.multiple_of(owners[i] * width, width), width)],
+            weight_hbm.at[pl.ds(pl.multiple_of(owner(i) * width, width), width)],
             weight_ref.at[i % slots],
             sems.at[i % slots],
         )
 
-    gain_copy.start()
+    small = [
+        pltpu.make_async_copy(inverse_hbm, inverse_ref, sems.at[slots]),
+        pltpu.make_async_copy(gain_hbm, gain_ref, sems.at[slots + 1]),
+        pltpu.make_async_copy(hidden_hbm, own_ref, sems.at[slots + 2]),
+    ]
+    for copy in small[:2]:
+        copy.start()
     for i in range(min(slots, count)):
         fetch(i).start()
-    gain_copy.wait()
+    small[2].start()
+    for copy in small[:2]:
+        copy.wait()
     inverse = inverse_ref[:, :1]
     for i in range(count):
-        gain = gain_ref[pl.ds(owners[i], 1)].reshape(1, width)
-        block = jnp.concatenate([blocks[2 * i][...], blocks[2 * i + 1][...]], axis=0).astype(F32)
+        gain = gain_ref[pl.ds(owner(i), 1)].reshape(1, width)
+        if order[i] == 0:
+            small[2].wait()
+            block = own_ref[...].astype(F32)
+        else:
+            at = 2 * order[i] - 2
+            block = jnp.concatenate([blocks[at][...], blocks[at + 1][...]], axis=0).astype(F32)
         normed = (block * inverse * gain).astype(BF16)
         fetch(i).wait()
         part = dot(normed, weight_ref[i % slots])
@@ -237,76 +257,83 @@
             fetch(i + slots).start()
 
 
-def query_products(scalars, columns_at, blocks, gains, weight, inverse):
-    width = blocks[0][0].shape[1]
+def query_products(scalars, columns_at, hidden, blocks, gains, weight, inverse):
+    rows, width = hidden.shape
     columns = weight.shape[1]
-    count = len(blocks)
+    count = 1 + len(blocks)
     flat = [half for block in blocks for half in block]
     slots = min(SLOTS, count)
     return pl.pallas_call(
-        functools.partial(query_kernel, count, columns_at),
-        in_specs=[SMEM] + [VMEM] * (2 * count + 1) + [HBM] * 2,
+        functools.partial(query_kernel, columns_at),
+        in_specs=[SMEM] + [VMEM] * len(flat) + [HBM] * 4,
         out_specs=VMEM,
-        out_shape=jax.ShapeDtypeStruct((inverse.shape[0], columns), F32),
+        out_shape=jax.ShapeDtypeStruct((rows, columns), F32),
         scratch_shapes=[
+            pltpu.VMEM(hidden.shape, BF16),
+            pltpu.VMEM(inverse.shape, F32),
             pltpu.VMEM(gains.shape, F32),
             pltpu.VMEM((slots, width, columns), BF16),
-            pltpu.SemaphoreType.DMA((slots + 1,)),
+            pltpu.SemaphoreType.DMA((slots + 3,)),
         ],
-        compiler_params=params(16),
+        compiler_params=params(24),
         cost_estimate=pl.CostEstimate(flops=2000000000, bytes_accessed=17000000, transcendentals=0),
         name="query_products",
-    )(scalars, *flat, inverse, in_hbm(gains), in_hbm(weight))
+    )(scalars, *flat, in_hbm(hidden), in_hbm(inverse), in_hbm(gains), in_hbm(weight))
+
+
+def spread(ids, values, first, second, each):
+    labels = [first + j for j in range(each)] + [second + j for j in range(each)]
+    return jnp.concatenate([jnp.where(ids == label, values, 0.0) for label in labels], axis=1).astype(BF16)
 
 
 def finish_kernel(
-    rank, first_ref, parts_ref, request_ref, acc_ref, up_own_hbm, up_other_hbm, kv_own_hbm, kv_other_hbm,
-    out_ref, kv_delta_ref, up_own_ref, up_other_ref, kv_own_ref, kv_other_ref, column_ref, sems,
+    rank, scalar_ref, parts_ref, acc_ref, up_other_ref, up_own_hbm, kv_own_hbm, kv_other_hbm,
+    out_ref, kv_delta_ref, up_ref, kv_ref, sems,
 ):
-    rows = request_ref.shape[1]
-    half = rows // 2
-    kv_width = kv_delta_ref.shape[1] // 2
-    sources = (up_own_hbm, up_other_hbm, kv_own_hbm, kv_other_hbm)
-    targets = (up_own_ref, up_other_ref, kv_own_ref, kv_other_ref)
-    copies = [pltpu.make_async_copy(sources[i], targets[i], sems.at[i]) for i in range(4)]
+    each = up_own_hbm.shape[0]
+    copies = [
+        pltpu.make_async_copy(up_own_hbm, up_ref, sems.at[0]),
+        pltpu.make_async_copy(kv_own_hbm, kv_ref.at[pl.ds(0, each)], sems.at[1]),
+        pltpu.make_async_copy(kv_other_hbm, kv_ref.at[pl.ds(each, each)], sems.at[2]),
+    ]
     for copy in copies:
         copy.start()
-    ids_ref = id_column(request_ref)
+    rows = out_ref.shape[0]
+    half = rows // 2
+    own_rows, kv_columns = kv_delta_ref.shape
+    kv_width = kv_columns // 2
+    columns = out_ref.shape[1]
+    first, second = scalar_ref[0, 0], scalar_ref[0, 1]
+    at = 3 + parts_ref.shape[0]
+    ids = id_column(scalar_ref, at, 2 * each, 0, rows)
+    own_ids = id_column(scalar_ref, at, 2 * each, scalar_ref[0, 2] * own_rows, own_rows)
     total = parts_ref[0]
     for peer in range(1, parts_ref.shape[0]):
         total = total + parts_ref[peer]
-    for copy in copies:
-        copy.wait()
     shrink = jnp.concatenate([total[:half, :rank], total[:half, rank:]], axis=0)
-    own_rows = kv_delta_ref.shape[0]
-    own = total[half:]
-    column_ref[...] = ids_ref
-    own_ids = column_ref[pl.ds(pl.multiple_of(first_ref[0, 2] * own_rows, own_rows), own_rows)]
-    delta = None
-    key_delta = value_delta = None
-    for side, (up_ref, kv_ref) in enumerate(((up_own_ref, kv_own_ref), (up_other_ref, kv_other_ref))):
-        for j in range(up_ref.shape[0]):
-            mine = ids_ref[:, :1] == first_ref[0, side] + j
-            part = dot(jnp.where(mine, shrink, 0.0).astype(BF16), up_ref[j])
-            delta = part if delta is None else delta + part
-            kept = jnp.where(own_ids[:, :1] == first_ref[0, side] + j, own, 0.0).astype(BF16)
-            key_part = dot(kept[:, :rank], kv_ref[j, 0])
-            value_part = dot(kept[:, rank:], kv_ref[j, 1])
-            key_delta = key_part if key_delta is None else key_delta + key_part
-            value_delta = value_part if value_delta is None else value_delta + value_part
-    out_ref[...] = (acc_ref[...] + delta).astype(BF16)
-    kv_delta_ref[:, :kv_width] = key_delta
-    kv_delta_ref[:, kv_width:] = value_delta
-
-
-def finish(scalars, parts, request, ups, kv_ups, acc, rank):
-    rows = request.shape[1]
+    query_spread = spread(ids, shrink, first, second, each)
+    key_spread = spread(own_ids, total[half:, :rank], first, second, each)
+    value_spread = spread(own_ids, total[half:, rank:], first, second, each)
+    depth = 2 * each * rank
+    other_part = dot(query_spread[:, depth // 2 :], up_other_ref[...].reshape(depth // 2, columns))
+    copies[0].wait()
+    own_part = dot(query_spread[:, : depth // 2], up_ref[...].reshape(depth // 2, columns))
+    out_ref[...] = (acc_ref[...] + own_part + other_part).astype(BF16)
+    copies[1].wait()
+    copies[2].wait()
+    kv_delta_ref[:, :kv_width] = dot(key_spread, kv_ref[:, 0].reshape(depth, kv_width))
+    kv_delta_ref[:, kv_width:] = dot(value_spread, kv_ref[:, 1].reshape(depth, kv_width))
+
+
+def finish(scalars, parts, ups, kv_ups, acc, rank):
+    rows = acc.shape[0]
     own_rows = rows // parts.shape[0]
     columns = ups[0].shape[2]
     kv_columns = 2 * kv_ups[0].shape[3]
+    each = ups[0].shape[0]
     return pl.pallas_call(
         functools.partial(finish_kernel, rank),
-        in_specs=[SMEM] + [VMEM] * 3 + [HBM] * 4,
+        in_specs=[SMEM] + [VMEM] * 3 + [HBM] * 3,
         out_specs=[VMEM, VMEM],
         out_shape=[
             jax.ShapeDtypeStruct((rows, columns), BF16),
@@ -314,16 +341,13 @@
         ],
         scratch_shapes=[
             pltpu.VMEM(ups[0].shape, BF16),
-            pltpu.VMEM(ups[1].shape, BF16),
-            pltpu.VMEM(kv_ups[0].shape, BF16),
-            pltpu.VMEM(kv_ups[1].shape, BF16),
-            pltpu.VMEM((rows, LANES), jnp.int32),
-            pltpu.SemaphoreType.DMA((4,)),
+            pltpu.VMEM((2 * each,) + kv_ups[0].shape[1:], BF16),
+            pltpu.SemaphoreType.DMA((3,)),
         ],
         compiler_params=params(),
         cost_estimate=pl.CostEstimate(flops=100000000, bytes_accessed=2000000, transcendentals=0),
         name="adapter_terms",
-    )(scalars, parts, in_hbm(request), acc, *[in_hbm(value) for value in (*ups, *kv_ups)])
+    )(scalars, parts, acc, ups[1], in_hbm(ups[0]), in_hbm(kv_ups[0]), in_hbm(kv_ups[1]))
 
 
 def pair_kernel(scalar_ref, keep_ref, got_ref, *out_refs):
@@ -477,7 +501,7 @@
             pltpu.VMEM((own_rows, heads, cache.shape[2]), BF16),
             pltpu.VMEM((own_rows, heads, HEAD_WIDTH), F32),
             pltpu.VMEM((2, own_rows) + cache.shape[2:], BF16),
-            pltpu.SemaphoreType.DMA((2, 4)),
+            pltpu.SemaphoreType.DMA((2, 2)),
         ],
         compiler_params=params(),
         cost_estimate=pl.CostEstimate(flops=400000000, bytes_accessed=7000000, transcendentals=100000),
@@ -531,11 +555,16 @@
         rank = adapter_up_query.shape[1]
         kv_width = adapter_up_key_value.shape[3]
         gains = input_norm_scale.reshape(tensor, 1, width)
-        scalars = lax.dynamic_slice_in_dim(jnp.asarray(table(own_adapters)), side * tensor + position, 1, 0)
+        labels = jnp.arange(shards * own_adapters, dtype=jnp.int32)
+        first_rows = jnp.sum((request_adapter < labels[:, None]).astype(jnp.int32), axis=1)
+        scalars = jnp.concatenate(
+            [
+                lax.dynamic_slice_in_dim(jnp.asarray(table(own_adapters)), side * tensor + position, 1, 0),
+                first_rows[None],
+            ],
+            axis=1,
+        )
         own_down = adapter_down_weight.transpose(0, 2, 1)
-        other_down, other_up, other_kv = (
-            lax.ppermute(w, "adapter", swap) for w in (own_down, adapter_up_query, adapter_up_key_value)
-        )
         cosine, sine = rotary_tables(lengths[0])
 
         local = (hidden[0, :half], hidden[0, half:])
@@ -555,24 +584,27 @@
             blocks += [from_left, from_right]
             fresh_blocks += [from_left, from_right]
         last = (go(from_left[0], right), go(from_right[1], left))
+        panels = (own_down, adapter_up_query, adapter_up_key_value)
+
+        other_down, other_up, other_kv = (lax.ppermute(w, "adapter", swap) for w in panels)
         sums = square_sums(fresh_blocks, sums)
         blocks.append(last)
 
         inverse, keep, give, shrink = prep(
-            scalars, sums, last, local, request_adapter, gains, key_value_weight, own_down, other_down, rank, tensor
+            scalars, sums, last, local, gains, key_value_weight, own_down, other_down, rank, tensor
         )
         shrink_parts = everyone(shrink)
+        acc = query_products(scalars, 3, hidden[0], blocks, gains, query_weight, inverse)
         got = go(give.astype(NARROW), [(t, t ^ 1) for t in range(tensor)])
         pair = pair_sums(scalars, keep, got.astype(F32))
         kv_parts = [pair[0]] + [
             go(pair[d].astype(NARROW), [(t, t ^ (2 * d)) for t in range(tensor)]).astype(F32)
             for d in range(1, tensor // 2)
         ]
-        acc = query_products(scalars, 3, [local] + blocks, gains, query_weight, inverse)
         query, kv_delta = finish(
-            scalars, shrink_parts, request_adapter, (adapter_up_query, other_up), (adapter_up_key_value, other_kv), after(acc, *pair), rank
+            scalars, shrink_parts, (adapter_up_query, other_up), (adapter_up_key_value, other_kv), acc, rank
         )
-        query_rows = everyone(query.reshape(tensor, own_rows, -1))
+        query_rows = everyone(after(query, got).reshape(tensor, own_rows, -1))
         newest, newest_heads = fresh(kv_parts, kv_delta, cosine, sine)
         attended = attend(query_rows, newest_heads, cosine, sine, key_value_cache[0], lengths)
         return attended[None], newest[None]

time: 81 us -> 76.6 us (0.946)
  waiting for transfers between devices: 20.5 us -> 17.6 us
  local copies, waits for them, and re-layouts: 3.84 us -> 1.68 us
  other arithmetic: 0.34 us -> 1.9 us
  Pallas kernels: 23.6 us -> 22.6 us
    ppermute x18, waiting for transfers between devices: 20.5 us -> 17.6 us  [go(): return lax.ppermute(x, 'tensor', pairs)]
    unnamed x8 -> x2, local copies, waits for them, and re-layouts: 2.16 us -> 0.01 us
  transfers between devices with their start and end apart: 23 -> 23, of which waited for: 12 -> 11; matrix products, arithmetic and copies ran while one was open for 3% -> 5% of each run, Pallas kernels for 12% -> 16%
where the time goes in v3:
time: 76.6 us; the launch traced here: 76.2 us
  starting transfers between devices  31.6 us (41%)
  Pallas kernels  22.6 us (30%)
  waiting for transfers between devices  17.6 us (23%)
  other arithmetic  1.9 us (2%)
  local copies, waits for them, and re-layouts  1.68 us (2%)
  between operations  0.8 us (1%)
    ppermute x18, starting transfers between devices, go(): return lax.ppermute(x, 'tensor', pairs)  21.5 us
    ppermute x18, waiting for transfers between devices, go(): return lax.ppermute(x, 'tensor', pairs)  17.6 us
    all_to_all x2, starting transfers between devices, everyone(): return lax.all_to_all(x, 'tensor', 0, 0, tiled=True)  9.4 us
    pallas_call x1, Pallas kernels, query_products(): pl.pallas_call(functools.partial(query_kernel, columns_at), in_specs=[SME...  7.26 us
    pallas_call x1, Pallas kernels, attend(): pl.pallas_call(attend_kernel, in_specs=[SMEM] + [VMEM] * 4 + [HBM], out_s...  5.84 us
    pallas_call x1, Pallas kernels, prep(): pl.pallas_call(functools.partial(prep_kernel, rank), in_specs=[SMEM] + [V...  4.41 us
    pallas_call x1, Pallas kernels, finish(): pl.pallas_call(functools.partial(finish_kernel, rank), in_specs=[SMEM] +...  2.56 us
  transfers between devices with their start and end apart: 23, of which 11 were waited for; matrix products, arithmetic and copies ran while one was open for 5% of the time, Pallas kernels for 16%

profile of v3, /device:TPU:0, one launch (start us, length us, event | category | flops | bytes accessed | tf_op | source)
XLA Modules:
  0.0 76.2 jit_solution(7999050358158533500)
XLA Ops:
  0.6 0.5 collective-permute-start.14
  1.1 1.0 %slice_bitcast_fusion = (bf16[64,1024]{1,0:T(8,128)(2,1)S(1)}, bf16[64,1024]{1,0:T(8,128)(2,1)S(1)}) fusion(bf16[1,128,1024]{2,1,0:T(8,128)(2,1)} %param.11), kind=kLoop, calls=%fused_computation | loop fusion | bytes 524288 | tf_op jit(solution)/shard_map/squeeze | solution.py:570
  2.1 2.6 %collective-permute-start = (bf16[64,1024]{1,0:T(8,128)(2,1)S(1)}, bf16[64,1024]{1,0:T(8,128)(2,1)S(1)}, u32[]{:S(2)}, u32[]{:S(2)}) collective-permute-start(bf16[64,1024]{1,0:T(8,128)(2,1)S(1)} %get-tuple-element.29.refs_0_.top_ref), channel_id=1, source_target_pairs={{0,4},{4,8},{8,12},{12,14},{14,10},{10,6},{6,2},{2,0},{1,5},{5,9},... | collective-permute-start | bytes 393224 | tf_op jit(solution)/shard_map/ppermute | solution.py:535
  4.8 0.0 collective-permute-start.9
  4.8 2.0 %collective-permute-start.3 = (bf16[64,1024]{1,0:T(8,128)(2,1)S(1)}, bf16[64,1024]{1,0:T(8,128)(2,1)S(1)}, u32[]{:S(2)}, u32[]{:S(2)}) collective-permute-start(bf16[64,1024]{1,0:T(8,128)(2,1)S(1)} %get-tuple-element.28.refs_1_.bottom_ref), channel_id=1, source_target_pairs={{0,4},{4,8},{8,12},{12,14},{14,10},{10,6},{6,2},{2,0},{1,5},{5,9},... | collective-permute-start | bytes 393224 | tf_op jit(solution)/shard_map/ppermute | solution.py:535
  6.8 0.0 collective-permute-start.6
  6.8 2.3 %collective-permute-done.refs_2_.refs_0_ = bf16[64,1024]{1,0:T(8,128)(2,1)S(1)} collective-permute-done((bf16[64,1024]{1,0:T(8,128)(2,1)S(1)}, bf16[64,1024]{1,0:T(8,128)(2,1)S(1)}, u32[]{:S(2)}, u32[]{:S(2)}) %collective-permute-start) | collective-permute-done | bytes 131104 | tf_op jit(solution)/shard_map/ppermute | solution.py:535
  9.1 2.0 %collective-permute-start.1 = (bf16[64,1024]{1,0:T(8,128)(2,1)S(1)}, bf16[64,1024]{1,0:T(8,128)(2,1)S(1)}, u32[]{:S(2)}, u32[]{:S(2)}) collective-permute-start(bf16[64,1024]{1,0:T(8,128)(2,1)S(1)} %collective-permute-done.refs_2_.refs_0_), channel_id=1, source_target_pairs={{0,4},{4,8},{8,12},{12,14},{14,10},{10,6},{6,2},{2,0},{1,5},{5,9},... | collective-permute-start | bytes 393224 | tf_op jit(solution)/shard_map/ppermute | solution.py:535
  11.1 0.0 collective-permute-done.9.refs_5_.refs_3_
  11.1 0.0 collective-permute-start.10
  11.1 0.8 %collective-permute-done.3.refs_3_.refs_1_ = bf16[64,1024]{1,0:T(8,128)(2,1)S(1)} collective-permute-done((bf16[64,1024]{1,0:T(8,128)(2,1)S(1)}, bf16[64,1024]{1,0:T(8,128)(2,1)S(1)}, u32[]{:S(2)}, u32[]{:S(2)}) %collective-permute-start.3) | collective-permute-done | bytes 131104 | tf_op jit(solution)/shard_map/ppermute | solution.py:535
  11.9 2.0 %collective-permute-start.4 = (bf16[64,1024]{1,0:T(8,128)(2,1)S(1)}, bf16[64,1024]{1,0:T(8,128)(2,1)S(1)}, u32[]{:S(2)}, u32[]{:S(2)}) collective-permute-start(bf16[64,1024]{1,0:T(8,128)(2,1)S(1)} %collective-permute-done.3.refs_3_.refs_1_), channel_id=1, source_target_pairs={{0,4},{4,8},{8,12},{12,14},{14,10},{10,6},{6,2},{2,0},{1,5},{5,9},... | collective-permute-start | bytes 393224 | tf_op jit(solution)/shard_map/ppermute | solution.py:535
  13.9 0.0 collective-permute-done.6.refs_4_.refs_2_
  13.9 0.0 collective-permute-start.7
  13.9 0.8 %collective-permute-done.1.refs_6_.refs_4_ = bf16[64,1024]{1,0:T(8,128)(2,1)S(1)} collective-permute-done((bf16[64,1024]{1,0:T(8,128)(2,1)S(1)}, bf16[64,1024]{1,0:T(8,128)(2,1)S(1)}, u32[]{:S(2)}, u32[]{:S(2)}) %collective-permute-start.1) | collective-permute-done | bytes 131104 | tf_op jit(solution)/shard_map/ppermute | solution.py:535
  14.7 2.0 %collective-permute-start.2 = (bf16[64,1024]{1,0:T(8,128)(2,1)S(1)}, bf16[64,1024]{1,0:T(8,128)(2,1)S(1)}, u32[]{:S(2)}, u32[]{:S(2)}) collective-permute-start(bf16[64,1024]{1,0:T(8,128)(2,1)S(1)} %collective-permute-done.1.refs_6_.refs_4_), channel_id=1, source_target_pairs={{0,4},{4,8},{8,12},{12,14},{14,10},{10,6},{6,2},{2,0},{1,5},{5,9},... | collective-permute-start | bytes 393224 | tf_op jit(solution)/shard_map/ppermute | solution.py:535
  16.8 0.0 collective-permute-done.10.refs_9_.refs_7_
  16.8 0.0 collective-permute-start.11
  16.8 0.8 %convert_reduce_fusion = s32[4]{0:T(128)S(1)} fusion(s32[128]{0:T(128)} %bitcast.23), kind=kLoop, calls=%fused_computation.7 | loop fusion | flops 1532 | bytes 528 | tf_op jit(solution)/shard_map/reduce_sum | solution.py:559
  17.6 0.7 collective-permute-done.4.refs_7_.refs_5_
  18.3 2.1 %collective-permute-start.5 = (bf16[64,1024]{1,0:T(8,128)(2,1)S(1)}, bf16[64,1024]{1,0:T(8,128)(2,1)S(1)}, u32[]{:S(2)}, u32[]{:S(2)}) collective-permute-start(bf16[64,1024]{1,0:T(8,128)(2,1)S(1)} %collective-permute-done.4.refs_7_.refs_5_), channel_id=1, source_target_pairs={{0,4},{4,8},{8,12},{12,14},{14,10},{10,6},{6,2},{2,0},{1,5},{5,9},... | collective-permute-start | bytes 393224 | tf_op jit(solution)/shard_map/ppermute | solution.py:535
  20.3 0.0 collective-permute-done.7.refs_8_.refs_6_
  20.4 0.0 collective-permute-start.8
  20.4 0.8 %collective-permute-done.2.refs_0_.refs_8_ = bf16[64,1024]{1,0:T(8,128)(2,1)S(1)} collective-permute-done((bf16[64,1024]{1,0:T(8,128)(2,1)S(1)}, bf16[64,1024]{1,0:T(8,128)(2,1)S(1)}, u32[]{:S(2)}, u32[]{:S(2)}) %collective-permute-start.2) | collective-permute-done | bytes 131104 | tf_op jit(solution)/shard_map/ppermute | solution.py:535
  21.2 2.0 %collective-permute-start.12 = (bf16[64,1024]{1,0:T(8,128)(2,1)S(1)}, bf16[64,1024]{1,0:T(8,128)(2,1)S(1)}, u32[]{:S(2)}, u32[]{:S(2)}) collective-permute-start(bf16[64,1024]{1,0:T(8,128)(2,1)S(1)} %collective-permute-done.2.refs_0_.refs_8_), channel_id=1, source_target_pairs={{0,4},{4,8},{8,12},{12,14},{14,10},{10,6},{6,2},{2,0},{1,5},{5,9},... | collective-permute-start | bytes 393224 | tf_op jit(solution)/shard_map/ppermute | solution.py:535
  23.2 0.0 collective-permute-done.11.refs_3_.refs_11_
  23.2 0.0 collective-permute-start.13
  23.2 0.7 constant_dynamic-slice_fusion
  23.9 0.1 pad_add_fusion.scalar_ref
  24.0 0.3 square_sums.2.refs_4_
  24.2 0.3 collective-permute-done.5.refs_1_.refs_9_
  24.6 1.4 %collective-permute-done.8.refs_2_.refs_10_ = bf16[64,1024]{1,0:T(8,128)(2,1)S(1)} collective-permute-done((bf16[64,1024]{1,0:T(8,128)(2,1)S(1)}, bf16[64,1024]{1,0:T(8,128)(2,1)S(1)}, u32[]{:S(2)}, u32[]{:S(2)}) %collective-permute-start.8) | collective-permute-done | bytes 131104 | tf_op jit(solution)/shard_map/ppermute | solution.py:535
  25.9 0.1 square_sums.3.sums_ref
  26.0 0.1 collective-permute-done.12.last_top_ref.refs_12_
  26.1 2.1 %collective-permute-done.13.last_bottom_ref.refs_13_ = bf16[64,1024]{1,0:T(8,128)(2,1)S(1)} collective-permute-done((bf16[64,1024]{1,0:T(8,128)(2,1)S(1)}, bf16[64,1024]{1,0:T(8,128)(2,1)S(1)}, u32[]{:S(2)}, u32[]{:S(2)}) %collective-permute-start.13) | collective-permute-done | bytes 131104 | tf_op jit(solution)/shard_map/ppermute | solution.py:535
  28.2 0.0 collective-permute-done.14.other_ref
  28.2 4.4 %norm_key_value_shrink.1 = (f32[128,128]{1,0:T(8,128)}, f32[4,16,2048]{2,1,0:T(8,128)}, f32[4,16,2176]{2,1,0:T(8,128)S(1)}, f32[8,80,128]{2,1,0:T(8,128)}) custom-call(s32[1,15]{1,0:T(1,128)S(1)} %pad_add_fusion.scalar_ref, f32[128,128]{1,0:T(8,128)S(1)} %square_sums.3.sums_ref, bf16[64,1024]{1,0:T(8,128)(2,1)S(1)} %collective-permute-done.12.last_top_ref.refs_12_, ...), custom_call_target="tpu_custom_call" | custom-call | flops 700000000 | bytes 6000000 | tf_op jit(solution)/shard_map/norm_key_value_shrink/pallas_call | solution.py:190
  32.6 4.8 %all-to-all-start = ((f32[8,80,128]{2,1,0:T(8,128)}), f32[8,80,128]{2,1,0:T(8,128)S(1)}, u32[]{:S(2)}, u32[]{:S(2)}) async-start(f32[8,80,128]{2,1,0:T(8,128)} %get-tuple-element.15), calls=%async_computation | async-start | bytes 655360 | tf_op jit(solution)/shard_map/all_to_all | solution.py:532
  37.5 0.0 collective-permute-start.16
  37.5 0.7 convert_element_type.45
  38.2 2.0 %collective-permute-start.17 = (f16[4,16,2176]{2,1,0:T(8,128)(2,1)}, f16[4,16,2176]{2,1,0:T(8,128)(2,1)S(1)}, u32[]{:S(2)}, u32[]{:S(2)}) collective-permute-start(f16[4,16,2176]{2,1,0:T(8,128)(2,1)} %convert_element_type.45), channel_id=1, source_target_pairs={{0,2},{2,0},{4,6},{6,4},{8,10},{10,8},{12,14},{14,12},{1,3},{3,1},... | collective-permute-start | bytes 835592 | tf_op jit(solution)/shard_map/ppermute | solution.py:535
  40.2 0.2 collective-permute-start.15
  40.4 0.0 copy-start
  40.5 7.3 %query_products.1.acc_ref = f32[128,1024]{1,0:T(8,128)S(1)} custom-call(s32[1,15]{1,0:T(1,128)S(1)} %pad_add_fusion.scalar_ref, bf16[64,1024]{1,0:T(8,128)(2,1)S(1)} %collective-permute-done.refs_2_.refs_0_, bf16[64,1024]{1,0:T(8,128)(2,1)S(1)} %collective-permute-done.3.refs_3_.refs_1_, bf16[64,1024]{1,0:T(8,128)(2,1)S(1)} %collective-permute-done.6.refs_4_.refs_2_, ...), custom_call_target="tpu_custom_call" | custom-call | flops 2000000000 | bytes 17000000 | tf_op jit(solution)/shard_map/query_products/pallas_call | solution.py:266
  47.7 0.0 collective-permute-done.15.up_other_ref
  47.7 0.0 collective-permute-done.16.kv_other_hbm
  47.7 0.0 all-to-all-done.parts_ref
  47.8 2.6 %adapter_terms.1 = (bf16[128,1024]{1,0:T(8,128)(2,1)}, f32[16,2048]{1,0:T(8,128)S(1)}) custom-call(s32[1,15]{1,0:T(1,128)S(1)} %pad_add_fusion.scalar_ref, f32[8,80,128]{2,1,0:T(8,128)S(1)} %all-to-all-done.parts_ref, f32[128,1024]{1,0:T(8,128)S(1)} %query_products.1.acc_ref, bf16[2,64,1024]{2,1,0:T(8,128)(2,1)S(1)} %collective-permute-done.15.up_other_ref, ...), custom_call_target="tpu_custom_call" | custom-call | flops 100000000 | bytes 2000000 | tf_op jit(solution)/shard_map/adapter_terms/pallas_call | solution.py:334
  50.3 0.0 collective-permute-done.17
  50.3 4.6 %all-to-all-start.1 = ((bf16[8,16,1024]{2,1,0:T(8,128)(2,1)}), bf16[8,16,1024]{2,1,0:T(8,128)(2,1)S(1)}, u32[]{:S(2)}, u32[]{:S(2)}) async-start(bf16[8,16,1024]{2,1,0:T(8,128)(2,1)} %bitcast.7), calls=%async_computation.1 | async-start | bytes 524288 | tf_op jit(solution)/shard_map/all_to_all | solution.py:532
  54.9 0.0 copy-done
  54.9 0.1 fusion
  55.1 1.3 %pair_sums.1 = (f32[16,2048]{1,0:T(8,128)S(1)}, f32[16,2176]{1,0:T(8,128)S(1)}, f32[16,2176]{1,0:T(8,128)S(1)}, f32[16,2176]{1,0:T(8,128)S(1)}) custom-call(s32[1,15]{1,0:T(1,128)S(1)} %pad_add_fusion.scalar_ref, f32[4,16,2048]{2,1,0:T(8,128)} %get-tuple-element.20.keep_ref, f32[4,16,2176]{2,1,0:T(8,128)S(1)} %convert_element_type.46.got_ref), custom_call_target="tpu_custom_call" | custom-call | flops 100000 | bytes 1500000 | tf_op jit(solution)/shard_map/pair_sums/pallas_call | solution.py:363
  56.4 2.1 %collective-permute-start.18 = (f16[16,2176]{1,0:T(8,128)(2,1)S(1)}, f16[16,2176]{1,0:T(8,128)(2,1)S(1)}, u32[]{:S(2)}, u32[]{:S(2)}) collective-permute-start(f16[16,2176]{1,0:T(8,128)(2,1)S(1)} %convert_element_type.47), channel_id=1, source_target_pairs={{0,4},{2,6},{4,0},{6,2},{8,12},{10,14},{12,8},{14,10},{1,5},{3,7},... | collective-permute-start | bytes 208904 | tf_op jit(solution)/shard_map/ppermute | solution.py:535
  58.5 2.4 %collective-permute-start.19 = (f16[16,2176]{1,0:T(8,128)(2,1)S(1)}, f16[16,2176]{1,0:T(8,128)(2,1)S(1)}, u32[]{:S(2)}, u32[]{:S(2)}) collective-permute-start(f16[16,2176]{1,0:T(8,128)(2,1)S(1)} %convert_element_type.49), channel_id=1, source_target_pairs={{0,8},{2,10},{4,12},{6,14},{8,0},{10,2},{12,4},{14,6},{1,9},{3,11}... | collective-permute-start | bytes 208904 | tf_op jit(solution)/shard_map/ppermute | solution.py:535
  60.9 0.1 collective-permute-start.20
  61.0 0.1 pad_maximum_fusion
  61.1 2.4 %collective-permute-done.18 = f16[16,2176]{1,0:T(8,128)(2,1)S(1)} collective-permute-done((f16[16,2176]{1,0:T(8,128)(2,1)S(1)}, f16[16,2176]{1,0:T(8,128)(2,1)S(1)}, u32[]{:S(2)}, u32[]{:S(2)}) %collective-permute-start.18) | collective-permute-done | bytes 69664 | tf_op jit(solution)/shard_map/ppermute | solution.py:535
  63.6 5.9 %collective-permute-done.19 = f16[16,2176]{1,0:T(8,128)(2,1)S(1)} collective-permute-done((f16[16,2176]{1,0:T(8,128)(2,1)S(1)}, f16[16,2176]{1,0:T(8,128)(2,1)S(1)}, u32[]{:S(2)}, u32[]{:S(2)}) %collective-permute-start.19) | collective-permute-done | bytes 69664 | tf_op jit(solution)/shard_map/ppermute | solution.py:535
  69.4 0.0 collective-permute-done.20
  69.5 0.8 %new_key_value.1 = (bf16[16,2,1024]{2,1,0:T(2,128)(2,1)}, f32[16,16,128]{2,1,0:T(8,128)S(1)}) custom-call(f32[16,2048]{1,0:T(8,128)S(1)} %get-tuple-element.21.refs_0_, f32[16,2176]{1,0:T(8,128)S(1)} %convert_element_type.48.refs_1_, f32[16,2176]{1,0:T(8,128)S(1)} %convert_element_type.50.refs_2_, f32[16,2176]{1,0:T(8,128)S(1)} %convert_element_type.52.refs_3_, ...), custom_call_target="tpu_custom_call" | custom-call | flops 100000 | bytes 1000000 | tf_op jit(solution)/shard_map/new_key_value/pallas_call | solution.py:395
  70.3 0.0 all-to-all-done.1.query_ref
  70.3 5.8 %attention.1 = bf16[16,8192]{1,0:T(8,128)(2,1)} custom-call(s32[1,16]{1,0:T(1,128)S(1)} %copy-done, bf16[8,16,1024]{2,1,0:T(8,128)(2,1)S(1)} %all-to-all-done.1.query_ref, f32[16,16,128]{2,1,0:T(8,128)S(1)} %get-tuple-element.26.newest_ref, f32[16,128]{1,0:T(8,128)S(1)} %get-tuple-element.33.refs_5_.cosine_ref, ...), custom_call_target="tpu_custom_call" | custom-call | flops 400000000 | bytes 7000000 | tf_op jit(solution)/shard_map/attention/pallas_call | solution.py:493
  (9 shorter events, 0.1 us)
Async XLA Ops:
  0.6 27.6 %collective-permute-start.14 = (bf16[2,192,1024]{2,1,0:T(8,128)(2,1)}, bf16[2,192,1024]{2,1,0:T(8,128)(2,1)S(1)}, u32[]{:S(2)}, u32[]{:S(2)}) collective-permute-start(bf16[2,192,1024]{2,1,0:T(8,128)(2,1)} %bitcast.17), channel_id=1, source_target_pairs={{0,1},{1,0},{2,3},{3,2},{4,5},{5,4},{6,7},{7,6},{8,9},{9,8},{10,11... | collective-permute-start | bytes 2359304 | tf_op jit(solution)/shard_map/ppermute | solution.py:589
  2.1 6.9 %collective-permute-start = (bf16[64,1024]{1,0:T(8,128)(2,1)S(1)}, bf16[64,1024]{1,0:T(8,128)(2,1)S(1)}, u32[]{:S(2)}, u32[]{:S(2)}) collective-permute-start(bf16[64,1024]{1,0:T(8,128)(2,1)S(1)} %get-tuple-element.29.refs_0_.top_ref), channel_id=1, source_target_pairs={{0,4},{4,8},{8,12},{12,14},{14,10},{10,6},{6,2},{2,0},{1,5},{5,9},... | collective-permute-start | bytes 393224 | tf_op jit(solution)/shard_map/ppermute | solution.py:535
  4.8 6.3 %collective-permute-start.9 = (bf16[64,1024]{1,0:T(8,128)(2,1)S(1)}, bf16[64,1024]{1,0:T(8,128)(2,1)S(1)}, u32[]{:S(2)}, u32[]{:S(2)}) collective-permute-start(bf16[64,1024]{1,0:T(8,128)(2,1)S(1)} %get-tuple-element.28.refs_1_.bottom_ref), channel_id=1, source_target_pairs={{4,0},{8,4},{12,8},{14,12},{10,14},{6,10},{2,6},{0,2},{5,1},{9,5},... | collective-permute-start | bytes 393224 | tf_op jit(solution)/shard_map/ppermute | solution.py:535
  4.8 7.1 %collective-permute-start.3 = (bf16[64,1024]{1,0:T(8,128)(2,1)S(1)}, bf16[64,1024]{1,0:T(8,128)(2,1)S(1)}, u32[]{:S(2)}, u32[]{:S(2)}) collective-permute-start(bf16[64,1024]{1,0:T(8,128)(2,1)S(1)} %get-tuple-element.28.refs_1_.bottom_ref), channel_id=1, source_target_pairs={{0,4},{4,8},{8,12},{12,14},{14,10},{10,6},{6,2},{2,0},{1,5},{5,9},... | collective-permute-start | bytes 393224 | tf_op jit(solution)/shard_map/ppermute | solution.py:535
  6.8 7.1 %collective-permute-start.6 = (bf16[64,1024]{1,0:T(8,128)(2,1)S(1)}, bf16[64,1024]{1,0:T(8,128)(2,1)S(1)}, u32[]{:S(2)}, u32[]{:S(2)}) collective-permute-start(bf16[64,1024]{1,0:T(8,128)(2,1)S(1)} %get-tuple-element.29.refs_0_.top_ref), channel_id=1, source_target_pairs={{4,0},{8,4},{12,8},{14,12},{10,14},{6,10},{2,6},{0,2},{5,1},{9,5},... | collective-permute-start | bytes 393224 | tf_op jit(solution)/shard_map/ppermute | solution.py:535
  9.1 5.7 %collective-permute-start.1 = (bf16[64,1024]{1,0:T(8,128)(2,1)S(1)}, bf16[64,1024]{1,0:T(8,128)(2,1)S(1)}, u32[]{:S(2)}, u32[]{:S(2)}) collective-permute-start(bf16[64,1024]{1,0:T(8,128)(2,1)S(1)} %collective-permute-done.refs_2_.refs_0_), channel_id=1, source_target_pairs={{0,4},{4,8},{8,12},{12,14},{14,10},{10,6},{6,2},{2,0},{1,5},{5,9},... | collective-permute-start | bytes 393224 | tf_op jit(solution)/shard_map/ppermute | solution.py:535
  11.1 5.7 %collective-permute-start.10 = (bf16[64,1024]{1,0:T(8,128)(2,1)S(1)}, bf16[64,1024]{1,0:T(8,128)(2,1)S(1)}, u32[]{:S(2)}, u32[]{:S(2)}) collective-permute-start(bf16[64,1024]{1,0:T(8,128)(2,1)S(1)} %collective-permute-done.9.refs_5_.refs_3_), channel_id=1, source_target_pairs={{4,0},{8,4},{12,8},{14,12},{10,14},{6,10},{2,6},{0,2},{5,1},{9,5},... | collective-permute-start | bytes 393224 | tf_op jit(solution)/shard_map/ppermute | solution.py:535
  11.9 6.4 %collective-permute-start.4 = (bf16[64,1024]{1,0:T(8,128)(2,1)S(1)}, bf16[64,1024]{1,0:T(8,128)(2,1)S(1)}, u32[]{:S(2)}, u32[]{:S(2)}) collective-permute-start(bf16[64,1024]{1,0:T(8,128)(2,1)S(1)} %collective-permute-done.3.refs_3_.refs_1_), channel_id=1, source_target_pairs={{0,4},{4,8},{8,12},{12,14},{14,10},{10,6},{6,2},{2,0},{1,5},{5,9},... | collective-permute-start | bytes 393224 | tf_op jit(solution)/shard_map/ppermute | solution.py:535
  13.9 6.5 %collective-permute-start.7 = (bf16[64,1024]{1,0:T(8,128)(2,1)S(1)}, bf16[64,1024]{1,0:T(8,128)(2,1)S(1)}, u32[]{:S(2)}, u32[]{:S(2)}) collective-permute-start(bf16[64,1024]{1,0:T(8,128)(2,1)S(1)} %collective-permute-done.6.refs_4_.refs_2_), channel_id=1, source_target_pairs={{4,0},{8,4},{12,8},{14,12},{10,14},{6,10},{2,6},{0,2},{5,1},{9,5},... | collective-permute-start | bytes 393224 | tf_op jit(solution)/shard_map/ppermute | solution.py:535
  14.7 6.4 %collective-permute-start.2 = (bf16[64,1024]{1,0:T(8,128)(2,1)S(1)}, bf16[64,1024]{1,0:T(8,128)(2,1)S(1)}, u32[]{:S(2)}, u32[]{:S(2)}) collective-permute-start(bf16[64,1024]{1,0:T(8,128)(2,1)S(1)} %collective-permute-done.1.refs_6_.refs_4_), channel_id=1, source_target_pairs={{0,4},{4,8},{8,12},{12,14},{14,10},{10,6},{6,2},{2,0},{1,5},{5,9},... | collective-permute-start | bytes 393224 | tf_op jit(solution)/shard_map/ppermute | solution.py:535
  16.8 6.4 %collective-permute-start.11 = (bf16[64,1024]{1,0:T(8,128)(2,1)S(1)}, bf16[64,1024]{1,0:T(8,128)(2,1)S(1)}, u32[]{:S(2)}, u32[]{:S(2)}) collective-permute-start(bf16[64,1024]{1,0:T(8,128)(2,1)S(1)} %collective-permute-done.10.refs_9_.refs_7_), channel_id=1, source_target_pairs={{4,0},{8,4},{12,8},{14,12},{10,14},{6,10},{2,6},{0,2},{5,1},{9,5},... | collective-permute-start | bytes 393224 | tf_op jit(solution)/shard_map/ppermute | solution.py:535
  18.3 6.3 %collective-permute-start.5 = (bf16[64,1024]{1,0:T(8,128)(2,1)S(1)}, bf16[64,1024]{1,0:T(8,128)(2,1)S(1)}, u32[]{:S(2)}, u32[]{:S(2)}) collective-permute-start(bf16[64,1024]{1,0:T(8,128)(2,1)S(1)} %collective-permute-done.4.refs_7_.refs_5_), channel_id=1, source_target_pairs={{0,4},{4,8},{8,12},{12,14},{14,10},{10,6},{6,2},{2,0},{1,5},{5,9},... | collective-permute-start | bytes 393224 | tf_op jit(solution)/shard_map/ppermute | solution.py:535
  20.4 5.6 %collective-permute-start.8 = (bf16[64,1024]{1,0:T(8,128)(2,1)S(1)}, bf16[64,1024]{1,0:T(8,128)(2,1)S(1)}, u32[]{:S(2)}, u32[]{:S(2)}) collective-permute-start(bf16[64,1024]{1,0:T(8,128)(2,1)S(1)} %collective-permute-done.7.refs_8_.refs_6_), channel_id=1, source_target_pairs={{4,0},{8,4},{12,8},{14,12},{10,14},{6,10},{2,6},{0,2},{5,1},{9,5},... | collective-permute-start | bytes 393224 | tf_op jit(solution)/shard_map/ppermute | solution.py:535
  21.2 5.0 %collective-permute-start.12 = (bf16[64,1024]{1,0:T(8,128)(2,1)S(1)}, bf16[64,1024]{1,0:T(8,128)(2,1)S(1)}, u32[]{:S(2)}, u32[]{:S(2)}) collective-permute-start(bf16[64,1024]{1,0:T(8,128)(2,1)S(1)} %collective-permute-done.2.refs_0_.refs_8_), channel_id=1, source_target_pairs={{0,4},{4,8},{8,12},{12,14},{14,10},{10,6},{6,2},{2,0},{1,5},{5,9},... | collective-permute-start | bytes 393224 | tf_op jit(solution)/shard_map/ppermute | solution.py:535
  23.2 5.0 %collective-permute-start.13 = (bf16[64,1024]{1,0:T(8,128)(2,1)S(1)}, bf16[64,1024]{1,0:T(8,128)(2,1)S(1)}, u32[]{:S(2)}, u32[]{:S(2)}) collective-permute-start(bf16[64,1024]{1,0:T(8,128)(2,1)S(1)} %collective-permute-done.11.refs_3_.refs_11_), channel_id=1, source_target_pairs={{4,0},{8,4},{12,8},{14,12},{10,14},{6,10},{2,6},{0,2},{5,1},{9,5},... | collective-permute-start | bytes 393224 | tf_op jit(solution)/shard_map/ppermute | solution.py:535
  32.6 15.1 %all-to-all-start = ((f32[8,80,128]{2,1,0:T(8,128)}), f32[8,80,128]{2,1,0:T(8,128)S(1)}, u32[]{:S(2)}, u32[]{:S(2)}) async-start(f32[8,80,128]{2,1,0:T(8,128)} %get-tuple-element.15), calls=%async_computation | async-start | bytes 655360 | tf_op jit(solution)/shard_map/all_to_all | solution.py:532
  37.5 10.3 %collective-permute-start.16 = (bf16[2,2,64,1024]{3,2,1,0:T(8,128)(2,1)}, bf16[2,2,64,1024]{3,2,1,0:T(8,128)(2,1)}, u32[]{:S(2)}, u32[]{:S(2)}) collective-permute-start(bf16[2,2,64,1024]{3,2,1,0:T(8,128)(2,1)} %kv_own_hbm.1), channel_id=1, source_target_pairs={{0,1},{1,0},{2,3},{3,2},{4,5},{5,4},{6,7},{7,6},{8,9},{9,8},{10,11... | collective-permute-start | bytes 1572872 | tf_op jit(solution)/shard_map/ppermute | solution.py:589
  38.2 12.1 %collective-permute-start.17 = (f16[4,16,2176]{2,1,0:T(8,128)(2,1)}, f16[4,16,2176]{2,1,0:T(8,128)(2,1)S(1)}, u32[]{:S(2)}, u32[]{:S(2)}) collective-permute-start(f16[4,16,2176]{2,1,0:T(8,128)(2,1)} %convert_element_type.45), channel_id=1, source_target_pairs={{0,2},{2,0},{4,6},{6,4},{8,10},{10,8},{12,14},{14,12},{1,3},{3,1},... | collective-permute-start | bytes 835592 | tf_op jit(solution)/shard_map/ppermute | solution.py:535
  40.2 7.5 %collective-permute-start.15 = (bf16[2,64,1024]{2,1,0:T(8,128)(2,1)}, bf16[2,64,1024]{2,1,0:T(8,128)(2,1)S(1)}, u32[]{:S(2)}, u32[]{:S(2)}) collective-permute-start(bf16[2,64,1024]{2,1,0:T(8,128)(2,1)} %up_own_hbm.1), channel_id=1, source_target_pairs={{0,1},{1,0},{2,3},{3,2},{4,5},{5,4},{6,7},{7,6},{8,9},{9,8},{10,11... | collective-permute-start | bytes 786440 | tf_op jit(solution)/shard_map/ppermute | solution.py:589
  40.4 14.4 %copy-start = (s32[1,16]{1,0:T(1,128)S(1)}, s32[1,16]{1,0:T(1,128)}, u32[]{:S(2)}) copy-start(s32[1,16]{1,0:T(1,128)} %lengths_ref.1) | copy-start | bytes 196
  50.3 20.0 %all-to-all-start.1 = ((bf16[8,16,1024]{2,1,0:T(8,128)(2,1)}), bf16[8,16,1024]{2,1,0:T(8,128)(2,1)S(1)}, u32[]{:S(2)}, u32[]{:S(2)}) async-start(bf16[8,16,1024]{2,1,0:T(8,128)(2,1)} %bitcast.7), calls=%async_computation.1 | async-start | bytes 524288 | tf_op jit(solution)/shard_map/all_to_all | solution.py:532
  56.4 7.1 %collective-permute-start.18 = (f16[16,2176]{1,0:T(8,128)(2,1)S(1)}, f16[16,2176]{1,0:T(8,128)(2,1)S(1)}, u32[]{:S(2)}, u32[]{:S(2)}) collective-permute-start(f16[16,2176]{1,0:T(8,128)(2,1)S(1)} %convert_element_type.47), channel_id=1, source_target_pairs={{0,4},{2,6},{4,0},{6,2},{8,12},{10,14},{12,8},{14,10},{1,5},{3,7},... | collective-permute-start | bytes 208904 | tf_op jit(solution)/shard_map/ppermute | solution.py:535
  58.5 10.9 %collective-permute-start.19 = (f16[16,2176]{1,0:T(8,128)(2,1)S(1)}, f16[16,2176]{1,0:T(8,128)(2,1)S(1)}, u32[]{:S(2)}, u32[]{:S(2)}) collective-permute-start(f16[16,2176]{1,0:T(8,128)(2,1)S(1)} %convert_element_type.49), channel_id=1, source_target_pairs={{0,8},{2,10},{4,12},{6,14},{8,0},{10,2},{12,4},{14,6},{1,9},{3,11}... | collective-permute-start | bytes 208904 | tf_op jit(solution)/shard_map/ppermute | solution.py:535
  60.9 8.5 %collective-permute-start.20 = (f16[16,2176]{1,0:T(8,128)(2,1)S(1)}, f16[16,2176]{1,0:T(8,128)(2,1)S(1)}, u32[]{:S(2)}, u32[]{:S(2)}) collective-permute-start(f16[16,2176]{1,0:T(8,128)(2,1)S(1)} %convert_element_type.51), channel_id=1, source_target_pairs={{0,12},{2,14},{4,8},{6,10},{8,4},{10,6},{12,0},{14,2},{1,13},{3,15... | collective-permute-start | bytes 208904 | tf_op jit(solution)/shard_map/ppermute | solution.py:535

commit v4 on v3

--- a/solution.py
+++ b/solution.py
@@ -125,9 +125,10 @@
 
 def prep_kernel(
     rank, scalar_ref, sums_ref, last_top_ref, last_bottom_ref, top_ref, bottom_ref, other_ref,
-    gain_hbm, own_hbm, weight_hbm, inverse_ref, keep_ref, give_ref, shrink_ref,
-    kv_ref, gain_ref, own_ref, weight_ref, sems,
+    gain_hbm, own_hbm, weight_hbm, inverse_ref, keep_ref, shrink_ref, *refs,
 ):
+    give_refs = refs[:-5]
+    kv_ref, gain_ref, own_ref, weight_ref, sems = refs[-5:]
     rows, width = inverse_ref.shape[0], top_ref.shape[1]
     model_width = gain_hbm.shape[0] * width
     chunks = sems.shape[0] - 2
@@ -173,12 +174,11 @@
         part = dot(normed[:, c * depth : (c + 1) * depth], weight_ref[c * depth : (c + 1) * depth])
         total = part if total is None else total + part
     kv_ref[...] = total
-    parity = scalar_ref[0, 2] % 2
-    for pair in range(tensor // 2):
-        keep_ref[pair] = kv_ref[pl.ds(pl.multiple_of((2 * pair + parity) * own_rows, own_rows), own_rows)]
-        give_ref[pair] = pack_rows(
-            kv_ref[pl.ds(pl.multiple_of((2 * pair + 1 - parity) * own_rows, own_rows), own_rows)]
-        )
+    index = lax.div(scalar_ref[0, 2], 2)
+    both = 2 * own_rows
+    keep_ref[...] = kv_ref[pl.ds(pl.multiple_of(index * both, both), both)]
+    for distance, give_ref in enumerate(give_refs, 1):
+        give_ref[...] = pack_rows(kv_ref[pl.ds(pl.multiple_of((index ^ distance) * both, both), both)])
 
 
 def prep(scalars, sums, last, local, gains, weight, own, other, rank, tensor):
@@ -190,13 +190,13 @@
     return pl.pallas_call(
         functools.partial(prep_kernel, rank),
         in_specs=[SMEM] + [VMEM] * 6 + [HBM] * 3,
-        out_specs=[VMEM] * 4,
+        out_specs=[VMEM] * (tensor // 2 + 2),
         out_shape=[
             pltpu.HBM((rows, LANES), F32),
-            pltpu.HBM((tensor // 2, rows // tensor, columns), F32),
-            jax.ShapeDtypeStruct((tensor // 2, rows // tensor, columns + LANES), F32),
+            pltpu.HBM((2 * rows // tensor, columns), F32),
             pltpu.HBM((tensor, page, LANES), F32),
-        ],
+        ]
+        + [jax.ShapeDtypeStruct((2 * rows // tensor, columns + LANES), F32)] * (tensor // 2 - 1),
         scratch_shapes=[
             pltpu.VMEM((rows, columns), F32),
             pltpu.VMEM((1, width), F32),
@@ -350,26 +350,33 @@
     )(scalars, parts, acc, ups[1], in_hbm(ups[0]), in_hbm(kv_ups[0]), in_hbm(kv_ups[1]))
 
 
-def pair_kernel(scalar_ref, keep_ref, got_ref, *out_refs):
-    index = lax.div(scalar_ref[0, 2], 2)
-    for distance, out_ref in enumerate(out_refs):
-        other = index ^ distance
-        total = keep_ref[other] + unpack_rows(got_ref[other])
-        out_ref[...] = total if distance == 0 else pack_rows(total)
-
-
-def pair_sums(scalars, keep, got):
-    count, own_rows, columns = keep.shape
+def line_kernel(scalar_ref, keep_ref, *refs):
+    got_refs, (mine_ref, give_ref, total_ref) = refs[:-3], refs[-3:]
+    own_rows = mine_ref.shape[0]
+    total = keep_ref[...]
+    for got_ref in got_refs:
+        total = total + unpack_rows(got_ref[...])
+    total_ref[...] = total
+    parity = scalar_ref[0, 2] % 2
+    mine_ref[...] = total_ref[pl.ds(pl.multiple_of(parity * own_rows, own_rows), own_rows)]
+    give_ref[...] = pack_rows(total_ref[pl.ds(pl.multiple_of((1 - parity) * own_rows, own_rows), own_rows)])
+
+
+def line_sums(scalars, keep, got):
+    both, columns = keep.shape
     return pl.pallas_call(
-        pair_kernel,
-        in_specs=[SMEM, VMEM, VMEM],
-        out_specs=[VMEM] * count,
-        out_shape=[jax.ShapeDtypeStruct((own_rows, columns), F32)]
-        + [jax.ShapeDtypeStruct((own_rows, columns + LANES), F32)] * (count - 1),
+        line_kernel,
+        in_specs=[SMEM] + [VMEM] * (1 + len(got)),
+        out_specs=[VMEM] * 2,
+        out_shape=[
+            jax.ShapeDtypeStruct((both // 2, columns), F32),
+            jax.ShapeDtypeStruct((both // 2, columns + LANES), F32),
+        ],
+        scratch_shapes=[pltpu.VMEM(keep.shape, F32)],
         compiler_params=params(),
         cost_estimate=pl.CostEstimate(flops=100000, bytes_accessed=1500000, transcendentals=0),
-        name="pair_sums",
-    )(scalars, in_hbm(keep), got)
+        name="line_sums",
+    )(scalars, in_hbm(keep), *got)
 
 
 def fresh_kernel(count, *refs):
@@ -590,21 +597,21 @@
         sums = square_sums(fresh_blocks, sums)
         blocks.append(last)
 
-        inverse, keep, give, shrink = prep(
+        inverse, keep, shrink, *gives = prep(
             scalars, sums, last, local, gains, key_value_weight, own_down, other_down, rank, tensor
         )
-        shrink_parts = everyone(shrink)
+        gives = [give.astype(NARROW) for give in gives]
+        shrink_parts = everyone(after(shrink, *gives))
         acc = query_products(scalars, 3, hidden[0], blocks, gains, query_weight, inverse)
-        got = go(give.astype(NARROW), [(t, t ^ 1) for t in range(tensor)])
-        pair = pair_sums(scalars, keep, got.astype(F32))
-        kv_parts = [pair[0]] + [
-            go(pair[d].astype(NARROW), [(t, t ^ (2 * d)) for t in range(tensor)]).astype(F32)
-            for d in range(1, tensor // 2)
+        got = [
+            go(give, [(t, t ^ (2 * d)) for t in range(tensor)]) for d, give in enumerate(gives, 1)
         ]
+        mine, give = line_sums(scalars, keep, [part.astype(F32) for part in got])
+        kv_parts = [mine, go(give.astype(NARROW), [(t, t ^ 1) for t in range(tensor)]).astype(F32)]
         query, kv_delta = finish(
             scalars, shrink_parts, (adapter_up_query, other_up), (adapter_up_key_value, other_kv), acc, rank
         )
-        query_rows = everyone(after(query, got).reshape(tensor, own_rows, -1))
+        query_rows = everyone(after(query, *got).reshape(tensor, own_rows, -1))
         newest, newest_heads = fresh(kv_parts, kv_delta, cosine, sine)
         attended = attend(query_rows, newest_heads, cosine, sine, key_value_cache[0], lengths)
         return attended[None], newest[None]

time: 76.6 us -> 75.9 us (level)
  waiting for transfers between devices: 17.6 us -> 15.4 us
  other arithmetic: 1.9 us -> 2.76 us
  starting transfers between devices: 31.6 us -> 32.4 us
    ppermute x18, waiting for transfers between devices: 17.6 us -> 15.2 us  [go(): return lax.ppermute(x, 'tensor', pairs)]
    convert_element_type x8, other arithmetic: 0.85 us -> 1.71 us  [the longest x3 0.97 us: body(): mine, give = line_sums(scalars, keep, [part.astype(F32) for part in got])]
  transfers between devices with their start and end apart: 23 -> 23, of which waited for: 11 -> 12; matrix products, arithmetic and copies ran while one was open for 5% -> 5% of each run, Pallas kernels for 16% -> 16%
where the time goes in v4:
time: 75.9 us; the launch traced here: 75.4 us
  starting transfers between devices  32.4 us (43%)
  Pallas kernels  22.4 us (30%)
  waiting for transfers between devices  15.4 us (20%)
  other arithmetic  2.76 us (4%)
  local copies, waits for them, and re-layouts  1.68 us (2%)
  between operations  0.79 us (1%)
    ppermute x18, starting transfers between devices, go(): return lax.ppermute(x, 'tensor', pairs)  21.3 us
    ppermute x18, waiting for transfers between devices, go(): return lax.ppermute(x, 'tensor', pairs)  15.2 us
    all_to_all x2, starting transfers between devices, everyone(): return lax.all_to_all(x, 'tensor', 0, 0, tiled=True)  10 us
    pallas_call x1, Pallas kernels, query_products(): pl.pallas_call(functools.partial(query_kernel, columns_at), in_specs=[SME...  7.26 us
    pallas_call x1, Pallas kernels, attend(): pl.pallas_call(attend_kernel, in_specs=[SMEM] + [VMEM] * 4 + [HBM], out_s...  5.84 us
    pallas_call x1, Pallas kernels, prep(): pl.pallas_call(functools.partial(prep_kernel, rank), in_specs=[SMEM] + [V...  4.31 us
    pallas_call x1, Pallas kernels, finish(): pl.pallas_call(functools.partial(finish_kernel, rank), in_specs=[SMEM] +...  2.58 us
  transfers between devices with their start and end apart: 23, of which 12 were waited for; matrix products, arithmetic and copies ran while one was open for 5% of the time, Pallas kernels for 16%

profile of v4, /device:TPU:0, one launch (start us, length us, event | category | flops | bytes accessed | tf_op | source)
XLA Modules:
  0.0 75.4 jit_solution(1307248570406779375)
XLA Ops:
  0.6 0.5 collective-permute-start.14
  1.1 1.0 %slice_bitcast_fusion = (bf16[64,1024]{1,0:T(8,128)(2,1)S(1)}, bf16[64,1024]{1,0:T(8,128)(2,1)S(1)}) fusion(bf16[1,128,1024]{2,1,0:T(8,128)(2,1)} %param.11), kind=kLoop, calls=%fused_computation | loop fusion | bytes 524288 | tf_op jit(solution)/shard_map/squeeze | solution.py:577
  2.1 2.6 %collective-permute-start = (bf16[64,1024]{1,0:T(8,128)(2,1)S(1)}, bf16[64,1024]{1,0:T(8,128)(2,1)S(1)}, u32[]{:S(2)}, u32[]{:S(2)}) collective-permute-start(bf16[64,1024]{1,0:T(8,128)(2,1)S(1)} %get-tuple-element.31.refs_0_.top_ref), channel_id=1, source_target_pairs={{0,4},{4,8},{8,12},{12,14},{14,10},{10,6},{6,2},{2,0},{1,5},{5,9},... | collective-permute-start | bytes 393224 | tf_op jit(solution)/shard_map/ppermute | solution.py:542
  4.8 0.0 collective-permute-start.9
  4.8 2.0 %collective-permute-start.3 = (bf16[64,1024]{1,0:T(8,128)(2,1)S(1)}, bf16[64,1024]{1,0:T(8,128)(2,1)S(1)}, u32[]{:S(2)}, u32[]{:S(2)}) collective-permute-start(bf16[64,1024]{1,0:T(8,128)(2,1)S(1)} %get-tuple-element.30.refs_1_.bottom_ref), channel_id=1, source_target_pairs={{0,4},{4,8},{8,12},{12,14},{14,10},{10,6},{6,2},{2,0},{1,5},{5,9},... | collective-permute-start | bytes 393224 | tf_op jit(solution)/shard_map/ppermute | solution.py:542
  6.8 0.0 collective-permute-start.6
  6.8 2.3 %collective-permute-done.refs_2_.refs_0_ = bf16[64,1024]{1,0:T(8,128)(2,1)S(1)} collective-permute-done((bf16[64,1024]{1,0:T(8,128)(2,1)S(1)}, bf16[64,1024]{1,0:T(8,128)(2,1)S(1)}, u32[]{:S(2)}, u32[]{:S(2)}) %collective-permute-start) | collective-permute-done | bytes 131104 | tf_op jit(solution)/shard_map/ppermute | solution.py:542
  9.1 2.0 %collective-permute-start.1 = (bf16[64,1024]{1,0:T(8,128)(2,1)S(1)}, bf16[64,1024]{1,0:T(8,128)(2,1)S(1)}, u32[]{:S(2)}, u32[]{:S(2)}) collective-permute-start(bf16[64,1024]{1,0:T(8,128)(2,1)S(1)} %collective-permute-done.refs_2_.refs_0_), channel_id=1, source_target_pairs={{0,4},{4,8},{8,12},{12,14},{14,10},{10,6},{6,2},{2,0},{1,5},{5,9},... | collective-permute-start | bytes 393224 | tf_op jit(solution)/shard_map/ppermute | solution.py:542
  11.1 0.0 collective-permute-done.9.refs_5_.refs_3_
  11.1 0.0 collective-permute-start.10
  11.1 0.8 %collective-permute-done.3.refs_3_.refs_1_ = bf16[64,1024]{1,0:T(8,128)(2,1)S(1)} collective-permute-done((bf16[64,1024]{1,0:T(8,128)(2,1)S(1)}, bf16[64,1024]{1,0:T(8,128)(2,1)S(1)}, u32[]{:S(2)}, u32[]{:S(2)}) %collective-permute-start.3) | collective-permute-done | bytes 131104 | tf_op jit(solution)/shard_map/ppermute | solution.py:542
  11.9 2.0 %collective-permute-start.4 = (bf16[64,1024]{1,0:T(8,128)(2,1)S(1)}, bf16[64,1024]{1,0:T(8,128)(2,1)S(1)}, u32[]{:S(2)}, u32[]{:S(2)}) collective-permute-start(bf16[64,1024]{1,0:T(8,128)(2,1)S(1)} %collective-permute-done.3.refs_3_.refs_1_), channel_id=1, source_target_pairs={{0,4},{4,8},{8,12},{12,14},{14,10},{10,6},{6,2},{2,0},{1,5},{5,9},... | collective-permute-start | bytes 393224 | tf_op jit(solution)/shard_map/ppermute | solution.py:542
  13.9 0.0 collective-permute-done.6.refs_4_.refs_2_
  13.9 0.0 collective-permute-start.7
  13.9 0.8 %collective-permute-done.1.refs_6_.refs_4_ = bf16[64,1024]{1,0:T(8,128)(2,1)S(1)} collective-permute-done((bf16[64,1024]{1,0:T(8,128)(2,1)S(1)}, bf16[64,1024]{1,0:T(8,128)(2,1)S(1)}, u32[]{:S(2)}, u32[]{:S(2)}) %collective-permute-start.1) | collective-permute-done | bytes 131104 | tf_op jit(solution)/shard_map/ppermute | solution.py:542
  14.7 2.0 %collective-permute-start.2 = (bf16[64,1024]{1,0:T(8,128)(2,1)S(1)}, bf16[64,1024]{1,0:T(8,128)(2,1)S(1)}, u32[]{:S(2)}, u32[]{:S(2)}) collective-permute-start(bf16[64,1024]{1,0:T(8,128)(2,1)S(1)} %collective-permute-done.1.refs_6_.refs_4_), channel_id=1, source_target_pairs={{0,4},{4,8},{8,12},{12,14},{14,10},{10,6},{6,2},{2,0},{1,5},{5,9},... | collective-permute-start | bytes 393224 | tf_op jit(solution)/shard_map/ppermute | solution.py:542
  16.8 0.0 collective-permute-done.10.refs_9_.refs_7_
  16.8 0.0 collective-permute-start.11
  16.8 0.8 %convert_reduce_fusion = s32[4]{0:T(128)S(1)} fusion(s32[128]{0:T(128)} %bitcast.23), kind=kLoop, calls=%fused_computation.7 | loop fusion | flops 1532 | bytes 528 | tf_op jit(solution)/shard_map/reduce_sum | solution.py:566
  17.6 0.7 collective-permute-done.4.refs_7_.refs_5_
  18.3 2.1 %collective-permute-start.5 = (bf16[64,1024]{1,0:T(8,128)(2,1)S(1)}, bf16[64,1024]{1,0:T(8,128)(2,1)S(1)}, u32[]{:S(2)}, u32[]{:S(2)}) collective-permute-start(bf16[64,1024]{1,0:T(8,128)(2,1)S(1)} %collective-permute-done.4.refs_7_.refs_5_), channel_id=1, source_target_pairs={{0,4},{4,8},{8,12},{12,14},{14,10},{10,6},{6,2},{2,0},{1,5},{5,9},... | collective-permute-start | bytes 393224 | tf_op jit(solution)/shard_map/ppermute | solution.py:542
  20.3 0.0 collective-permute-done.7.refs_8_.refs_6_
  20.4 0.0 collective-permute-start.8
  20.4 0.8 %collective-permute-done.2.refs_0_.refs_8_ = bf16[64,1024]{1,0:T(8,128)(2,1)S(1)} collective-permute-done((bf16[64,1024]{1,0:T(8,128)(2,1)S(1)}, bf16[64,1024]{1,0:T(8,128)(2,1)S(1)}, u32[]{:S(2)}, u32[]{:S(2)}) %collective-permute-start.2) | collective-permute-done | bytes 131104 | tf_op jit(solution)/shard_map/ppermute | solution.py:542
  21.2 2.0 %collective-permute-start.12 = (bf16[64,1024]{1,0:T(8,128)(2,1)S(1)}, bf16[64,1024]{1,0:T(8,128)(2,1)S(1)}, u32[]{:S(2)}, u32[]{:S(2)}) collective-permute-start(bf16[64,1024]{1,0:T(8,128)(2,1)S(1)} %collective-permute-done.2.refs_0_.refs_8_), channel_id=1, source_target_pairs={{0,4},{4,8},{8,12},{12,14},{14,10},{10,6},{6,2},{2,0},{1,5},{5,9},... | collective-permute-start | bytes 393224 | tf_op jit(solution)/shard_map/ppermute | solution.py:542
  23.2 0.0 collective-permute-done.11.refs_3_.refs_11_
  23.2 0.0 collective-permute-start.13
  23.2 0.7 constant_dynamic-slice_fusion
  23.9 0.1 pad_add_fusion.scalar_ref
  24.0 0.3 square_sums.2.refs_4_
  24.2 0.3 collective-permute-done.5.refs_1_.refs_9_
  24.6 1.4 %collective-permute-done.8.refs_2_.refs_10_ = bf16[64,1024]{1,0:T(8,128)(2,1)S(1)} collective-permute-done((bf16[64,1024]{1,0:T(8,128)(2,1)S(1)}, bf16[64,1024]{1,0:T(8,128)(2,1)S(1)}, u32[]{:S(2)}, u32[]{:S(2)}) %collective-permute-start.8) | collective-permute-done | bytes 131104 | tf_op jit(solution)/shard_map/ppermute | solution.py:542
  25.9 0.1 square_sums.3.sums_ref
  26.0 0.1 collective-permute-done.12.last_top_ref.refs_12_
  26.1 2.1 %collective-permute-done.13.last_bottom_ref.refs_13_ = bf16[64,1024]{1,0:T(8,128)(2,1)S(1)} collective-permute-done((bf16[64,1024]{1,0:T(8,128)(2,1)S(1)}, bf16[64,1024]{1,0:T(8,128)(2,1)S(1)}, u32[]{:S(2)}, u32[]{:S(2)}) %collective-permute-start.13) | collective-permute-done | bytes 131104 | tf_op jit(solution)/shard_map/ppermute | solution.py:542
  28.2 0.0 collective-permute-done.14.other_ref
  28.2 4.3 %norm_key_value_shrink.1 = (f32[128,128]{1,0:T(8,128)}, f32[32,2048]{1,0:T(8,128)}, f32[8,80,128]{2,1,0:T(8,128)}, f32[32,2176]{1,0:T(8,128)S(1)}, f32[32,2176]{1,0:T(8,128)S(1)}, /*index=5*/f32[32,2176]{1,0:T(8,128)S(1)}) custom-call(s32[1,15]{1,0:T(1,128)S(1)} %pad_add_fusion.scalar_ref, f32[128,128]{1,0:T(8,128)S(1)} %square_sums.3.sums_ref, ...), custom_call_target="tpu_custom_call" | custom-call | flops 700000000 | bytes 6000000 | tf_op jit(solution)/shard_map/norm_key_value_shrink/pallas_call | solution.py:190
  32.5 0.7 convert_element_type.45
  33.2 4.8 %all-to-all-start = ((f32[8,80,128]{2,1,0:T(8,128)}), f32[8,80,128]{2,1,0:T(8,128)S(1)}, u32[]{:S(2)}, u32[]{:S(2)}) async-start(f32[8,80,128]{2,1,0:T(8,128)} %get-tuple-element.20), calls=%async_computation | async-start | bytes 655360 | tf_op jit(solution)/shard_map/all_to_all | solution.py:539
  38.1 0.0 collective-permute-start.16
  38.1 0.5 collective-permute-start.15
  38.6 2.0 %collective-permute-start.17 = (f16[32,2176]{1,0:T(8,128)(2,1)}, f16[32,2176]{1,0:T(8,128)(2,1)S(1)}, u32[]{:S(2)}, u32[]{:S(2)}) collective-permute-start(f16[32,2176]{1,0:T(8,128)(2,1)} %convert_element_type.45), channel_id=1, source_target_pairs={{0,4},{2,6},{4,0},{6,2},{8,12},{10,14},{12,8},{14,10},{1,5},{3,7},... | collective-permute-start | bytes 417800 | tf_op jit(solution)/shard_map/ppermute | solution.py:542
  40.6 2.4 %collective-permute-start.18 = (f16[32,2176]{1,0:T(8,128)(2,1)S(1)}, f16[32,2176]{1,0:T(8,128)(2,1)S(1)}, u32[]{:S(2)}, u32[]{:S(2)}) collective-permute-start(f16[32,2176]{1,0:T(8,128)(2,1)S(1)} %convert_element_type.46), channel_id=1, source_target_pairs={{0,8},{2,10},{4,12},{6,14},{8,0},{10,2},{12,4},{14,6},{1,9},{3,11}... | collective-permute-start | bytes 417800 | tf_op jit(solution)/shard_map/ppermute | solution.py:542
  43.0 0.0 collective-permute-start.19
  43.0 0.0 copy-start
  43.0 7.3 %query_products.1.acc_ref = f32[128,1024]{1,0:T(8,128)S(1)} custom-call(s32[1,15]{1,0:T(1,128)S(1)} %pad_add_fusion.scalar_ref, bf16[64,1024]{1,0:T(8,128)(2,1)S(1)} %collective-permute-done.refs_2_.refs_0_, bf16[64,1024]{1,0:T(8,128)(2,1)S(1)} %collective-permute-done.3.refs_3_.refs_1_, bf16[64,1024]{1,0:T(8,128)(2,1)S(1)} %collective-permute-done.6.refs_4_.refs_2_, ...), custom_call_target="tpu_custom_call" | custom-call | flops 2000000000 | bytes 17000000 | tf_op jit(solution)/shard_map/query_products/pallas_call | solution.py:266
  50.2 0.0 collective-permute-done.15.up_other_ref
  50.3 0.0 collective-permute-done.16.kv_other_hbm
  50.3 0.0 all-to-all-done.parts_ref
  50.3 2.6 %adapter_terms.1 = (bf16[128,1024]{1,0:T(8,128)(2,1)}, f32[16,2048]{1,0:T(8,128)S(1)}) custom-call(s32[1,15]{1,0:T(1,128)S(1)} %pad_add_fusion.scalar_ref, f32[8,80,128]{2,1,0:T(8,128)S(1)} %all-to-all-done.parts_ref, f32[128,1024]{1,0:T(8,128)S(1)} %query_products.1.acc_ref, bf16[2,64,1024]{2,1,0:T(8,128)(2,1)S(1)} %collective-permute-done.15.up_other_ref, ...), custom_call_target="tpu_custom_call" | custom-call | flops 100000000 | bytes 2000000 | tf_op jit(solution)/shard_map/adapter_terms/pallas_call | solution.py:334
  52.9 0.0 collective-permute-done.17
  52.9 3.0 %collective-permute-done.18 = f16[32,2176]{1,0:T(8,128)(2,1)S(1)} collective-permute-done((f16[32,2176]{1,0:T(8,128)(2,1)S(1)}, f16[32,2176]{1,0:T(8,128)(2,1)S(1)}, u32[]{:S(2)}, u32[]{:S(2)}) %collective-permute-start.18) | collective-permute-done | bytes 139296 | tf_op jit(solution)/shard_map/ppermute | solution.py:542
  55.9 0.0 collective-permute-done.19
  55.9 5.2 %all-to-all-start.1 = ((bf16[8,16,1024]{2,1,0:T(8,128)(2,1)}), bf16[8,16,1024]{2,1,0:T(8,128)(2,1)S(1)}, u32[]{:S(2)}, u32[]{:S(2)}) async-start(bf16[8,16,1024]{2,1,0:T(8,128)(2,1)} %bitcast.7), calls=%async_computation.1 | async-start | bytes 524288 | tf_op jit(solution)/shard_map/all_to_all | solution.py:539
  61.1 0.0 copy-done
  61.1 0.1 fusion
  61.3 0.9 %convert_element_type.50.refs_2_ = f32[32,2176]{1,0:T(8,128)S(1)} convert(f16[32,2176]{1,0:T(8,128)(2,1)} %collective-permute-done.19) | non-fusion elementwise | flops 69632 | bytes 417792 | tf_op jit(solution)/shard_map/convert_element_type | solution.py:609
  62.2 1.3 %line_sums.1 = (f32[16,2048]{1,0:T(8,128)S(1)}, f32[16,2176]{1,0:T(8,128)S(1)}) custom-call(s32[1,15]{1,0:T(1,128)S(1)} %pad_add_fusion.scalar_ref, f32[32,2048]{1,0:T(8,128)} %get-tuple-element.24.keep_ref, f32[32,2176]{1,0:T(8,128)S(1)} %convert_element_type.48.refs_0_, f32[32,2176]{1,0:T(8,128)S(1)} %convert_element_type.49.refs_1_, ...), custom_call_target="tpu_custom_call" | custom-call | flops 100000 | bytes 1500000 | tf_op jit(solution)/shard_map/line_sums/pallas_call | solution.py:367
  63.5 2.1 %collective-permute-start.20 = (f16[16,2176]{1,0:T(8,128)(2,1)S(1)}, f16[16,2176]{1,0:T(8,128)(2,1)S(1)}, u32[]{:S(2)}, u32[]{:S(2)}) collective-permute-start(f16[16,2176]{1,0:T(8,128)(2,1)S(1)} %convert_element_type.51), channel_id=1, source_target_pairs={{0,2},{2,0},{4,6},{6,4},{8,10},{10,8},{12,14},{14,12},{1,3},{3,1},... | collective-permute-start | bytes 208904 | tf_op jit(solution)/shard_map/ppermute | solution.py:542
  65.6 0.1 pad_maximum_fusion
  65.7 2.9 %collective-permute-done.20 = f16[16,2176]{1,0:T(8,128)(2,1)S(1)} collective-permute-done((f16[16,2176]{1,0:T(8,128)(2,1)S(1)}, f16[16,2176]{1,0:T(8,128)(2,1)S(1)}, u32[]{:S(2)}, u32[]{:S(2)}) %collective-permute-start.20) | collective-permute-done | bytes 69664 | tf_op jit(solution)/shard_map/ppermute | solution.py:542
  68.6 0.8 %new_key_value.1 = (bf16[16,2,1024]{2,1,0:T(2,128)(2,1)}, f32[16,16,128]{2,1,0:T(8,128)S(1)}) custom-call(f32[16,2048]{1,0:T(8,128)S(1)} %get-tuple-element.25.refs_0_, f32[16,2176]{1,0:T(8,128)S(1)} %convert_element_type.52.refs_1_, f32[16,2048]{1,0:T(8,128)S(1)} %get-tuple-element.27.refs_2_, f32[16,128]{1,0:T(8,128)S(1)} %get-tuple-element.35.refs_3_.cosine_ref, ...), custom_call_target="tpu_custom_call" | custom-call | flops 100000 | bytes 1000000 | tf_op jit(solution)/shard_map/new_key_value/pallas_call | solution.py:402
  69.5 0.2 all-to-all-done.1.query_ref
  69.6 5.8 %attention.1 = bf16[16,8192]{1,0:T(8,128)(2,1)} custom-call(s32[1,16]{1,0:T(1,128)S(1)} %copy-done, bf16[8,16,1024]{2,1,0:T(8,128)(2,1)S(1)} %all-to-all-done.1.query_ref, f32[16,16,128]{2,1,0:T(8,128)S(1)} %get-tuple-element.28.newest_ref, f32[16,128]{1,0:T(8,128)S(1)} %get-tuple-element.35.refs_3_.cosine_ref, ...), custom_call_target="tpu_custom_call" | custom-call | flops 400000000 | bytes 7000000 | tf_op jit(solution)/shard_map/attention/pallas_call | solution.py:500
  (8 shorter events, 0.1 us)
Async XLA Ops:
  0.6 27.6 %collective-permute-start.14 = (bf16[2,192,1024]{2,1,0:T(8,128)(2,1)}, bf16[2,192,1024]{2,1,0:T(8,128)(2,1)S(1)}, u32[]{:S(2)}, u32[]{:S(2)}) collective-permute-start(bf16[2,192,1024]{2,1,0:T(8,128)(2,1)} %bitcast.17), channel_id=1, source_target_pairs={{0,1},{1,0},{2,3},{3,2},{4,5},{5,4},{6,7},{7,6},{8,9},{9,8},{10,11... | collective-permute-start | bytes 2359304 | tf_op jit(solution)/shard_map/ppermute | solution.py:596
  2.1 6.9 %collective-permute-start = (bf16[64,1024]{1,0:T(8,128)(2,1)S(1)}, bf16[64,1024]{1,0:T(8,128)(2,1)S(1)}, u32[]{:S(2)}, u32[]{:S(2)}) collective-permute-start(bf16[64,1024]{1,0:T(8,128)(2,1)S(1)} %get-tuple-element.31.refs_0_.top_ref), channel_id=1, source_target_pairs={{0,4},{4,8},{8,12},{12,14},{14,10},{10,6},{6,2},{2,0},{1,5},{5,9},... | collective-permute-start | bytes 393224 | tf_op jit(solution)/shard_map/ppermute | solution.py:542
  4.8 6.3 %collective-permute-start.9 = (bf16[64,1024]{1,0:T(8,128)(2,1)S(1)}, bf16[64,1024]{1,0:T(8,128)(2,1)S(1)}, u32[]{:S(2)}, u32[]{:S(2)}) collective-permute-start(bf16[64,1024]{1,0:T(8,128)(2,1)S(1)} %get-tuple-element.30.refs_1_.bottom_ref), channel_id=1, source_target_pairs={{4,0},{8,4},{12,8},{14,12},{10,14},{6,10},{2,6},{0,2},{5,1},{9,5},... | collective-permute-start | bytes 393224 | tf_op jit(solution)/shard_map/ppermute | solution.py:542
  4.8 7.1 %collective-permute-start.3 = (bf16[64,1024]{1,0:T(8,128)(2,1)S(1)}, bf16[64,1024]{1,0:T(8,128)(2,1)S(1)}, u32[]{:S(2)}, u32[]{:S(2)}) collective-permute-start(bf16[64,1024]{1,0:T(8,128)(2,1)S(1)} %get-tuple-element.30.refs_1_.bottom_ref), channel_id=1, source_target_pairs={{0,4},{4,8},{8,12},{12,14},{14,10},{10,6},{6,2},{2,0},{1,5},{5,9},... | collective-permute-start | bytes 393224 | tf_op jit(solution)/shard_map/ppermute | solution.py:542
  6.8 7.1 %collective-permute-start.6 = (bf16[64,1024]{1,0:T(8,128)(2,1)S(1)}, bf16[64,1024]{1,0:T(8,128)(2,1)S(1)}, u32[]{:S(2)}, u32[]{:S(2)}) collective-permute-start(bf16[64,1024]{1,0:T(8,128)(2,1)S(1)} %get-tuple-element.31.refs_0_.top_ref), channel_id=1, source_target_pairs={{4,0},{8,4},{12,8},{14,12},{10,14},{6,10},{2,6},{0,2},{5,1},{9,5},... | collective-permute-start | bytes 393224 | tf_op jit(solution)/shard_map/ppermute | solution.py:542
  9.1 5.7 %collective-permute-start.1 = (bf16[64,1024]{1,0:T(8,128)(2,1)S(1)}, bf16[64,1024]{1,0:T(8,128)(2,1)S(1)}, u32[]{:S(2)}, u32[]{:S(2)}) collective-permute-start(bf16[64,1024]{1,0:T(8,128)(2,1)S(1)} %collective-permute-done.refs_2_.refs_0_), channel_id=1, source_target_pairs={{0,4},{4,8},{8,12},{12,14},{14,10},{10,6},{6,2},{2,0},{1,5},{5,9},... | collective-permute-start | bytes 393224 | tf_op jit(solution)/shard_map/ppermute | solution.py:542
  11.1 5.7 %collective-permute-start.10 = (bf16[64,1024]{1,0:T(8,128)(2,1)S(1)}, bf16[64,1024]{1,0:T(8,128)(2,1)S(1)}, u32[]{:S(2)}, u32[]{:S(2)}) collective-permute-start(bf16[64,1024]{1,0:T(8,128)(2,1)S(1)} %collective-permute-done.9.refs_5_.refs_3_), channel_id=1, source_target_pairs={{4,0},{8,4},{12,8},{14,12},{10,14},{6,10},{2,6},{0,2},{5,1},{9,5},... | collective-permute-start | bytes 393224 | tf_op jit(solution)/shard_map/ppermute | solution.py:542
  11.9 6.4 %collective-permute-start.4 = (bf16[64,1024]{1,0:T(8,128)(2,1)S(1)}, bf16[64,1024]{1,0:T(8,128)(2,1)S(1)}, u32[]{:S(2)}, u32[]{:S(2)}) collective-permute-start(bf16[64,1024]{1,0:T(8,128)(2,1)S(1)} %collective-permute-done.3.refs_3_.refs_1_), channel_id=1, source_target_pairs={{0,4},{4,8},{8,12},{12,14},{14,10},{10,6},{6,2},{2,0},{1,5},{5,9},... | collective-permute-start | bytes 393224 | tf_op jit(solution)/shard_map/ppermute | solution.py:542
  13.9 6.5 %collective-permute-start.7 = (bf16[64,1024]{1,0:T(8,128)(2,1)S(1)}, bf16[64,1024]{1,0:T(8,128)(2,1)S(1)}, u32[]{:S(2)}, u32[]{:S(2)}) collective-permute-start(bf16[64,1024]{1,0:T(8,128)(2,1)S(1)} %collective-permute-done.6.refs_4_.refs_2_), channel_id=1, source_target_pairs={{4,0},{8,4},{12,8},{14,12},{10,14},{6,10},{2,6},{0,2},{5,1},{9,5},... | collective-permute-start | bytes 393224 | tf_op jit(solution)/shard_map/ppermute | solution.py:542
  14.7 6.4 %collective-permute-start.2 = (bf16[64,1024]{1,0:T(8,128)(2,1)S(1)}, bf16[64,1024]{1,0:T(8,128)(2,1)S(1)}, u32[]{:S(2)}, u32[]{:S(2)}) collective-permute-start(bf16[64,1024]{1,0:T(8,128)(2,1)S(1)} %collective-permute-done.1.refs_6_.refs_4_), channel_id=1, source_target_pairs={{0,4},{4,8},{8,12},{12,14},{14,10},{10,6},{6,2},{2,0},{1,5},{5,9},... | collective-permute-start | bytes 393224 | tf_op jit(solution)/shard_map/ppermute | solution.py:542
  16.8 6.4 %collective-permute-start.11 = (bf16[64,1024]{1,0:T(8,128)(2,1)S(1)}, bf16[64,1024]{1,0:T(8,128)(2,1)S(1)}, u32[]{:S(2)}, u32[]{:S(2)}) collective-permute-start(bf16[64,1024]{1,0:T(8,128)(2,1)S(1)} %collective-permute-done.10.refs_9_.refs_7_), channel_id=1, source_target_pairs={{4,0},{8,4},{12,8},{14,12},{10,14},{6,10},{2,6},{0,2},{5,1},{9,5},... | collective-permute-start | bytes 393224 | tf_op jit(solution)/shard_map/ppermute | solution.py:542
  18.3 6.3 %collective-permute-start.5 = (bf16[64,1024]{1,0:T(8,128)(2,1)S(1)}, bf16[64,1024]{1,0:T(8,128)(2,1)S(1)}, u32[]{:S(2)}, u32[]{:S(2)}) collective-permute-start(bf16[64,1024]{1,0:T(8,128)(2,1)S(1)} %collective-permute-done.4.refs_7_.refs_5_), channel_id=1, source_target_pairs={{0,4},{4,8},{8,12},{12,14},{14,10},{10,6},{6,2},{2,0},{1,5},{5,9},... | collective-permute-start | bytes 393224 | tf_op jit(solution)/shard_map/ppermute | solution.py:542
  20.4 5.6 %collective-permute-start.8 = (bf16[64,1024]{1,0:T(8,128)(2,1)S(1)}, bf16[64,1024]{1,0:T(8,128)(2,1)S(1)}, u32[]{:S(2)}, u32[]{:S(2)}) collective-permute-start(bf16[64,1024]{1,0:T(8,128)(2,1)S(1)} %collective-permute-done.7.refs_8_.refs_6_), channel_id=1, source_target_pairs={{4,0},{8,4},{12,8},{14,12},{10,14},{6,10},{2,6},{0,2},{5,1},{9,5},... | collective-permute-start | bytes 393224 | tf_op jit(solution)/shard_map/ppermute | solution.py:542
  21.2 5.0 %collective-permute-start.12 = (bf16[64,1024]{1,0:T(8,128)(2,1)S(1)}, bf16[64,1024]{1,0:T(8,128)(2,1)S(1)}, u32[]{:S(2)}, u32[]{:S(2)}) collective-permute-start(bf16[64,1024]{1,0:T(8,128)(2,1)S(1)} %collective-permute-done.2.refs_0_.refs_8_), channel_id=1, source_target_pairs={{0,4},{4,8},{8,12},{12,14},{14,10},{10,6},{6,2},{2,0},{1,5},{5,9},... | collective-permute-start | bytes 393224 | tf_op jit(solution)/shard_map/ppermute | solution.py:542
  23.2 5.0 %collective-permute-start.13 = (bf16[64,1024]{1,0:T(8,128)(2,1)S(1)}, bf16[64,1024]{1,0:T(8,128)(2,1)S(1)}, u32[]{:S(2)}, u32[]{:S(2)}) collective-permute-start(bf16[64,1024]{1,0:T(8,128)(2,1)S(1)} %collective-permute-done.11.refs_3_.refs_11_), channel_id=1, source_target_pairs={{4,0},{8,4},{12,8},{14,12},{10,14},{6,10},{2,6},{0,2},{5,1},{9,5},... | collective-permute-start | bytes 393224 | tf_op jit(solution)/shard_map/ppermute | solution.py:542
  33.2 17.0 %all-to-all-start = ((f32[8,80,128]{2,1,0:T(8,128)}), f32[8,80,128]{2,1,0:T(8,128)S(1)}, u32[]{:S(2)}, u32[]{:S(2)}) async-start(f32[8,80,128]{2,1,0:T(8,128)} %get-tuple-element.20), calls=%async_computation | async-start | bytes 655360 | tf_op jit(solution)/shard_map/all_to_all | solution.py:539
  38.1 12.2 %collective-permute-start.16 = (bf16[2,2,64,1024]{3,2,1,0:T(8,128)(2,1)}, bf16[2,2,64,1024]{3,2,1,0:T(8,128)(2,1)}, u32[]{:S(2)}, u32[]{:S(2)}) collective-permute-start(bf16[2,2,64,1024]{3,2,1,0:T(8,128)(2,1)} %kv_own_hbm.1), channel_id=1, source_target_pairs={{0,1},{1,0},{2,3},{3,2},{4,5},{5,4},{6,7},{7,6},{8,9},{9,8},{10,11... | collective-permute-start | bytes 1572872 | tf_op jit(solution)/shard_map/ppermute | solution.py:596
  38.1 12.2 %collective-permute-start.15 = (bf16[2,64,1024]{2,1,0:T(8,128)(2,1)}, bf16[2,64,1024]{2,1,0:T(8,128)(2,1)S(1)}, u32[]{:S(2)}, u32[]{:S(2)}) collective-permute-start(bf16[2,64,1024]{2,1,0:T(8,128)(2,1)} %up_own_hbm.1), channel_id=1, source_target_pairs={{0,1},{1,0},{2,3},{3,2},{4,5},{5,4},{6,7},{7,6},{8,9},{9,8},{10,11... | collective-permute-start | bytes 786440 | tf_op jit(solution)/shard_map/ppermute | solution.py:596
  38.6 14.3 %collective-permute-start.17 = (f16[32,2176]{1,0:T(8,128)(2,1)}, f16[32,2176]{1,0:T(8,128)(2,1)S(1)}, u32[]{:S(2)}, u32[]{:S(2)}) collective-permute-start(f16[32,2176]{1,0:T(8,128)(2,1)} %convert_element_type.45), channel_id=1, source_target_pairs={{0,4},{2,6},{4,0},{6,2},{8,12},{10,14},{12,8},{14,10},{1,5},{3,7},... | collective-permute-start | bytes 417800 | tf_op jit(solution)/shard_map/ppermute | solution.py:542
  40.6 15.3 %collective-permute-start.18 = (f16[32,2176]{1,0:T(8,128)(2,1)S(1)}, f16[32,2176]{1,0:T(8,128)(2,1)S(1)}, u32[]{:S(2)}, u32[]{:S(2)}) collective-permute-start(f16[32,2176]{1,0:T(8,128)(2,1)S(1)} %convert_element_type.46), channel_id=1, source_target_pairs={{0,8},{2,10},{4,12},{6,14},{8,0},{10,2},{12,4},{14,6},{1,9},{3,11}... | collective-permute-start | bytes 417800 | tf_op jit(solution)/shard_map/ppermute | solution.py:542
  43.0 12.9 %collective-permute-start.19 = (f16[32,2176]{1,0:T(8,128)(2,1)S(1)}, f16[32,2176]{1,0:T(8,128)(2,1)}, u32[]{:S(2)}, u32[]{:S(2)}) collective-permute-start(f16[32,2176]{1,0:T(8,128)(2,1)S(1)} %convert_element_type.47), channel_id=1, source_target_pairs={{0,12},{2,14},{4,8},{6,10},{8,4},{10,6},{12,0},{14,2},{1,13},{3,15... | collective-permute-start | bytes 417800 | tf_op jit(solution)/shard_map/ppermute | solution.py:542
  43.0 18.1 %copy-start = (s32[1,16]{1,0:T(1,128)S(1)}, s32[1,16]{1,0:T(1,128)}, u32[]{:S(2)}) copy-start(s32[1,16]{1,0:T(1,128)} %lengths_ref.1) | copy-start | bytes 196
  55.9 13.7 %all-to-all-start.1 = ((bf16[8,16,1024]{2,1,0:T(8,128)(2,1)}), bf16[8,16,1024]{2,1,0:T(8,128)(2,1)S(1)}, u32[]{:S(2)}, u32[]{:S(2)}) async-start(bf16[8,16,1024]{2,1,0:T(8,128)(2,1)} %bitcast.7), calls=%async_computation.1 | async-start | bytes 524288 | tf_op jit(solution)/shard_map/all_to_all | solution.py:539
  63.5 5.1 %collective-permute-start.20 = (f16[16,2176]{1,0:T(8,128)(2,1)S(1)}, f16[16,2176]{1,0:T(8,128)(2,1)S(1)}, u32[]{:S(2)}, u32[]{:S(2)}) collective-permute-start(f16[16,2176]{1,0:T(8,128)(2,1)S(1)} %convert_element_type.51), channel_id=1, source_target_pairs={{0,2},{2,0},{4,6},{6,4},{8,10},{10,8},{12,14},{14,12},{1,3},{3,1},... | collective-permute-start | bytes 208904 | tf_op jit(solution)/shard_map/ppermute | solution.py:542

commit v5 on v4

--- a/solution.py
+++ b/solution.py
@@ -483,13 +483,16 @@
             )
         return carry
 
-    for i, copy in enumerate(copies[0]):
-        copy.wait()
-        lax.fori_loop(i * step, (i + 1) * step, score_step, 0, unroll=True)
-    lax.fori_loop(0, own_rows, weight_step, 0, unroll=UNROLL)
-    for i, copy in enumerate(copies[1]):
-        copy.wait()
-        lax.fori_loop(i * step, (i + 1) * step, value_step, 0, unroll=True)
+    for i in range(parts):
+        copies[0][i].wait()
+        for row in range(i * step, (i + 1) * step):
+            score_step(row, 0)
+        for row in range(i * step, (i + 1) * step):
+            weight_step(row, 0)
+    for i in range(parts):
+        copies[1][i].wait()
+        for row in range(i * step, (i + 1) * step):
+            value_step(row, 0)
     for head in range(heads):
         out_ref[:, head * HEAD_WIDTH : (head + 1) * HEAD_WIDTH] = query_heads_ref[:, head, :].astype(BF16)
 

time: 75.9 us -> 75.2 us (level)
  no operation moved by 1% of the time
where the time goes in v5:
time: 75.2 us; the launch traced here: 74.8 us
  starting transfers between devices  32.4 us (43%)
  Pallas kernels  21.8 us (29%)
  waiting for transfers between devices  15.4 us (20%)
  other arithmetic  2.76 us (4%)
  local copies, waits for them, and re-layouts  1.68 us (2%)
  between operations  0.79 us (1%)
    ppermute x18, starting transfers between devices, go(): return lax.ppermute(x, 'tensor', pairs)  21.3 us
    ppermute x18, waiting for transfers between devices, go(): return lax.ppermute(x, 'tensor', pairs)  15.2 us
    all_to_all x2, starting transfers between devices, everyone(): return lax.all_to_all(x, 'tensor', 0, 0, tiled=True)  10 us
    pallas_call x1, Pallas kernels, query_products(): pl.pallas_call(functools.partial(query_kernel, columns_at), in_specs=[SME...  7.26 us
    pallas_call x1, Pallas kernels, attend(): pl.pallas_call(attend_kernel, in_specs=[SMEM] + [VMEM] * 4 + [HBM], out_s...  5.18 us
    pallas_call x1, Pallas kernels, prep(): pl.pallas_call(functools.partial(prep_kernel, rank), in_specs=[SMEM] + [V...  4.31 us
    pallas_call x1, Pallas kernels, finish(): pl.pallas_call(functools.partial(finish_kernel, rank), in_specs=[SMEM] +...  2.58 us
  transfers between devices with their start and end apart: 23, of which 12 were waited for; matrix products, arithmetic and copies ran while one was open for 5% of the time, Pallas kernels for 16%

profile of v5, /device:TPU:0, one launch (start us, length us, event | category | flops | bytes accessed | tf_op | source)
XLA Modules:
  0.0 74.8 jit_solution(13898624655565563903)
XLA Ops:
  0.6 0.5 collective-permute-start.14
  1.1 1.0 %slice_bitcast_fusion = (bf16[64,1024]{1,0:T(8,128)(2,1)S(1)}, bf16[64,1024]{1,0:T(8,128)(2,1)S(1)}) fusion(bf16[1,128,1024]{2,1,0:T(8,128)(2,1)} %param.11), kind=kLoop, calls=%fused_computation | loop fusion | bytes 524288 | tf_op jit(solution)/shard_map/squeeze | solution.py:580
  2.1 2.6 %collective-permute-start = (bf16[64,1024]{1,0:T(8,128)(2,1)S(1)}, bf16[64,1024]{1,0:T(8,128)(2,1)S(1)}, u32[]{:S(2)}, u32[]{:S(2)}) collective-permute-start(bf16[64,1024]{1,0:T(8,128)(2,1)S(1)} %get-tuple-element.31.refs_0_.top_ref), channel_id=1, source_target_pairs={{0,4},{4,8},{8,12},{12,14},{14,10},{10,6},{6,2},{2,0},{1,5},{5,9},... | collective-permute-start | bytes 393224 | tf_op jit(solution)/shard_map/ppermute | solution.py:545
  4.8 0.0 collective-permute-start.9
  4.8 2.0 %collective-permute-start.3 = (bf16[64,1024]{1,0:T(8,128)(2,1)S(1)}, bf16[64,1024]{1,0:T(8,128)(2,1)S(1)}, u32[]{:S(2)}, u32[]{:S(2)}) collective-permute-start(bf16[64,1024]{1,0:T(8,128)(2,1)S(1)} %get-tuple-element.30.refs_1_.bottom_ref), channel_id=1, source_target_pairs={{0,4},{4,8},{8,12},{12,14},{14,10},{10,6},{6,2},{2,0},{1,5},{5,9},... | collective-permute-start | bytes 393224 | tf_op jit(solution)/shard_map/ppermute | solution.py:545
  6.8 0.0 collective-permute-start.6
  6.8 2.3 %collective-permute-done.refs_2_.refs_0_ = bf16[64,1024]{1,0:T(8,128)(2,1)S(1)} collective-permute-done((bf16[64,1024]{1,0:T(8,128)(2,1)S(1)}, bf16[64,1024]{1,0:T(8,128)(2,1)S(1)}, u32[]{:S(2)}, u32[]{:S(2)}) %collective-permute-start) | collective-permute-done | bytes 131104 | tf_op jit(solution)/shard_map/ppermute | solution.py:545
  9.1 2.0 %collective-permute-start.1 = (bf16[64,1024]{1,0:T(8,128)(2,1)S(1)}, bf16[64,1024]{1,0:T(8,128)(2,1)S(1)}, u32[]{:S(2)}, u32[]{:S(2)}) collective-permute-start(bf16[64,1024]{1,0:T(8,128)(2,1)S(1)} %collective-permute-done.refs_2_.refs_0_), channel_id=1, source_target_pairs={{0,4},{4,8},{8,12},{12,14},{14,10},{10,6},{6,2},{2,0},{1,5},{5,9},... | collective-permute-start | bytes 393224 | tf_op jit(solution)/shard_map/ppermute | solution.py:545
  11.1 0.0 collective-permute-done.9.refs_5_.refs_3_
  11.1 0.0 collective-permute-start.10
  11.1 0.8 %collective-permute-done.3.refs_3_.refs_1_ = bf16[64,1024]{1,0:T(8,128)(2,1)S(1)} collective-permute-done((bf16[64,1024]{1,0:T(8,128)(2,1)S(1)}, bf16[64,1024]{1,0:T(8,128)(2,1)S(1)}, u32[]{:S(2)}, u32[]{:S(2)}) %collective-permute-start.3) | collective-permute-done | bytes 131104 | tf_op jit(solution)/shard_map/ppermute | solution.py:545
  11.9 2.0 %collective-permute-start.4 = (bf16[64,1024]{1,0:T(8,128)(2,1)S(1)}, bf16[64,1024]{1,0:T(8,128)(2,1)S(1)}, u32[]{:S(2)}, u32[]{:S(2)}) collective-permute-start(bf16[64,1024]{1,0:T(8,128)(2,1)S(1)} %collective-permute-done.3.refs_3_.refs_1_), channel_id=1, source_target_pairs={{0,4},{4,8},{8,12},{12,14},{14,10},{10,6},{6,2},{2,0},{1,5},{5,9},... | collective-permute-start | bytes 393224 | tf_op jit(solution)/shard_map/ppermute | solution.py:545
  13.9 0.0 collective-permute-done.6.refs_4_.refs_2_
  13.9 0.0 collective-permute-start.7
  13.9 0.8 %collective-permute-done.1.refs_6_.refs_4_ = bf16[64,1024]{1,0:T(8,128)(2,1)S(1)} collective-permute-done((bf16[64,1024]{1,0:T(8,128)(2,1)S(1)}, bf16[64,1024]{1,0:T(8,128)(2,1)S(1)}, u32[]{:S(2)}, u32[]{:S(2)}) %collective-permute-start.1) | collective-permute-done | bytes 131104 | tf_op jit(solution)/shard_map/ppermute | solution.py:545
  14.7 2.0 %collective-permute-start.2 = (bf16[64,1024]{1,0:T(8,128)(2,1)S(1)}, bf16[64,1024]{1,0:T(8,128)(2,1)S(1)}, u32[]{:S(2)}, u32[]{:S(2)}) collective-permute-start(bf16[64,1024]{1,0:T(8,128)(2,1)S(1)} %collective-permute-done.1.refs_6_.refs_4_), channel_id=1, source_target_pairs={{0,4},{4,8},{8,12},{12,14},{14,10},{10,6},{6,2},{2,0},{1,5},{5,9},... | collective-permute-start | bytes 393224 | tf_op jit(solution)/shard_map/ppermute | solution.py:545
  16.8 0.0 collective-permute-done.10.refs_9_.refs_7_
  16.8 0.0 collective-permute-start.11
  16.8 0.8 %convert_reduce_fusion = s32[4]{0:T(128)S(1)} fusion(s32[128]{0:T(128)} %bitcast.23), kind=kLoop, calls=%fused_computation.7 | loop fusion | flops 1532 | bytes 528 | tf_op jit(solution)/shard_map/reduce_sum | solution.py:569
  17.6 0.7 collective-permute-done.4.refs_7_.refs_5_
  18.3 2.1 %collective-permute-start.5 = (bf16[64,1024]{1,0:T(8,128)(2,1)S(1)}, bf16[64,1024]{1,0:T(8,128)(2,1)S(1)}, u32[]{:S(2)}, u32[]{:S(2)}) collective-permute-start(bf16[64,1024]{1,0:T(8,128)(2,1)S(1)} %collective-permute-done.4.refs_7_.refs_5_), channel_id=1, source_target_pairs={{0,4},{4,8},{8,12},{12,14},{14,10},{10,6},{6,2},{2,0},{1,5},{5,9},... | collective-permute-start | bytes 393224 | tf_op jit(solution)/shard_map/ppermute | solution.py:545
  20.3 0.0 collective-permute-done.7.refs_8_.refs_6_
  20.4 0.0 collective-permute-start.8
  20.4 0.8 %collective-permute-done.2.refs_0_.refs_8_ = bf16[64,1024]{1,0:T(8,128)(2,1)S(1)} collective-permute-done((bf16[64,1024]{1,0:T(8,128)(2,1)S(1)}, bf16[64,1024]{1,0:T(8,128)(2,1)S(1)}, u32[]{:S(2)}, u32[]{:S(2)}) %collective-permute-start.2) | collective-permute-done | bytes 131104 | tf_op jit(solution)/shard_map/ppermute | solution.py:545
  21.2 2.0 %collective-permute-start.12 = (bf16[64,1024]{1,0:T(8,128)(2,1)S(1)}, bf16[64,1024]{1,0:T(8,128)(2,1)S(1)}, u32[]{:S(2)}, u32[]{:S(2)}) collective-permute-start(bf16[64,1024]{1,0:T(8,128)(2,1)S(1)} %collective-permute-done.2.refs_0_.refs_8_), channel_id=1, source_target_pairs={{0,4},{4,8},{8,12},{12,14},{14,10},{10,6},{6,2},{2,0},{1,5},{5,9},... | collective-permute-start | bytes 393224 | tf_op jit(solution)/shard_map/ppermute | solution.py:545
  23.2 0.0 collective-permute-done.11.refs_3_.refs_11_
  23.2 0.0 collective-permute-start.13
  23.2 0.7 constant_dynamic-slice_fusion
  23.9 0.1 pad_add_fusion.scalar_ref
  24.0 0.3 square_sums.2.refs_4_
  24.2 0.3 collective-permute-done.5.refs_1_.refs_9_
  24.6 1.4 %collective-permute-done.8.refs_2_.refs_10_ = bf16[64,1024]{1,0:T(8,128)(2,1)S(1)} collective-permute-done((bf16[64,1024]{1,0:T(8,128)(2,1)S(1)}, bf16[64,1024]{1,0:T(8,128)(2,1)S(1)}, u32[]{:S(2)}, u32[]{:S(2)}) %collective-permute-start.8) | collective-permute-done | bytes 131104 | tf_op jit(solution)/shard_map/ppermute | solution.py:545
  25.9 0.1 square_sums.3.sums_ref
  26.0 0.1 collective-permute-done.12.last_top_ref.refs_12_
  26.1 2.1 %collective-permute-done.13.last_bottom_ref.refs_13_ = bf16[64,1024]{1,0:T(8,128)(2,1)S(1)} collective-permute-done((bf16[64,1024]{1,0:T(8,128)(2,1)S(1)}, bf16[64,1024]{1,0:T(8,128)(2,1)S(1)}, u32[]{:S(2)}, u32[]{:S(2)}) %collective-permute-start.13) | collective-permute-done | bytes 131104 | tf_op jit(solution)/shard_map/ppermute | solution.py:545
  28.2 0.0 collective-permute-done.14.other_ref
  28.2 4.3 %norm_key_value_shrink.1 = (f32[128,128]{1,0:T(8,128)}, f32[32,2048]{1,0:T(8,128)}, f32[8,80,128]{2,1,0:T(8,128)}, f32[32,2176]{1,0:T(8,128)S(1)}, f32[32,2176]{1,0:T(8,128)S(1)}, /*index=5*/f32[32,2176]{1,0:T(8,128)S(1)}) custom-call(s32[1,15]{1,0:T(1,128)S(1)} %pad_add_fusion.scalar_ref, f32[128,128]{1,0:T(8,128)S(1)} %square_sums.3.sums_ref, ...), custom_call_target="tpu_custom_call" | custom-call | flops 700000000 | bytes 6000000 | tf_op jit(solution)/shard_map/norm_key_value_shrink/pallas_call | solution.py:190
  32.5 0.7 convert_element_type.45
  33.2 4.8 %all-to-all-start = ((f32[8,80,128]{2,1,0:T(8,128)}), f32[8,80,128]{2,1,0:T(8,128)S(1)}, u32[]{:S(2)}, u32[]{:S(2)}) async-start(f32[8,80,128]{2,1,0:T(8,128)} %get-tuple-element.20), calls=%async_computation | async-start | bytes 655360 | tf_op jit(solution)/shard_map/all_to_all | solution.py:542
  38.1 0.0 collective-permute-start.16
  38.1 0.5 collective-permute-start.15
  38.6 2.0 %collective-permute-start.17 = (f16[32,2176]{1,0:T(8,128)(2,1)}, f16[32,2176]{1,0:T(8,128)(2,1)S(1)}, u32[]{:S(2)}, u32[]{:S(2)}) collective-permute-start(f16[32,2176]{1,0:T(8,128)(2,1)} %convert_element_type.45), channel_id=1, source_target_pairs={{0,4},{2,6},{4,0},{6,2},{8,12},{10,14},{12,8},{14,10},{1,5},{3,7},... | collective-permute-start | bytes 417800 | tf_op jit(solution)/shard_map/ppermute | solution.py:545
  40.6 2.4 %collective-permute-start.18 = (f16[32,2176]{1,0:T(8,128)(2,1)S(1)}, f16[32,2176]{1,0:T(8,128)(2,1)S(1)}, u32[]{:S(2)}, u32[]{:S(2)}) collective-permute-start(f16[32,2176]{1,0:T(8,128)(2,1)S(1)} %convert_element_type.46), channel_id=1, source_target_pairs={{0,8},{2,10},{4,12},{6,14},{8,0},{10,2},{12,4},{14,6},{1,9},{3,11}... | collective-permute-start | bytes 417800 | tf_op jit(solution)/shard_map/ppermute | solution.py:545
  43.0 0.0 collective-permute-start.19
  43.0 0.0 copy-start
  43.0 7.3 %query_products.1.acc_ref = f32[128,1024]{1,0:T(8,128)S(1)} custom-call(s32[1,15]{1,0:T(1,128)S(1)} %pad_add_fusion.scalar_ref, bf16[64,1024]{1,0:T(8,128)(2,1)S(1)} %collective-permute-done.refs_2_.refs_0_, bf16[64,1024]{1,0:T(8,128)(2,1)S(1)} %collective-permute-done.3.refs_3_.refs_1_, bf16[64,1024]{1,0:T(8,128)(2,1)S(1)} %collective-permute-done.6.refs_4_.refs_2_, ...), custom_call_target="tpu_custom_call" | custom-call | flops 2000000000 | bytes 17000000 | tf_op jit(solution)/shard_map/query_products/pallas_call | solution.py:266
  50.2 0.0 collective-permute-done.15.up_other_ref
  50.3 0.0 collective-permute-done.16.kv_other_hbm
  50.3 0.0 all-to-all-done.parts_ref
  50.3 2.6 %adapter_terms.1 = (bf16[128,1024]{1,0:T(8,128)(2,1)}, f32[16,2048]{1,0:T(8,128)S(1)}) custom-call(s32[1,15]{1,0:T(1,128)S(1)} %pad_add_fusion.scalar_ref, f32[8,80,128]{2,1,0:T(8,128)S(1)} %all-to-all-done.parts_ref, f32[128,1024]{1,0:T(8,128)S(1)} %query_products.1.acc_ref, bf16[2,64,1024]{2,1,0:T(8,128)(2,1)S(1)} %collective-permute-done.15.up_other_ref, ...), custom_call_target="tpu_custom_call" | custom-call | flops 100000000 | bytes 2000000 | tf_op jit(solution)/shard_map/adapter_terms/pallas_call | solution.py:334
  52.9 0.0 collective-permute-done.17
  52.9 3.0 %collective-permute-done.18 = f16[32,2176]{1,0:T(8,128)(2,1)S(1)} collective-permute-done((f16[32,2176]{1,0:T(8,128)(2,1)S(1)}, f16[32,2176]{1,0:T(8,128)(2,1)S(1)}, u32[]{:S(2)}, u32[]{:S(2)}) %collective-permute-start.18) | collective-permute-done | bytes 139296 | tf_op jit(solution)/shard_map/ppermute | solution.py:545
  55.9 0.0 collective-permute-done.19
  55.9 5.2 %all-to-all-start.1 = ((bf16[8,16,1024]{2,1,0:T(8,128)(2,1)}), bf16[8,16,1024]{2,1,0:T(8,128)(2,1)S(1)}, u32[]{:S(2)}, u32[]{:S(2)}) async-start(bf16[8,16,1024]{2,1,0:T(8,128)(2,1)} %bitcast.7), calls=%async_computation.1 | async-start | bytes 524288 | tf_op jit(solution)/shard_map/all_to_all | solution.py:542
  61.1 0.0 copy-done
  61.1 0.1 fusion
  61.3 0.9 %convert_element_type.50.refs_2_ = f32[32,2176]{1,0:T(8,128)S(1)} convert(f16[32,2176]{1,0:T(8,128)(2,1)} %collective-permute-done.19) | non-fusion elementwise | flops 69632 | bytes 417792 | tf_op jit(solution)/shard_map/convert_element_type | solution.py:612
  62.2 1.3 %line_sums.1 = (f32[16,2048]{1,0:T(8,128)S(1)}, f32[16,2176]{1,0:T(8,128)S(1)}) custom-call(s32[1,15]{1,0:T(1,128)S(1)} %pad_add_fusion.scalar_ref, f32[32,2048]{1,0:T(8,128)} %get-tuple-element.24.keep_ref, f32[32,2176]{1,0:T(8,128)S(1)} %convert_element_type.48.refs_0_, f32[32,2176]{1,0:T(8,128)S(1)} %convert_element_type.49.refs_1_, ...), custom_call_target="tpu_custom_call" | custom-call | flops 100000 | bytes 1500000 | tf_op jit(solution)/shard_map/line_sums/pallas_call | solution.py:367
  63.5 2.1 %collective-permute-start.20 = (f16[16,2176]{1,0:T(8,128)(2,1)S(1)}, f16[16,2176]{1,0:T(8,128)(2,1)S(1)}, u32[]{:S(2)}, u32[]{:S(2)}) collective-permute-start(f16[16,2176]{1,0:T(8,128)(2,1)S(1)} %convert_element_type.51), channel_id=1, source_target_pairs={{0,2},{2,0},{4,6},{6,4},{8,10},{10,8},{12,14},{14,12},{1,3},{3,1},... | collective-permute-start | bytes 208904 | tf_op jit(solution)/shard_map/ppermute | solution.py:545
  65.6 0.1 pad_maximum_fusion
  65.7 2.9 %collective-permute-done.20 = f16[16,2176]{1,0:T(8,128)(2,1)S(1)} collective-permute-done((f16[16,2176]{1,0:T(8,128)(2,1)S(1)}, f16[16,2176]{1,0:T(8,128)(2,1)S(1)}, u32[]{:S(2)}, u32[]{:S(2)}) %collective-permute-start.20) | collective-permute-done | bytes 69664 | tf_op jit(solution)/shard_map/ppermute | solution.py:545
  68.6 0.8 %new_key_value.1 = (bf16[16,2,1024]{2,1,0:T(2,128)(2,1)}, f32[16,16,128]{2,1,0:T(8,128)S(1)}) custom-call(f32[16,2048]{1,0:T(8,128)S(1)} %get-tuple-element.25.refs_0_, f32[16,2176]{1,0:T(8,128)S(1)} %convert_element_type.52.refs_1_, f32[16,2048]{1,0:T(8,128)S(1)} %get-tuple-element.27.refs_2_, f32[16,128]{1,0:T(8,128)S(1)} %get-tuple-element.35.refs_3_.cosine_ref, ...), custom_call_target="tpu_custom_call" | custom-call | flops 100000 | bytes 1000000 | tf_op jit(solution)/shard_map/new_key_value/pallas_call | solution.py:402
  69.5 0.2 all-to-all-done.1.query_ref
  69.6 5.2 %attention.1 = bf16[16,8192]{1,0:T(8,128)(2,1)} custom-call(s32[1,16]{1,0:T(1,128)S(1)} %copy-done, bf16[8,16,1024]{2,1,0:T(8,128)(2,1)S(1)} %all-to-all-done.1.query_ref, f32[16,16,128]{2,1,0:T(8,128)S(1)} %get-tuple-element.28.newest_ref, f32[16,128]{1,0:T(8,128)S(1)} %get-tuple-element.35.refs_3_.cosine_ref, ...), custom_call_target="tpu_custom_call" | custom-call | flops 400000000 | bytes 7000000 | tf_op jit(solution)/shard_map/attention/pallas_call | solution.py:503
  (8 shorter events, 0.1 us)
Async XLA Ops:
  0.6 27.6 %collective-permute-start.14 = (bf16[2,192,1024]{2,1,0:T(8,128)(2,1)}, bf16[2,192,1024]{2,1,0:T(8,128)(2,1)S(1)}, u32[]{:S(2)}, u32[]{:S(2)}) collective-permute-start(bf16[2,192,1024]{2,1,0:T(8,128)(2,1)} %bitcast.17), channel_id=1, source_target_pairs={{0,1},{1,0},{2,3},{3,2},{4,5},{5,4},{6,7},{7,6},{8,9},{9,8},{10,11... | collective-permute-start | bytes 2359304 | tf_op jit(solution)/shard_map/ppermute | solution.py:599
  2.1 6.9 %collective-permute-start = (bf16[64,1024]{1,0:T(8,128)(2,1)S(1)}, bf16[64,1024]{1,0:T(8,128)(2,1)S(1)}, u32[]{:S(2)}, u32[]{:S(2)}) collective-permute-start(bf16[64,1024]{1,0:T(8,128)(2,1)S(1)} %get-tuple-element.31.refs_0_.top_ref), channel_id=1, source_target_pairs={{0,4},{4,8},{8,12},{12,14},{14,10},{10,6},{6,2},{2,0},{1,5},{5,9},... | collective-permute-start | bytes 393224 | tf_op jit(solution)/shard_map/ppermute | solution.py:545
  4.8 6.3 %collective-permute-start.9 = (bf16[64,1024]{1,0:T(8,128)(2,1)S(1)}, bf16[64,1024]{1,0:T(8,128)(2,1)S(1)}, u32[]{:S(2)}, u32[]{:S(2)}) collective-permute-start(bf16[64,1024]{1,0:T(8,128)(2,1)S(1)} %get-tuple-element.30.refs_1_.bottom_ref), channel_id=1, source_target_pairs={{4,0},{8,4},{12,8},{14,12},{10,14},{6,10},{2,6},{0,2},{5,1},{9,5},... | collective-permute-start | bytes 393224 | tf_op jit(solution)/shard_map/ppermute | solution.py:545
  4.8 7.1 %collective-permute-start.3 = (bf16[64,1024]{1,0:T(8,128)(2,1)S(1)}, bf16[64,1024]{1,0:T(8,128)(2,1)S(1)}, u32[]{:S(2)}, u32[]{:S(2)}) collective-permute-start(bf16[64,1024]{1,0:T(8,128)(2,1)S(1)} %get-tuple-element.30.refs_1_.bottom_ref), channel_id=1, source_target_pairs={{0,4},{4,8},{8,12},{12,14},{14,10},{10,6},{6,2},{2,0},{1,5},{5,9},... | collective-permute-start | bytes 393224 | tf_op jit(solution)/shard_map/ppermute | solution.py:545
  6.8 7.1 %collective-permute-start.6 = (bf16[64,1024]{1,0:T(8,128)(2,1)S(1)}, bf16[64,1024]{1,0:T(8,128)(2,1)S(1)}, u32[]{:S(2)}, u32[]{:S(2)}) collective-permute-start(bf16[64,1024]{1,0:T(8,128)(2,1)S(1)} %get-tuple-element.31.refs_0_.top_ref), channel_id=1, source_target_pairs={{4,0},{8,4},{12,8},{14,12},{10,14},{6,10},{2,6},{0,2},{5,1},{9,5},... | collective-permute-start | bytes 393224 | tf_op jit(solution)/shard_map/ppermute | solution.py:545
  9.1 5.7 %collective-permute-start.1 = (bf16[64,1024]{1,0:T(8,128)(2,1)S(1)}, bf16[64,1024]{1,0:T(8,128)(2,1)S(1)}, u32[]{:S(2)}, u32[]{:S(2)}) collective-permute-start(bf16[64,1024]{1,0:T(8,128)(2,1)S(1)} %collective-permute-done.refs_2_.refs_0_), channel_id=1, source_target_pairs={{0,4},{4,8},{8,12},{12,14},{14,10},{10,6},{6,2},{2,0},{1,5},{5,9},... | collective-permute-start | bytes 393224 | tf_op jit(solution)/shard_map/ppermute | solution.py:545
  11.1 5.7 %collective-permute-start.10 = (bf16[64,1024]{1,0:T(8,128)(2,1)S(1)}, bf16[64,1024]{1,0:T(8,128)(2,1)S(1)}, u32[]{:S(2)}, u32[]{:S(2)}) collective-permute-start(bf16[64,1024]{1,0:T(8,128)(2,1)S(1)} %collective-permute-done.9.refs_5_.refs_3_), channel_id=1, source_target_pairs={{4,0},{8,4},{12,8},{14,12},{10,14},{6,10},{2,6},{0,2},{5,1},{9,5},... | collective-permute-start | bytes 393224 | tf_op jit(solution)/shard_map/ppermute | solution.py:545
  11.9 6.4 %collective-permute-start.4 = (bf16[64,1024]{1,0:T(8,128)(2,1)S(1)}, bf16[64,1024]{1,0:T(8,128)(2,1)S(1)}, u32[]{:S(2)}, u32[]{:S(2)}) collective-permute-start(bf16[64,1024]{1,0:T(8,128)(2,1)S(1)} %collective-permute-done.3.refs_3_.refs_1_), channel_id=1, source_target_pairs={{0,4},{4,8},{8,12},{12,14},{14,10},{10,6},{6,2},{2,0},{1,5},{5,9},... | collective-permute-start | bytes 393224 | tf_op jit(solution)/shard_map/ppermute | solution.py:545
  13.9 6.5 %collective-permute-start.7 = (bf16[64,1024]{1,0:T(8,128)(2,1)S(1)}, bf16[64,1024]{1,0:T(8,128)(2,1)S(1)}, u32[]{:S(2)}, u32[]{:S(2)}) collective-permute-start(bf16[64,1024]{1,0:T(8,128)(2,1)S(1)} %collective-permute-done.6.refs_4_.refs_2_), channel_id=1, source_target_pairs={{4,0},{8,4},{12,8},{14,12},{10,14},{6,10},{2,6},{0,2},{5,1},{9,5},... | collective-permute-start | bytes 393224 | tf_op jit(solution)/shard_map/ppermute | solution.py:545
  14.7 6.4 %collective-permute-start.2 = (bf16[64,1024]{1,0:T(8,128)(2,1)S(1)}, bf16[64,1024]{1,0:T(8,128)(2,1)S(1)}, u32[]{:S(2)}, u32[]{:S(2)}) collective-permute-start(bf16[64,1024]{1,0:T(8,128)(2,1)S(1)} %collective-permute-done.1.refs_6_.refs_4_), channel_id=1, source_target_pairs={{0,4},{4,8},{8,12},{12,14},{14,10},{10,6},{6,2},{2,0},{1,5},{5,9},... | collective-permute-start | bytes 393224 | tf_op jit(solution)/shard_map/ppermute | solution.py:545
  16.8 6.4 %collective-permute-start.11 = (bf16[64,1024]{1,0:T(8,128)(2,1)S(1)}, bf16[64,1024]{1,0:T(8,128)(2,1)S(1)}, u32[]{:S(2)}, u32[]{:S(2)}) collective-permute-start(bf16[64,1024]{1,0:T(8,128)(2,1)S(1)} %collective-permute-done.10.refs_9_.refs_7_), channel_id=1, source_target_pairs={{4,0},{8,4},{12,8},{14,12},{10,14},{6,10},{2,6},{0,2},{5,1},{9,5},... | collective-permute-start | bytes 393224 | tf_op jit(solution)/shard_map/ppermute | solution.py:545
  18.3 6.3 %collective-permute-start.5 = (bf16[64,1024]{1,0:T(8,128)(2,1)S(1)}, bf16[64,1024]{1,0:T(8,128)(2,1)S(1)}, u32[]{:S(2)}, u32[]{:S(2)}) collective-permute-start(bf16[64,1024]{1,0:T(8,128)(2,1)S(1)} %collective-permute-done.4.refs_7_.refs_5_), channel_id=1, source_target_pairs={{0,4},{4,8},{8,12},{12,14},{14,10},{10,6},{6,2},{2,0},{1,5},{5,9},... | collective-permute-start | bytes 393224 | tf_op jit(solution)/shard_map/ppermute | solution.py:545
  20.4 5.6 %collective-permute-start.8 = (bf16[64,1024]{1,0:T(8,128)(2,1)S(1)}, bf16[64,1024]{1,0:T(8,128)(2,1)S(1)}, u32[]{:S(2)}, u32[]{:S(2)}) collective-permute-start(bf16[64,1024]{1,0:T(8,128)(2,1)S(1)} %collective-permute-done.7.refs_8_.refs_6_), channel_id=1, source_target_pairs={{4,0},{8,4},{12,8},{14,12},{10,14},{6,10},{2,6},{0,2},{5,1},{9,5},... | collective-permute-start | bytes 393224 | tf_op jit(solution)/shard_map/ppermute | solution.py:545
  21.2 5.0 %collective-permute-start.12 = (bf16[64,1024]{1,0:T(8,128)(2,1)S(1)}, bf16[64,1024]{1,0:T(8,128)(2,1)S(1)}, u32[]{:S(2)}, u32[]{:S(2)}) collective-permute-start(bf16[64,1024]{1,0:T(8,128)(2,1)S(1)} %collective-permute-done.2.refs_0_.refs_8_), channel_id=1, source_target_pairs={{0,4},{4,8},{8,12},{12,14},{14,10},{10,6},{6,2},{2,0},{1,5},{5,9},... | collective-permute-start | bytes 393224 | tf_op jit(solution)/shard_map/ppermute | solution.py:545
  23.2 5.0 %collective-permute-start.13 = (bf16[64,1024]{1,0:T(8,128)(2,1)S(1)}, bf16[64,1024]{1,0:T(8,128)(2,1)S(1)}, u32[]{:S(2)}, u32[]{:S(2)}) collective-permute-start(bf16[64,1024]{1,0:T(8,128)(2,1)S(1)} %collective-permute-done.11.refs_3_.refs_11_), channel_id=1, source_target_pairs={{4,0},{8,4},{12,8},{14,12},{10,14},{6,10},{2,6},{0,2},{5,1},{9,5},... | collective-permute-start | bytes 393224 | tf_op jit(solution)/shard_map/ppermute | solution.py:545
  33.2 17.0 %all-to-all-start = ((f32[8,80,128]{2,1,0:T(8,128)}), f32[8,80,128]{2,1,0:T(8,128)S(1)}, u32[]{:S(2)}, u32[]{:S(2)}) async-start(f32[8,80,128]{2,1,0:T(8,128)} %get-tuple-element.20), calls=%async_computation | async-start | bytes 655360 | tf_op jit(solution)/shard_map/all_to_all | solution.py:542
  38.1 12.2 %collective-permute-start.16 = (bf16[2,2,64,1024]{3,2,1,0:T(8,128)(2,1)}, bf16[2,2,64,1024]{3,2,1,0:T(8,128)(2,1)}, u32[]{:S(2)}, u32[]{:S(2)}) collective-permute-start(bf16[2,2,64,1024]{3,2,1,0:T(8,128)(2,1)} %kv_own_hbm.1), channel_id=1, source_target_pairs={{0,1},{1,0},{2,3},{3,2},{4,5},{5,4},{6,7},{7,6},{8,9},{9,8},{10,11... | collective-permute-start | bytes 1572872 | tf_op jit(solution)/shard_map/ppermute | solution.py:599
  38.1 12.2 %collective-permute-start.15 = (bf16[2,64,1024]{2,1,0:T(8,128)(2,1)}, bf16[2,64,1024]{2,1,0:T(8,128)(2,1)S(1)}, u32[]{:S(2)}, u32[]{:S(2)}) collective-permute-start(bf16[2,64,1024]{2,1,0:T(8,128)(2,1)} %up_own_hbm.1), channel_id=1, source_target_pairs={{0,1},{1,0},{2,3},{3,2},{4,5},{5,4},{6,7},{7,6},{8,9},{9,8},{10,11... | collective-permute-start | bytes 786440 | tf_op jit(solution)/shard_map/ppermute | solution.py:599
  38.6 14.3 %collective-permute-start.17 = (f16[32,2176]{1,0:T(8,128)(2,1)}, f16[32,2176]{1,0:T(8,128)(2,1)S(1)}, u32[]{:S(2)}, u32[]{:S(2)}) collective-permute-start(f16[32,2176]{1,0:T(8,128)(2,1)} %convert_element_type.45), channel_id=1, source_target_pairs={{0,4},{2,6},{4,0},{6,2},{8,12},{10,14},{12,8},{14,10},{1,5},{3,7},... | collective-permute-start | bytes 417800 | tf_op jit(solution)/shard_map/ppermute | solution.py:545
  40.6 15.3 %collective-permute-start.18 = (f16[32,2176]{1,0:T(8,128)(2,1)S(1)}, f16[32,2176]{1,0:T(8,128)(2,1)S(1)}, u32[]{:S(2)}, u32[]{:S(2)}) collective-permute-start(f16[32,2176]{1,0:T(8,128)(2,1)S(1)} %convert_element_type.46), channel_id=1, source_target_pairs={{0,8},{2,10},{4,12},{6,14},{8,0},{10,2},{12,4},{14,6},{1,9},{3,11}... | collective-permute-start | bytes 417800 | tf_op jit(solution)/shard_map/ppermute | solution.py:545
  43.0 12.9 %collective-permute-start.19 = (f16[32,2176]{1,0:T(8,128)(2,1)S(1)}, f16[32,2176]{1,0:T(8,128)(2,1)}, u32[]{:S(2)}, u32[]{:S(2)}) collective-permute-start(f16[32,2176]{1,0:T(8,128)(2,1)S(1)} %convert_element_type.47), channel_id=1, source_target_pairs={{0,12},{2,14},{4,8},{6,10},{8,4},{10,6},{12,0},{14,2},{1,13},{3,15... | collective-permute-start | bytes 417800 | tf_op jit(solution)/shard_map/ppermute | solution.py:545
  43.0 18.1 %copy-start = (s32[1,16]{1,0:T(1,128)S(1)}, s32[1,16]{1,0:T(1,128)}, u32[]{:S(2)}) copy-start(s32[1,16]{1,0:T(1,128)} %lengths_ref.1) | copy-start | bytes 196
  55.9 13.7 %all-to-all-start.1 = ((bf16[8,16,1024]{2,1,0:T(8,128)(2,1)}), bf16[8,16,1024]{2,1,0:T(8,128)(2,1)S(1)}, u32[]{:S(2)}, u32[]{:S(2)}) async-start(bf16[8,16,1024]{2,1,0:T(8,128)(2,1)} %bitcast.7), calls=%async_computation.1 | async-start | bytes 524288 | tf_op jit(solution)/shard_map/all_to_all | solution.py:542
  63.5 5.1 %collective-permute-start.20 = (f16[16,2176]{1,0:T(8,128)(2,1)S(1)}, f16[16,2176]{1,0:T(8,128)(2,1)S(1)}, u32[]{:S(2)}, u32[]{:S(2)}) collective-permute-start(f16[16,2176]{1,0:T(8,128)(2,1)S(1)} %convert_element_type.51), channel_id=1, source_target_pairs={{0,2},{2,0},{4,6},{6,4},{8,10},{10,8},{12,14},{14,12},{1,3},{3,1},... | collective-permute-start | bytes 208904 | tf_op jit(solution)/shard_map/ppermute | solution.py:545

commit v6 on v5

--- a/solution.py
+++ b/solution.py
@@ -604,7 +604,7 @@
             scalars, sums, last, local, gains, key_value_weight, own_down, other_down, rank, tensor
         )
         gives = [give.astype(NARROW) for give in gives]
-        shrink_parts = everyone(after(shrink, *gives))
+        shrink_parts = everyone(after(shrink, *gives[1:]))
         acc = query_products(scalars, 3, hidden[0], blocks, gains, query_weight, inverse)
         got = [
             go(give, [(t, t ^ (2 * d)) for t in range(tensor)]) for d, give in enumerate(gives, 1)

time: 75.2 us -> 74.3 us (0.988)
    ppermute x18, waiting for transfers between devices: 15.2 us -> 12.2 us  [go(): return lax.ppermute(x, 'tensor', pairs)]
    all_to_all x2, waiting for transfers between devices: 0.16 us -> 2.94 us  [everyone(): return lax.all_to_all(x, 'tensor', 0, 0, tiled=True)]
  transfers between devices with their start and end apart: 23 -> 23, of which waited for: 12 -> 11; matrix products, arithmetic and copies ran while one was open for 5% -> 6% of each run, Pallas kernels for 16% -> 17%
where the time goes in v6:
time: 74.3 us; the launch traced here: 73.8 us
  starting transfers between devices  31.7 us (43%)
  Pallas kernels  21.8 us (29%)
  waiting for transfers between devices  15.1 us (20%)
  other arithmetic  2.76 us (4%)
  local copies, waits for them, and re-layouts  1.68 us (2%)
  between operations  0.81 us (1%)
    ppermute x18, starting transfers between devices, go(): return lax.ppermute(x, 'tensor', pairs)  21.3 us
    ppermute x18, waiting for transfers between devices, go(): return lax.ppermute(x, 'tensor', pairs)  12.2 us
    all_to_all x2, starting transfers between devices, everyone(): return lax.all_to_all(x, 'tensor', 0, 0, tiled=True)  9.32 us
    pallas_call x1, Pallas kernels, query_products(): pl.pallas_call(functools.partial(query_kernel, columns_at), in_specs=[SME...  7.26 us
    pallas_call x1, Pallas kernels, attend(): pl.pallas_call(attend_kernel, in_specs=[SMEM] + [VMEM] * 4 + [HBM], out_s...  5.18 us
    pallas_call x1, Pallas kernels, prep(): pl.pallas_call(functools.partial(prep_kernel, rank), in_specs=[SMEM] + [V...  4.31 us
    all_to_all x2, waiting for transfers between devices, everyone(): return lax.all_to_all(x, 'tensor', 0, 0, tiled=True)  2.94 us
    pallas_call x1, Pallas kernels, finish(): pl.pallas_call(functools.partial(finish_kernel, rank), in_specs=[SMEM] +...  2.57 us
  transfers between devices with their start and end apart: 23, of which 11 were waited for; matrix products, arithmetic and copies ran while one was open for 6% of the time, Pallas kernels for 17%

profile of v6, /device:TPU:0, one launch (start us, length us, event | category | flops | bytes accessed | tf_op | source)
XLA Modules:
  0.0 73.8 jit_solution(3599898898129182931)
XLA Ops:
  0.6 0.5 collective-permute-start.14
  1.1 1.0 %slice_bitcast_fusion = (bf16[64,1024]{1,0:T(8,128)(2,1)S(1)}, bf16[64,1024]{1,0:T(8,128)(2,1)S(1)}) fusion(bf16[1,128,1024]{2,1,0:T(8,128)(2,1)} %param.11), kind=kLoop, calls=%fused_computation | loop fusion | bytes 524288 | tf_op jit(solution)/shard_map/squeeze | solution.py:580
  2.1 2.6 %collective-permute-start = (bf16[64,1024]{1,0:T(8,128)(2,1)S(1)}, bf16[64,1024]{1,0:T(8,128)(2,1)S(1)}, u32[]{:S(2)}, u32[]{:S(2)}) collective-permute-start(bf16[64,1024]{1,0:T(8,128)(2,1)S(1)} %get-tuple-element.31.refs_0_.top_ref), channel_id=1, source_target_pairs={{0,4},{4,8},{8,12},{12,14},{14,10},{10,6},{6,2},{2,0},{1,5},{5,9},... | collective-permute-start | bytes 393224 | tf_op jit(solution)/shard_map/ppermute | solution.py:545
  4.8 0.0 collective-permute-start.9
  4.8 2.0 %collective-permute-start.3 = (bf16[64,1024]{1,0:T(8,128)(2,1)S(1)}, bf16[64,1024]{1,0:T(8,128)(2,1)S(1)}, u32[]{:S(2)}, u32[]{:S(2)}) collective-permute-start(bf16[64,1024]{1,0:T(8,128)(2,1)S(1)} %get-tuple-element.30.refs_1_.bottom_ref), channel_id=1, source_target_pairs={{0,4},{4,8},{8,12},{12,14},{14,10},{10,6},{6,2},{2,0},{1,5},{5,9},... | collective-permute-start | bytes 393224 | tf_op jit(solution)/shard_map/ppermute | solution.py:545
  6.8 0.0 collective-permute-start.6
  6.8 2.3 %collective-permute-done.refs_2_.refs_0_ = bf16[64,1024]{1,0:T(8,128)(2,1)S(1)} collective-permute-done((bf16[64,1024]{1,0:T(8,128)(2,1)S(1)}, bf16[64,1024]{1,0:T(8,128)(2,1)S(1)}, u32[]{:S(2)}, u32[]{:S(2)}) %collective-permute-start) | collective-permute-done | bytes 131104 | tf_op jit(solution)/shard_map/ppermute | solution.py:545
  9.1 2.0 %collective-permute-start.1 = (bf16[64,1024]{1,0:T(8,128)(2,1)S(1)}, bf16[64,1024]{1,0:T(8,128)(2,1)S(1)}, u32[]{:S(2)}, u32[]{:S(2)}) collective-permute-start(bf16[64,1024]{1,0:T(8,128)(2,1)S(1)} %collective-permute-done.refs_2_.refs_0_), channel_id=1, source_target_pairs={{0,4},{4,8},{8,12},{12,14},{14,10},{10,6},{6,2},{2,0},{1,5},{5,9},... | collective-permute-start | bytes 393224 | tf_op jit(solution)/shard_map/ppermute | solution.py:545
  11.1 0.0 collective-permute-done.9.refs_5_.refs_3_
  11.1 0.0 collective-permute-start.10
  11.1 0.8 %collective-permute-done.3.refs_3_.refs_1_ = bf16[64,1024]{1,0:T(8,128)(2,1)S(1)} collective-permute-done((bf16[64,1024]{1,0:T(8,128)(2,1)S(1)}, bf16[64,1024]{1,0:T(8,128)(2,1)S(1)}, u32[]{:S(2)}, u32[]{:S(2)}) %collective-permute-start.3) | collective-permute-done | bytes 131104 | tf_op jit(solution)/shard_map/ppermute | solution.py:545
  11.9 2.0 %collective-permute-start.4 = (bf16[64,1024]{1,0:T(8,128)(2,1)S(1)}, bf16[64,1024]{1,0:T(8,128)(2,1)S(1)}, u32[]{:S(2)}, u32[]{:S(2)}) collective-permute-start(bf16[64,1024]{1,0:T(8,128)(2,1)S(1)} %collective-permute-done.3.refs_3_.refs_1_), channel_id=1, source_target_pairs={{0,4},{4,8},{8,12},{12,14},{14,10},{10,6},{6,2},{2,0},{1,5},{5,9},... | collective-permute-start | bytes 393224 | tf_op jit(solution)/shard_map/ppermute | solution.py:545
  13.9 0.0 collective-permute-done.6.refs_4_.refs_2_
  13.9 0.0 collective-permute-start.7
  13.9 0.8 %collective-permute-done.1.refs_6_.refs_4_ = bf16[64,1024]{1,0:T(8,128)(2,1)S(1)} collective-permute-done((bf16[64,1024]{1,0:T(8,128)(2,1)S(1)}, bf16[64,1024]{1,0:T(8,128)(2,1)S(1)}, u32[]{:S(2)}, u32[]{:S(2)}) %collective-permute-start.1) | collective-permute-done | bytes 131104 | tf_op jit(solution)/shard_map/ppermute | solution.py:545
  14.7 2.0 %collective-permute-start.2 = (bf16[64,1024]{1,0:T(8,128)(2,1)S(1)}, bf16[64,1024]{1,0:T(8,128)(2,1)S(1)}, u32[]{:S(2)}, u32[]{:S(2)}) collective-permute-start(bf16[64,1024]{1,0:T(8,128)(2,1)S(1)} %collective-permute-done.1.refs_6_.refs_4_), channel_id=1, source_target_pairs={{0,4},{4,8},{8,12},{12,14},{14,10},{10,6},{6,2},{2,0},{1,5},{5,9},... | collective-permute-start | bytes 393224 | tf_op jit(solution)/shard_map/ppermute | solution.py:545
  16.8 0.0 collective-permute-done.10.refs_9_.refs_7_
  16.8 0.0 collective-permute-start.11
  16.8 0.8 %convert_reduce_fusion = s32[4]{0:T(128)S(1)} fusion(s32[128]{0:T(128)} %bitcast.23), kind=kLoop, calls=%fused_computation.7 | loop fusion | flops 1532 | bytes 528 | tf_op jit(solution)/shard_map/reduce_sum | solution.py:569
  17.6 0.7 collective-permute-done.4.refs_7_.refs_5_
  18.3 2.1 %collective-permute-start.5 = (bf16[64,1024]{1,0:T(8,128)(2,1)S(1)}, bf16[64,1024]{1,0:T(8,128)(2,1)S(1)}, u32[]{:S(2)}, u32[]{:S(2)}) collective-permute-start(bf16[64,1024]{1,0:T(8,128)(2,1)S(1)} %collective-permute-done.4.refs_7_.refs_5_), channel_id=1, source_target_pairs={{0,4},{4,8},{8,12},{12,14},{14,10},{10,6},{6,2},{2,0},{1,5},{5,9},... | collective-permute-start | bytes 393224 | tf_op jit(solution)/shard_map/ppermute | solution.py:545
  20.3 0.0 collective-permute-done.7.refs_8_.refs_6_
  20.4 0.0 collective-permute-start.8
  20.4 0.8 %collective-permute-done.2.refs_0_.refs_8_ = bf16[64,1024]{1,0:T(8,128)(2,1)S(1)} collective-permute-done((bf16[64,1024]{1,0:T(8,128)(2,1)S(1)}, bf16[64,1024]{1,0:T(8,128)(2,1)S(1)}, u32[]{:S(2)}, u32[]{:S(2)}) %collective-permute-start.2) | collective-permute-done | bytes 131104 | tf_op jit(solution)/shard_map/ppermute | solution.py:545
  21.2 2.0 %collective-permute-start.12 = (bf16[64,1024]{1,0:T(8,128)(2,1)S(1)}, bf16[64,1024]{1,0:T(8,128)(2,1)S(1)}, u32[]{:S(2)}, u32[]{:S(2)}) collective-permute-start(bf16[64,1024]{1,0:T(8,128)(2,1)S(1)} %collective-permute-done.2.refs_0_.refs_8_), channel_id=1, source_target_pairs={{0,4},{4,8},{8,12},{12,14},{14,10},{10,6},{6,2},{2,0},{1,5},{5,9},... | collective-permute-start | bytes 393224 | tf_op jit(solution)/shard_map/ppermute | solution.py:545
  23.2 0.0 collective-permute-done.11.refs_3_.refs_11_
  23.2 0.0 collective-permute-start.13
  23.2 0.7 constant_dynamic-slice_fusion
  23.9 0.1 pad_add_fusion.scalar_ref
  24.0 0.3 square_sums.2.refs_4_
  24.2 0.3 collective-permute-done.5.refs_1_.refs_9_
  24.6 1.4 %collective-permute-done.8.refs_2_.refs_10_ = bf16[64,1024]{1,0:T(8,128)(2,1)S(1)} collective-permute-done((bf16[64,1024]{1,0:T(8,128)(2,1)S(1)}, bf16[64,1024]{1,0:T(8,128)(2,1)S(1)}, u32[]{:S(2)}, u32[]{:S(2)}) %collective-permute-start.8) | collective-permute-done | bytes 131104 | tf_op jit(solution)/shard_map/ppermute | solution.py:545
  25.9 0.1 square_sums.3.sums_ref
  26.0 0.1 collective-permute-done.12.last_top_ref.refs_12_
  26.1 2.1 %collective-permute-done.13.last_bottom_ref.refs_13_ = bf16[64,1024]{1,0:T(8,128)(2,1)S(1)} collective-permute-done((bf16[64,1024]{1,0:T(8,128)(2,1)S(1)}, bf16[64,1024]{1,0:T(8,128)(2,1)S(1)}, u32[]{:S(2)}, u32[]{:S(2)}) %collective-permute-start.13) | collective-permute-done | bytes 131104 | tf_op jit(solution)/shard_map/ppermute | solution.py:545
  28.2 0.0 collective-permute-done.14.other_ref
  28.2 4.3 %norm_key_value_shrink.1 = (f32[128,128]{1,0:T(8,128)}, f32[32,2048]{1,0:T(8,128)}, f32[8,80,128]{2,1,0:T(8,128)}, f32[32,2176]{1,0:T(8,128)S(1)}, f32[32,2176]{1,0:T(8,128)S(1)}, /*index=5*/f32[32,2176]{1,0:T(8,128)S(1)}) custom-call(s32[1,15]{1,0:T(1,128)S(1)} %pad_add_fusion.scalar_ref, f32[128,128]{1,0:T(8,128)S(1)} %square_sums.3.sums_ref, ...), custom_call_target="tpu_custom_call" | custom-call | flops 700000000 | bytes 6000000 | tf_op jit(solution)/shard_map/norm_key_value_shrink/pallas_call | solution.py:190
  32.6 4.8 %all-to-all-start = ((f32[8,80,128]{2,1,0:T(8,128)}), f32[8,80,128]{2,1,0:T(8,128)S(1)}, u32[]{:S(2)}, u32[]{:S(2)}) async-start(f32[8,80,128]{2,1,0:T(8,128)} %get-tuple-element.19), calls=%async_computation | async-start | bytes 655360 | tf_op jit(solution)/shard_map/all_to_all | solution.py:542
  37.4 0.0 collective-permute-start.16
  37.4 0.5 collective-permute-start.15
  37.9 2.9 %collective-permute-start.18 = (f16[32,2176]{1,0:T(8,128)(2,1)S(1)}, f16[32,2176]{1,0:T(8,128)(2,1)S(1)}, u32[]{:S(2)}, u32[]{:S(2)}) collective-permute-start(f16[32,2176]{1,0:T(8,128)(2,1)S(1)} %convert_element_type.45), channel_id=1, source_target_pairs={{0,8},{2,10},{4,12},{6,14},{8,0},{10,2},{12,4},{14,6},{1,9},{3,11}... | collective-permute-start | bytes 417800 | tf_op jit(solution)/shard_map/ppermute | solution.py:545
  40.8 1.5 %collective-permute-start.19 = (f16[32,2176]{1,0:T(8,128)(2,1)S(1)}, f16[32,2176]{1,0:T(8,128)(2,1)S(1)}, u32[]{:S(2)}, u32[]{:S(2)}) collective-permute-start(f16[32,2176]{1,0:T(8,128)(2,1)S(1)} %convert_element_type.46), channel_id=1, source_target_pairs={{0,12},{2,14},{4,8},{6,10},{8,4},{10,6},{12,0},{14,2},{1,13},{3,15... | collective-permute-start | bytes 417800 | tf_op jit(solution)/shard_map/ppermute | solution.py:545
  42.3 0.7 convert_element_type.47
  43.0 0.0 collective-permute-start.17
  43.0 0.0 copy-start
  43.0 7.3 %query_products.1.acc_ref = f32[128,1024]{1,0:T(8,128)S(1)} custom-call(s32[1,15]{1,0:T(1,128)S(1)} %pad_add_fusion.scalar_ref, bf16[64,1024]{1,0:T(8,128)(2,1)S(1)} %collective-permute-done.refs_2_.refs_0_, bf16[64,1024]{1,0:T(8,128)(2,1)S(1)} %collective-permute-done.3.refs_3_.refs_1_, bf16[64,1024]{1,0:T(8,128)(2,1)S(1)} %collective-permute-done.6.refs_4_.refs_2_, ...), custom_call_target="tpu_custom_call" | custom-call | flops 2000000000 | bytes 17000000 | tf_op jit(solution)/shard_map/query_products/pallas_call | solution.py:266
  50.2 0.0 collective-permute-done.15.up_other_ref
  50.3 0.0 collective-permute-done.16.kv_other_hbm
  50.3 2.9 %all-to-all-done.parts_ref = f32[8,80,128]{2,1,0:T(8,128)S(1)} async-done(((f32[8,80,128]{2,1,0:T(8,128)}), f32[8,80,128]{2,1,0:T(8,128)S(1)}, u32[]{:S(2)}, u32[]{:S(2)}) %all-to-all-start) | async-done | bytes 327712 | tf_op jit(solution)/shard_map/all_to_all | solution.py:542
  53.2 2.6 %adapter_terms.1 = (bf16[128,1024]{1,0:T(8,128)(2,1)}, f32[16,2048]{1,0:T(8,128)S(1)}) custom-call(s32[1,15]{1,0:T(1,128)S(1)} %pad_add_fusion.scalar_ref, f32[8,80,128]{2,1,0:T(8,128)S(1)} %all-to-all-done.parts_ref, f32[128,1024]{1,0:T(8,128)S(1)} %query_products.1.acc_ref, bf16[2,64,1024]{2,1,0:T(8,128)(2,1)S(1)} %collective-permute-done.15.up_other_ref, ...), custom_call_target="tpu_custom_call" | custom-call | flops 100000000 | bytes 2000000 | tf_op jit(solution)/shard_map/adapter_terms/pallas_call | solution.py:334
  55.8 0.0 collective-permute-done.17
  55.8 0.0 collective-permute-done.18
  55.8 0.0 collective-permute-done.19
  55.8 4.5 %all-to-all-start.1 = ((bf16[8,16,1024]{2,1,0:T(8,128)(2,1)}), bf16[8,16,1024]{2,1,0:T(8,128)(2,1)S(1)}, u32[]{:S(2)}, u32[]{:S(2)}) async-start(bf16[8,16,1024]{2,1,0:T(8,128)(2,1)} %bitcast.7), calls=%async_computation.1 | async-start | bytes 524288 | tf_op jit(solution)/shard_map/all_to_all | solution.py:542
  60.3 0.0 copy-done
  60.3 0.1 fusion
  60.5 0.9 %convert_element_type.48.refs_0_ = f32[32,2176]{1,0:T(8,128)S(1)} convert(f16[32,2176]{1,0:T(8,128)(2,1)} %collective-permute-done.17) | non-fusion elementwise | flops 69632 | bytes 417792 | tf_op jit(solution)/shard_map/convert_element_type | solution.py:612
  61.4 1.3 %line_sums.1 = (f32[16,2048]{1,0:T(8,128)S(1)}, f32[16,2176]{1,0:T(8,128)S(1)}) custom-call(s32[1,15]{1,0:T(1,128)S(1)} %pad_add_fusion.scalar_ref, f32[32,2048]{1,0:T(8,128)} %get-tuple-element.24.keep_ref, f32[32,2176]{1,0:T(8,128)S(1)} %convert_element_type.48.refs_0_, f32[32,2176]{1,0:T(8,128)S(1)} %convert_element_type.49.refs_1_, ...), custom_call_target="tpu_custom_call" | custom-call | flops 100000 | bytes 1500000 | tf_op jit(solution)/shard_map/line_sums/pallas_call | solution.py:367
  62.7 2.1 %collective-permute-start.20 = (f16[16,2176]{1,0:T(8,128)(2,1)S(1)}, f16[16,2176]{1,0:T(8,128)(2,1)S(1)}, u32[]{:S(2)}, u32[]{:S(2)}) collective-permute-start(f16[16,2176]{1,0:T(8,128)(2,1)S(1)} %convert_element_type.51), channel_id=1, source_target_pairs={{0,2},{2,0},{4,6},{6,4},{8,10},{10,8},{12,14},{14,12},{1,3},{3,1},... | collective-permute-start | bytes 208904 | tf_op jit(solution)/shard_map/ppermute | solution.py:545
  64.8 0.1 pad_maximum_fusion
  64.9 2.9 %collective-permute-done.20 = f16[16,2176]{1,0:T(8,128)(2,1)S(1)} collective-permute-done((f16[16,2176]{1,0:T(8,128)(2,1)S(1)}, f16[16,2176]{1,0:T(8,128)(2,1)S(1)}, u32[]{:S(2)}, u32[]{:S(2)}) %collective-permute-start.20) | collective-permute-done | bytes 69664 | tf_op jit(solution)/shard_map/ppermute | solution.py:545
  67.8 0.8 %new_key_value.1 = (bf16[16,2,1024]{2,1,0:T(2,128)(2,1)}, f32[16,16,128]{2,1,0:T(8,128)S(1)}) custom-call(f32[16,2048]{1,0:T(8,128)S(1)} %get-tuple-element.25.refs_0_, f32[16,2176]{1,0:T(8,128)S(1)} %convert_element_type.52.refs_1_, f32[16,2048]{1,0:T(8,128)S(1)} %get-tuple-element.27.refs_2_, f32[16,128]{1,0:T(8,128)S(1)} %get-tuple-element.35.refs_3_.cosine_ref, ...), custom_call_target="tpu_custom_call" | custom-call | flops 100000 | bytes 1000000 | tf_op jit(solution)/shard_map/new_key_value/pallas_call | solution.py:402
  68.6 0.0 all-to-all-done.1.query_ref
  68.6 5.2 %attention.1 = bf16[16,8192]{1,0:T(8,128)(2,1)} custom-call(s32[1,16]{1,0:T(1,128)S(1)} %copy-done, bf16[8,16,1024]{2,1,0:T(8,128)(2,1)S(1)} %all-to-all-done.1.query_ref, f32[16,16,128]{2,1,0:T(8,128)S(1)} %get-tuple-element.28.newest_ref, f32[16,128]{1,0:T(8,128)S(1)} %get-tuple-element.35.refs_3_.cosine_ref, ...), custom_call_target="tpu_custom_call" | custom-call | flops 400000000 | bytes 7000000 | tf_op jit(solution)/shard_map/attention/pallas_call | solution.py:503
  (8 shorter events, 0.1 us)
Async XLA Ops:
  0.6 27.6 %collective-permute-start.14 = (bf16[2,192,1024]{2,1,0:T(8,128)(2,1)}, bf16[2,192,1024]{2,1,0:T(8,128)(2,1)S(1)}, u32[]{:S(2)}, u32[]{:S(2)}) collective-permute-start(bf16[2,192,1024]{2,1,0:T(8,128)(2,1)} %bitcast.17), channel_id=1, source_target_pairs={{0,1},{1,0},{2,3},{3,2},{4,5},{5,4},{6,7},{7,6},{8,9},{9,8},{10,11... | collective-permute-start | bytes 2359304 | tf_op jit(solution)/shard_map/ppermute | solution.py:599
  2.1 6.9 %collective-permute-start = (bf16[64,1024]{1,0:T(8,128)(2,1)S(1)}, bf16[64,1024]{1,0:T(8,128)(2,1)S(1)}, u32[]{:S(2)}, u32[]{:S(2)}) collective-permute-start(bf16[64,1024]{1,0:T(8,128)(2,1)S(1)} %get-tuple-element.31.refs_0_.top_ref), channel_id=1, source_target_pairs={{0,4},{4,8},{8,12},{12,14},{14,10},{10,6},{6,2},{2,0},{1,5},{5,9},... | collective-permute-start | bytes 393224 | tf_op jit(solution)/shard_map/ppermute | solution.py:545
  4.8 6.3 %collective-permute-start.9 = (bf16[64,1024]{1,0:T(8,128)(2,1)S(1)}, bf16[64,1024]{1,0:T(8,128)(2,1)S(1)}, u32[]{:S(2)}, u32[]{:S(2)}) collective-permute-start(bf16[64,1024]{1,0:T(8,128)(2,1)S(1)} %get-tuple-element.30.refs_1_.bottom_ref), channel_id=1, source_target_pairs={{4,0},{8,4},{12,8},{14,12},{10,14},{6,10},{2,6},{0,2},{5,1},{9,5},... | collective-permute-start | bytes 393224 | tf_op jit(solution)/shard_map/ppermute | solution.py:545
  4.8 7.1 %collective-permute-start.3 = (bf16[64,1024]{1,0:T(8,128)(2,1)S(1)}, bf16[64,1024]{1,0:T(8,128)(2,1)S(1)}, u32[]{:S(2)}, u32[]{:S(2)}) collective-permute-start(bf16[64,1024]{1,0:T(8,128)(2,1)S(1)} %get-tuple-element.30.refs_1_.bottom_ref), channel_id=1, source_target_pairs={{0,4},{4,8},{8,12},{12,14},{14,10},{10,6},{6,2},{2,0},{1,5},{5,9},... | collective-permute-start | bytes 393224 | tf_op jit(solution)/shard_map/ppermute | solution.py:545
  6.8 7.1 %collective-permute-start.6 = (bf16[64,1024]{1,0:T(8,128)(2,1)S(1)}, bf16[64,1024]{1,0:T(8,128)(2,1)S(1)}, u32[]{:S(2)}, u32[]{:S(2)}) collective-permute-start(bf16[64,1024]{1,0:T(8,128)(2,1)S(1)} %get-tuple-element.31.refs_0_.top_ref), channel_id=1, source_target_pairs={{4,0},{8,4},{12,8},{14,12},{10,14},{6,10},{2,6},{0,2},{5,1},{9,5},... | collective-permute-start | bytes 393224 | tf_op jit(solution)/shard_map/ppermute | solution.py:545
  9.1 5.7 %collective-permute-start.1 = (bf16[64,1024]{1,0:T(8,128)(2,1)S(1)}, bf16[64,1024]{1,0:T(8,128)(2,1)S(1)}, u32[]{:S(2)}, u32[]{:S(2)}) collective-permute-start(bf16[64,1024]{1,0:T(8,128)(2,1)S(1)} %collective-permute-done.refs_2_.refs_0_), channel_id=1, source_target_pairs={{0,4},{4,8},{8,12},{12,14},{14,10},{10,6},{6,2},{2,0},{1,5},{5,9},... | collective-permute-start | bytes 393224 | tf_op jit(solution)/shard_map/ppermute | solution.py:545
  11.1 5.7 %collective-permute-start.10 = (bf16[64,1024]{1,0:T(8,128)(2,1)S(1)}, bf16[64,1024]{1,0:T(8,128)(2,1)S(1)}, u32[]{:S(2)}, u32[]{:S(2)}) collective-permute-start(bf16[64,1024]{1,0:T(8,128)(2,1)S(1)} %collective-permute-done.9.refs_5_.refs_3_), channel_id=1, source_target_pairs={{4,0},{8,4},{12,8},{14,12},{10,14},{6,10},{2,6},{0,2},{5,1},{9,5},... | collective-permute-start | bytes 393224 | tf_op jit(solution)/shard_map/ppermute | solution.py:545
  11.9 6.4 %collective-permute-start.4 = (bf16[64,1024]{1,0:T(8,128)(2,1)S(1)}, bf16[64,1024]{1,0:T(8,128)(2,1)S(1)}, u32[]{:S(2)}, u32[]{:S(2)}) collective-permute-start(bf16[64,1024]{1,0:T(8,128)(2,1)S(1)} %collective-permute-done.3.refs_3_.refs_1_), channel_id=1, source_target_pairs={{0,4},{4,8},{8,12},{12,14},{14,10},{10,6},{6,2},{2,0},{1,5},{5,9},... | collective-permute-start | bytes 393224 | tf_op jit(solution)/shard_map/ppermute | solution.py:545
  13.9 6.5 %collective-permute-start.7 = (bf16[64,1024]{1,0:T(8,128)(2,1)S(1)}, bf16[64,1024]{1,0:T(8,128)(2,1)S(1)}, u32[]{:S(2)}, u32[]{:S(2)}) collective-permute-start(bf16[64,1024]{1,0:T(8,128)(2,1)S(1)} %collective-permute-done.6.refs_4_.refs_2_), channel_id=1, source_target_pairs={{4,0},{8,4},{12,8},{14,12},{10,14},{6,10},{2,6},{0,2},{5,1},{9,5},... | collective-permute-start | bytes 393224 | tf_op jit(solution)/shard_map/ppermute | solution.py:545
  14.7 6.4 %collective-permute-start.2 = (bf16[64,1024]{1,0:T(8,128)(2,1)S(1)}, bf16[64,1024]{1,0:T(8,128)(2,1)S(1)}, u32[]{:S(2)}, u32[]{:S(2)}) collective-permute-start(bf16[64,1024]{1,0:T(8,128)(2,1)S(1)} %collective-permute-done.1.refs_6_.refs_4_), channel_id=1, source_target_pairs={{0,4},{4,8},{8,12},{12,14},{14,10},{10,6},{6,2},{2,0},{1,5},{5,9},... | collective-permute-start | bytes 393224 | tf_op jit(solution)/shard_map/ppermute | solution.py:545
  16.8 6.4 %collective-permute-start.11 = (bf16[64,1024]{1,0:T(8,128)(2,1)S(1)}, bf16[64,1024]{1,0:T(8,128)(2,1)S(1)}, u32[]{:S(2)}, u32[]{:S(2)}) collective-permute-start(bf16[64,1024]{1,0:T(8,128)(2,1)S(1)} %collective-permute-done.10.refs_9_.refs_7_), channel_id=1, source_target_pairs={{4,0},{8,4},{12,8},{14,12},{10,14},{6,10},{2,6},{0,2},{5,1},{9,5},... | collective-permute-start | bytes 393224 | tf_op jit(solution)/shard_map/ppermute | solution.py:545
  18.3 6.3 %collective-permute-start.5 = (bf16[64,1024]{1,0:T(8,128)(2,1)S(1)}, bf16[64,1024]{1,0:T(8,128)(2,1)S(1)}, u32[]{:S(2)}, u32[]{:S(2)}) collective-permute-start(bf16[64,1024]{1,0:T(8,128)(2,1)S(1)} %collective-permute-done.4.refs_7_.refs_5_), channel_id=1, source_target_pairs={{0,4},{4,8},{8,12},{12,14},{14,10},{10,6},{6,2},{2,0},{1,5},{5,9},... | collective-permute-start | bytes 393224 | tf_op jit(solution)/shard_map/ppermute | solution.py:545
  20.4 5.6 %collective-permute-start.8 = (bf16[64,1024]{1,0:T(8,128)(2,1)S(1)}, bf16[64,1024]{1,0:T(8,128)(2,1)S(1)}, u32[]{:S(2)}, u32[]{:S(2)}) collective-permute-start(bf16[64,1024]{1,0:T(8,128)(2,1)S(1)} %collective-permute-done.7.refs_8_.refs_6_), channel_id=1, source_target_pairs={{4,0},{8,4},{12,8},{14,12},{10,14},{6,10},{2,6},{0,2},{5,1},{9,5},... | collective-permute-start | bytes 393224 | tf_op jit(solution)/shard_map/ppermute | solution.py:545
  21.2 5.0 %collective-permute-start.12 = (bf16[64,1024]{1,0:T(8,128)(2,1)S(1)}, bf16[64,1024]{1,0:T(8,128)(2,1)S(1)}, u32[]{:S(2)}, u32[]{:S(2)}) collective-permute-start(bf16[64,1024]{1,0:T(8,128)(2,1)S(1)} %collective-permute-done.2.refs_0_.refs_8_), channel_id=1, source_target_pairs={{0,4},{4,8},{8,12},{12,14},{14,10},{10,6},{6,2},{2,0},{1,5},{5,9},... | collective-permute-start | bytes 393224 | tf_op jit(solution)/shard_map/ppermute | solution.py:545
  23.2 5.0 %collective-permute-start.13 = (bf16[64,1024]{1,0:T(8,128)(2,1)S(1)}, bf16[64,1024]{1,0:T(8,128)(2,1)S(1)}, u32[]{:S(2)}, u32[]{:S(2)}) collective-permute-start(bf16[64,1024]{1,0:T(8,128)(2,1)S(1)} %collective-permute-done.11.refs_3_.refs_11_), channel_id=1, source_target_pairs={{4,0},{8,4},{12,8},{14,12},{10,14},{6,10},{2,6},{0,2},{5,1},{9,5},... | collective-permute-start | bytes 393224 | tf_op jit(solution)/shard_map/ppermute | solution.py:545
  32.6 20.7 %all-to-all-start = ((f32[8,80,128]{2,1,0:T(8,128)}), f32[8,80,128]{2,1,0:T(8,128)S(1)}, u32[]{:S(2)}, u32[]{:S(2)}) async-start(f32[8,80,128]{2,1,0:T(8,128)} %get-tuple-element.19), calls=%async_computation | async-start | bytes 655360 | tf_op jit(solution)/shard_map/all_to_all | solution.py:542
  37.4 12.9 %collective-permute-start.16 = (bf16[2,2,64,1024]{3,2,1,0:T(8,128)(2,1)}, bf16[2,2,64,1024]{3,2,1,0:T(8,128)(2,1)}, u32[]{:S(2)}, u32[]{:S(2)}) collective-permute-start(bf16[2,2,64,1024]{3,2,1,0:T(8,128)(2,1)} %kv_own_hbm.1), channel_id=1, source_target_pairs={{0,1},{1,0},{2,3},{3,2},{4,5},{5,4},{6,7},{7,6},{8,9},{9,8},{10,11... | collective-permute-start | bytes 1572872 | tf_op jit(solution)/shard_map/ppermute | solution.py:599
  37.4 12.8 %collective-permute-start.15 = (bf16[2,64,1024]{2,1,0:T(8,128)(2,1)}, bf16[2,64,1024]{2,1,0:T(8,128)(2,1)S(1)}, u32[]{:S(2)}, u32[]{:S(2)}) collective-permute-start(bf16[2,64,1024]{2,1,0:T(8,128)(2,1)} %up_own_hbm.1), channel_id=1, source_target_pairs={{0,1},{1,0},{2,3},{3,2},{4,5},{5,4},{6,7},{7,6},{8,9},{9,8},{10,11... | collective-permute-start | bytes 786440 | tf_op jit(solution)/shard_map/ppermute | solution.py:599
  37.9 17.9 %collective-permute-start.18 = (f16[32,2176]{1,0:T(8,128)(2,1)S(1)}, f16[32,2176]{1,0:T(8,128)(2,1)S(1)}, u32[]{:S(2)}, u32[]{:S(2)}) collective-permute-start(f16[32,2176]{1,0:T(8,128)(2,1)S(1)} %convert_element_type.45), channel_id=1, source_target_pairs={{0,8},{2,10},{4,12},{6,14},{8,0},{10,2},{12,4},{14,6},{1,9},{3,11}... | collective-permute-start | bytes 417800 | tf_op jit(solution)/shard_map/ppermute | solution.py:545
  40.8 15.0 %collective-permute-start.19 = (f16[32,2176]{1,0:T(8,128)(2,1)S(1)}, f16[32,2176]{1,0:T(8,128)(2,1)S(1)}, u32[]{:S(2)}, u32[]{:S(2)}) collective-permute-start(f16[32,2176]{1,0:T(8,128)(2,1)S(1)} %convert_element_type.46), channel_id=1, source_target_pairs={{0,12},{2,14},{4,8},{6,10},{8,4},{10,6},{12,0},{14,2},{1,13},{3,15... | collective-permute-start | bytes 417800 | tf_op jit(solution)/shard_map/ppermute | solution.py:545
  43.0 12.8 %collective-permute-start.17 = (f16[32,2176]{1,0:T(8,128)(2,1)}, f16[32,2176]{1,0:T(8,128)(2,1)}, u32[]{:S(2)}, u32[]{:S(2)}) collective-permute-start(f16[32,2176]{1,0:T(8,128)(2,1)} %convert_element_type.47), channel_id=1, source_target_pairs={{0,4},{2,6},{4,0},{6,2},{8,12},{10,14},{12,8},{14,10},{1,5},{3,7},... | collective-permute-start | bytes 417800 | tf_op jit(solution)/shard_map/ppermute | solution.py:545
  43.0 17.3 %copy-start = (s32[1,16]{1,0:T(1,128)S(1)}, s32[1,16]{1,0:T(1,128)}, u32[]{:S(2)}) copy-start(s32[1,16]{1,0:T(1,128)} %lengths_ref.1) | copy-start | bytes 196
  55.8 12.8 %all-to-all-start.1 = ((bf16[8,16,1024]{2,1,0:T(8,128)(2,1)}), bf16[8,16,1024]{2,1,0:T(8,128)(2,1)S(1)}, u32[]{:S(2)}, u32[]{:S(2)}) async-start(bf16[8,16,1024]{2,1,0:T(8,128)(2,1)} %bitcast.7), calls=%async_computation.1 | async-start | bytes 524288 | tf_op jit(solution)/shard_map/all_to_all | solution.py:542
  62.7 5.1 %collective-permute-start.20 = (f16[16,2176]{1,0:T(8,128)(2,1)S(1)}, f16[16,2176]{1,0:T(8,128)(2,1)S(1)}, u32[]{:S(2)}, u32[]{:S(2)}) collective-permute-start(f16[16,2176]{1,0:T(8,128)(2,1)S(1)} %convert_element_type.51), channel_id=1, source_target_pairs={{0,2},{2,0},{4,6},{6,4},{8,10},{10,8},{12,14},{14,12},{1,3},{3,1},... | collective-permute-start | bytes 208904 | tf_op jit(solution)/shard_map/ppermute | solution.py:545
